TPU v7x, 32 devices: a whole 2x2x4 slice. The times are simulated.
32 devices in a mesh: grp: 2 (over y), pb: 8 (over z, x), layer: 2 (over core).
Axes of the slice: x: 2, y: 2, z: 4, core: 2. Of those that a mesh axis runs over, the one named last changes fastest.
Arguments:
- query_grads: bfloat16 [32768, 2, 1024], P(('grp', 'pb'), 'layer'), parts along dimension 0, may hold values from -0.19921875 to 0.19921875
- train_grads: bfloat16 [512, 2, 1024], P(('grp', 'pb'), 'layer'), parts along dimension 0, may hold values from -6 to 6
- basis_in: float32 [2, 32, 32], P('layer'), may hold values from -1 to 1, as said below
- basis_out: float32 [2, 32, 32], P('layer'), may hold values from -1 to 1, as said below
- eigenvalues: float32 [2, 32, 32], P('layer'), may hold values from 0.05 to 1
Outputs:
- scores: bfloat16 [32768, 256], P(('grp', 'pb', 'layer')), parts along dimension 0
There are 2 independent parts, one for each index of `grp`. A program takes and returns all parts, laid end to end along the dimension named above; an argument that names none is the same for every part. Nothing has to cross between parts.
Inputs may be any that keep to these rules, and one draw needn't show every extreme that they name: `basis_in`: each layer's matrix is orthogonal. `basis_out`: each layer's matrix is orthogonal.
All inputs are finite; a program needn't handle non-finite values.
Results may differ from a plain program's by a relative error of at most 0.0076.
Values may be sent and summed in bfloat16 or wider, within the bound.
No kernel may reach another device: no remote copies, remote signals or barrier semaphores. Data moves between devices by JAX's collectives and lax.ppermute only.
A program may use at most 64 MiB of HBM per device.

v0:
```python
import jax
import jax.numpy as jnp
from jax import lax
from jax.sharding import PartitionSpec as P


def precondition(grads, basis_in, basis_out, eigenvalues):
    layers = grads.shape[1]
    kout = basis_out.shape[1]
    kin = basis_in.shape[1]
    whole = basis_out[:, :, None, :, None] * basis_in[:, None, :, None, :]
    kron = whole.reshape(layers, kout * kin, kout * kin).astype(jnp.bfloat16)
    rotated = jnp.einsum("qlg,lgh->qlh", grads, kron, preferred_element_type=jnp.float32)
    scaled = (rotated / (eigenvalues.reshape(layers, kout * kin)[None] + 0.1)).astype(jnp.bfloat16)
    back = jnp.einsum("qlh,lgh->qlg", scaled, kron, preferred_element_type=jnp.float32)
    return back.astype(jnp.bfloat16)


def rounded_product(left, right):
    term = lax.dot_general(
        left, right, (((1,), (1,)), ((), ())), preferred_element_type=jnp.float32
    )
    term = lax.optimization_barrier(term.astype(jnp.bfloat16))
    return term.astype(jnp.float32)


def on_device(query_grads, train_grads, basis_in, basis_out, eigenvalues):
    query_rows = query_grads.shape[0]
    prepared = precondition(query_grads, basis_in, basis_out, eigenvalues).reshape(query_rows, -1)
    piece = lax.all_gather(train_grads, "pb", axis=0, tiled=True)
    partial_scores = rounded_product(prepared, piece.reshape(piece.shape[0], -1))
    return lax.psum_scatter(
        partial_scores.astype(jnp.bfloat16), "layer", scatter_dimension=0, tiled=True
    )


def solution(mesh):
    placed = (
        P(("grp", "pb"), "layer", None),
        P(("grp", "pb"), "layer", None),
        P("layer", None, None),
        P("layer", None, None),
        P("layer", None, None),
    )
    return jax.shard_map(
        on_device,
        mesh=mesh,
        in_specs=placed,
        out_specs=P(("grp", "pb", "layer"), None),
        check_vma=False,
    )
```

profile of v0, /device:TPU:0, one launch (start us, length us, event | category | flops | bytes accessed | tf_op | source)
XLA Modules:
  0.0 90.6 jit_solution(14692505391515047863)
XLA Ops:
  6.5 0.0 reduce-scatter.2.cloned.1.call-start
  6.5 6.0 %multiply_convert_fusion = bf16[32,32,32,32]{3,2,1,0:T(8,128)(2,1)} fusion(f32[32,32]{1,0:T(8,128)} %bitcast.38, f32[32,32]{1,0:T(8,128)} %bitcast.39), kind=kLoop, calls=%fused_computation | loop fusion | flops 2097152 | bytes 2105344 | tf_op jit(solution)/shard_map/convert_element_type | solution.py:12
  12.5 0.0 copy-start.1
  12.5 0.0 copy-start
  12.5 11.4 %convert_element_type.41 = bf16[1024,1024]{1,0:T(8,128)(2,1)S(1)} reshape(bf16[32,32,32,32]{3,2,1,0:T(8,128)(2,1)} %multiply_convert_fusion) | data formatting | bytes 4194304 | tf_op jit(solution)/shard_map/convert_element_type | solution.py:12
  23.9 0.0 copy-done.1
  23.9 0.1 add.18
  24.0 0.0 copy-done
  24.0 33.0 %all_gather.3 = bf16[256,1,1024]{2,0,1:T(8,128)(2,1)S(1)} all-gather(bf16[32,1,1024]{2,0,1:T(8,128)(2,1)S(1)} %copy-done), channel_id=1, replica_groups=mesh['grp'=2,'pb'=8,'layer'=2] {'pb'}, dimensions={0}, use_global_device_ids=true | all-gather | bytes 589824 | tf_op jit(solution)/shard_map/all_gather | solution.py:30
  57.0 12.4 %fusion.3 = bf16[1024,2048]{1,0:T(8,128)(2,1)} fusion(bf16[1024,1024]{1,0:T(8,128)(2,1)S(1)} %convert_element_type.41, bf16[2048,1,1024]{2,0,1:T(8,128)(2,1)} %param.5, f32[1024]{0:T(1024)S(1)} %add.18), kind=kOutput, calls=%fused_computation.5 | convolution fusion | flops 8594128896 | bytes 10489856 | tf_op jit(solution)/shard_map/qlh,lgh->qlg/dot_general | solution.py:15
  69.4 4.5 %fusion.7 = bf16[2048,256]{1,0:T(8,128)(2,1)} fusion(bf16[1024,2048]{1,0:T(8,128)(2,1)} %fusion.3, bf16[256,1,1024]{2,0,1:T(8,128)(2,1)S(1)} %all_gather.3), kind=kOutput, calls=%fused_computation.9 | convolution fusion | flops 1074266112 | bytes 5767168 | tf_op jit(solution)/shard_map/dot_general | solution.py:20
  73.9 0.0 reduce-scatter.2.cloned.1.call-update
  74.0 9.8 %reduce-scatter.2.cloned.1.call-done = bf16[1024,256]{1,0:T(8,128)(2,1)} async-done(((bf16[2048,256]{1,0:T(8,128)(2,1)}), bf16[1024,256]{1,0:T(8,128)(2,1)}) %reduce-scatter.2.cloned.1.call-update) | async-done | bytes 524304 | tf_op jit(solution)/shard_map/reduce_scatter | solution.py:32
  (1 shorter events, 0.0 us)
Async XLA Ops:
  6.5 77.2 %reduce-scatter.2.cloned.1.call-start = ((), (), s32[]{:S(2)}) async-start(), calls=%async_computation.1 | async-start | bytes 1572864 | tf_op jit(solution)/shard_map/reduce_scatter | solution.py:32
  12.5 11.4 %copy-start.1 = (f32[1,32,32]{2,1,0:T(8,128)S(1)}, f32[1,32,32]{2,1,0:T(8,128)}, u32[]{:S(2)}) copy-start(f32[1,32,32]{2,1,0:T(8,128)} %param.9) | copy-start | bytes 12292
  12.5 11.5 %copy-start = (bf16[32,1,1024]{2,0,1:T(8,128)(2,1)S(1)}, bf16[32,1,1024]{2,0,1:T(8,128)(2,1)}, u32[]{:S(2)}) copy-start(bf16[32,1,1024]{2,0,1:T(8,128)(2,1)} %param.6) | copy-start | bytes 196612
Sparse Core Ops, SparseCore 0:
  74.1 9.6 reduce-scatter.1
where the time goes:
time: 91 us; the launch traced here: 90.6 us
  blocking collectives  33 us (36%)
  matrix products  16.9 us (19%)
  between operations  13.4 us (15%)
  local copies, waits for them, and re-layouts  11.4 us (13%)
  waiting for transfers between devices  9.82 us (11%)
  other arithmetic  6 us (7%)
    all_gather x1, blocking collectives, on_device(): piece = lax.all_gather(train_grads, 'pb', axis=0, tiled=True)  33 us
    dot_general x1, matrix products, precondition(): jnp.einsum('qlh,lgh->qlg', scaled, kron, preferred_element_type=jnp.float32)  12.4 us
    convert_element_type x1, local copies, waits for them, and re-layouts, precondition(): kron = whole.reshape(layers, kout * kin, kout * kin).astype(jnp.bfloat16)  11.4 us
    reduce_scatter x1, waiting for transfers between devices, on_device(): lax.psum_scatter(partial_scores.astype(jnp.bfloat16), 'layer', scatter_di...  9.81 us
    convert_element_type x1, other arithmetic, precondition(): kron = whole.reshape(layers, kout * kin, kout * kin).astype(jnp.bfloat16)  6 us
    dot_general x1, matrix products, rounded_product(): lax.dot_general(left, right, (((1,), (1,)), ((), ())), preferred_element_...  4.5 us
  transfers between devices with their start and end apart: 1, of which 1 were waited for; matrix products, arithmetic and copies ran while one was open for 0% of the time, Pallas kernels for 0%

commit v1 on v0

v1 whole, which is shorter than its diff:
```python
import functools

import jax
import jax.numpy as jnp
from jax import lax
from jax.experimental import pallas as pl
from jax.experimental.pallas import tpu as pltpu
from jax.sharding import PartitionSpec as P

F32, BF16 = jnp.float32, jnp.bfloat16
VMEM = pl.BlockSpec(memory_space=pltpu.VMEM)
HIGH = lax.Precision.HIGHEST
NT = (((1,), (1,)), ((), ()))
LIMIT = 24 * 1024 * 1024


def chunk(size, most):
    return most if size % most == 0 else size


def curvature_kernel(basis_in_ref, basis_out_ref, eigen_ref, m_ref, kron_ref, scaled_ref):
    kout, kin = basis_out_ref.shape[1], basis_in_ref.shape[1]
    grad = kout * kin
    lane_out = lax.broadcasted_iota(jnp.int32, (kout, grad), 1) // kin
    repeat = (lax.broadcasted_iota(jnp.int32, (kout, grad), 0) == lane_out).astype(F32)
    lane_in = lax.broadcasted_iota(jnp.int32, (kin, grad), 1) % kin
    tile = (lax.broadcasted_iota(jnp.int32, (kin, grad), 0) == lane_in).astype(F32)
    tiled_in = jnp.dot(basis_in_ref[0], tile, precision=HIGH, preferred_element_type=F32)
    spread_out = jnp.dot(basis_out_ref[0], repeat, precision=HIGH, preferred_element_type=F32)
    tiled_eigen = jnp.dot(eigen_ref[0], tile, precision=HIGH, preferred_element_type=F32)
    inverse = 1.0 / (jnp.sum(tiled_eigen * repeat, axis=0, keepdims=True) + 0.1)
    for b in range(kout):
        rows = (spread_out[b:b + 1, :] * tiled_in).astype(BF16)
        kron_ref[pl.ds(b * kin, kin), :] = rows
        scaled_ref[pl.ds(b * kin, kin), :] = (rows.astype(F32) * inverse).astype(BF16)
    step = chunk(grad, 256)

    @pl.loop(0, grad // step)
    def _(i):
        rows = pl.ds(pl.multiple_of(i * step, step), step)
        m_ref[rows, :] = lax.dot_general(scaled_ref[rows, :], kron_ref[...], NT, preferred_element_type=F32).astype(BF16)


def curvature(basis_in, basis_out, eigenvalues):
    grad = basis_in.shape[1] * basis_out.shape[1]
    return pl.pallas_call(
        curvature_kernel,
        out_shape=jax.ShapeDtypeStruct((grad, grad), BF16),
        in_specs=[VMEM] * 3,
        out_specs=VMEM,
        scratch_shapes=[pltpu.VMEM((grad, grad), BF16)] * 2,
        compiler_params=pltpu.CompilerParams(vmem_limit_bytes=LIMIT),
        cost_estimate=pl.CostEstimate(flops=2 * grad**3, bytes_accessed=2 * grad**2, transcendentals=0),
        name="curvature",
    )(basis_in, basis_out, eigenvalues)


def outgoing_kernel(masks, *refs):
    n = len(masks)
    blocks, (m_ref, q_ref, w_ref, out_ref, t_ref) = refs[:n], refs[n:]
    half = out_ref.shape[0]
    me = lax.axis_index("pb")
    for block, mask in zip(blocks, masks):
        size = block.shape[0]
        row = 0 if mask is None else pl.multiple_of((me ^ mask) * size, size)
        t_ref[pl.ds(row, size), :] = block[...]
    train = t_ref.shape[0]
    step = chunk(train, 256)
    other = 1 - lax.axis_index("layer")

    @pl.loop(0, train // step)
    def _(i):
        rows = pl.ds(pl.multiple_of(i * step, step), step)
        w_ref[rows, :] = jnp.dot(t_ref[rows, :], m_ref[...], preferred_element_type=F32).astype(BF16)

    qstep = chunk(half, 256)

    @pl.loop(0, half // qstep)
    def _(i):
        rows = pl.ds(pl.multiple_of(i * qstep, qstep), qstep)
        left = q_ref[pl.ds(pl.multiple_of(other * half + i * qstep, qstep), qstep), :]
        out_ref[rows, :] = lax.dot_general(left, w_ref[...], NT, preferred_element_type=F32).astype(BF16)


def outgoing(blocks, masks, m, q):
    train = sum(block.shape[0] for block in blocks)
    half, grad = q.shape[0] // 2, q.shape[1]
    return pl.pallas_call(
        functools.partial(outgoing_kernel, masks),
        out_shape=(jax.ShapeDtypeStruct((train, grad), BF16), jax.ShapeDtypeStruct((half, train), BF16)),
        in_specs=[VMEM] * (len(blocks) + 2),
        out_specs=(VMEM, VMEM),
        scratch_shapes=[pltpu.VMEM((train, grad), BF16)],
        compiler_params=pltpu.CompilerParams(vmem_limit_bytes=LIMIT),
        cost_estimate=pl.CostEstimate(flops=2 * train * grad * (grad + half), bytes_accessed=2 * half * grad, transcendentals=0),
        name="outgoing",
    )(*blocks, m, q)


def own_kernel(w_ref, q_ref, out_ref):
    half = out_ref.shape[0]
    own = lax.axis_index("layer")
    step = chunk(half, 256)

    @pl.loop(0, half // step)
    def _(i):
        rows = pl.ds(pl.multiple_of(i * step, step), step)
        left = q_ref[pl.ds(pl.multiple_of(own * half + i * step, step), step), :]
        out_ref[rows, :] = lax.dot_general(left, w_ref[...], NT, preferred_element_type=F32)


def own_scores(w, q):
    train, (half, grad) = w.shape[0], (q.shape[0] // 2, q.shape[1])
    return pl.pallas_call(
        own_kernel,
        out_shape=jax.ShapeDtypeStruct((half, train), F32),
        in_specs=[VMEM, VMEM],
        out_specs=VMEM,
        compiler_params=pltpu.CompilerParams(vmem_limit_bytes=LIMIT),
        cost_estimate=pl.CostEstimate(flops=2 * train * grad * half, bytes_accessed=2 * half * grad, transcendentals=0),
        name="own_scores",
    )(w, q)


def swap(x, n, mask):
    return lax.ppermute(x, "pb", [(i, i ^ mask) for i in range(n)])


def on_device(n, query_grads, train_grads, basis_in, basis_out, eigenvalues):
    train = train_grads.reshape(train_grads.shape[0], -1)
    queries = query_grads.reshape(query_grads.shape[0], -1)
    m = curvature(basis_in, basis_out, eigenvalues)
    if n == 8:
        far = [swap(train, n, mask) for mask in (4, 6)]
        near = [swap(train, n, mask) for mask in (2, 1, 3)]
        relayed = [swap(block, n, 1) for block in far]
        blocks, masks = [train] + far + near + relayed, (0, 4, 6, 2, 1, 3, 5, 7)
    else:
        blocks, masks = [lax.all_gather(train, "pb", axis=0, tiled=True)], (None,)
    w, sent = outgoing(blocks, masks, m, queries)
    received = lax.ppermute(sent, "layer", [(0, 1), (1, 0)])
    own = own_scores(w, queries)
    return (own + received.astype(F32)).astype(BF16)


def solution(mesh):
    placed = (
        P(("grp", "pb"), "layer", None),
        P(("grp", "pb"), "layer", None),
        P("layer", None, None),
        P("layer", None, None),
        P("layer", None, None),
    )
    return jax.shard_map(
        functools.partial(on_device, mesh.shape["pb"]),
        mesh=mesh,
        in_specs=placed,
        out_specs=P(("grp", "pb", "layer"), None),
        check_vma=False,
    )
```

time: 91 us -> 24.5 us (0.27)
  blocking collectives: 33 us -> 0 us
  matrix products: 16.9 us -> 0 us
  between operations: 13.4 us -> 0.1 us
  starting transfers between devices: 0.01 us -> 11.6 us
  local copies, waits for them, and re-layouts: 11.4 us -> 2.16 us
  waiting for transfers between devices: 9.82 us -> 1.55 us
  Pallas kernels: 0 us -> 7.75 us
  other arithmetic: 6 us -> 0.91 us
    all_gather x1 -> x0, blocking collectives: 33 us -> none  [on_device(): piece = lax.all_gather(train_grads, 'pb', axis=0, tiled=True)]
    dot_general x2 -> x0, matrix products: 16.9 us -> none  [the longest x1 12.4 us: precondition(): jnp.einsum('qlh,lgh->qlg', scaled, kron, preferred_element_type=jnp.float32)]
    ppermute x0 -> x8, starting transfers between devices: none -> 11.6 us  [the longest x7 11.5 us: swap(): return lax.ppermute(x, 'pb', [(i, i ^ mask) for i in range(n)])]
    convert_element_type x1 -> x0, local copies, waits for them, and re-layouts: 11.4 us -> none  [precondition(): kron = whole.reshape(layers, kout * kin, kout * kin).astype(jnp.bfloat16)]
    reduce_scatter x1 -> x0, waiting for transfers between devices: 9.81 us -> none  [on_device(): lax.psum_scatter(partial_scores.astype(jnp.bfloat16), 'layer', scatter_di...]
    pallas_call x0 -> x3, Pallas kernels: none -> 7.75 us  [the longest x1 4.32 us: curvature(): pl.pallas_call(curvature_kernel, out_shape=jax.ShapeDtypeStruct((grad, gr...]
    convert_element_type x1, other arithmetic: 6 us -> 0.91 us  [on_device(): return (own + received.astype(F32)).astype(BF16)]
    unnamed x4 -> x10, local copies, waits for them, and re-layouts: 0.01 us -> 2.16 us
  transfers between devices with their start and end apart: 1 -> 8, of which waited for: 1 -> 2; matrix products, arithmetic and copies ran while one was open for 0% -> 0% of each run, Pallas kernels for 0% -> 24%
where the time goes in v1:
time: 24.5 us; the launch traced here: 24.1 us
  starting transfers between devices  11.6 us (47%)
  Pallas kernels  7.75 us (32%)
  local copies, waits for them, and re-layouts  2.16 us (9%)
  waiting for transfers between devices  1.55 us (6%)
  other arithmetic  0.91 us (4%)
    ppermute x7, starting transfers between devices, swap(): return lax.ppermute(x, 'pb', [(i, i ^ mask) for i in range(n)])  11.5 us
    pallas_call x1, Pallas kernels, curvature(): pl.pallas_call(curvature_kernel, out_shape=jax.ShapeDtypeStruct((grad, gr...  4.32 us
    unnamed x10, local copies, waits for them, and re-layouts  2.16 us
    pallas_call x1, Pallas kernels, outgoing(): pl.pallas_call(functools.partial(outgoing_kernel, masks), out_shape=(jax....  2.08 us
    pallas_call x1, Pallas kernels, own_scores(): pl.pallas_call(own_kernel, out_shape=jax.ShapeDtypeStruct((half, train),...  1.35 us
    ppermute x7, waiting for transfers between devices, swap(): return lax.ppermute(x, 'pb', [(i, i ^ mask) for i in range(n)])  1.01 us
    convert_element_type x1, other arithmetic, on_device(): return (own + received.astype(F32)).astype(BF16)  0.91 us
    ppermute x1, waiting for transfers between devices, on_device(): received = lax.ppermute(sent, 'layer', [(0, 1), (1, 0)])  0.54 us
  transfers between devices with their start and end apart: 8, of which 2 were waited for; matrix products, arithmetic and copies ran while one was open for 0% of the time, Pallas kernels for 24%

profile of v1, /device:TPU:0, one launch (start us, length us, event | category | flops | bytes accessed | tf_op | source)
XLA Modules:
  0.0 24.1 jit_solution(10420674190936102211)
XLA Ops:
  0.0 0.0 copy-start.1
  0.0 0.0 copy-start
  0.0 5.0 %collective-permute-start.1 = (bf16[32,1024]{1,0:T(8,128)(2,1)}, bf16[32,1024]{1,0:T(8,128)(2,1)S(1)}, u32[]{:S(2)}, u32[]{:S(2)}) collective-permute-start(bf16[32,1024]{1,0:T(8,128)(2,1)} %bitcast.4), channel_id=1, source_target_pairs={{0,12},{2,14},{4,8},{6,10},{8,4},{10,6},{12,0},{14,2},{1,13},{3,15... | collective-permute-start | bytes 196616 | tf_op jit(solution)/shard_map/ppermute | solution.py:126
  5.1 0.0 collective-permute-start
  5.1 1.7 %collective-permute-start.4 = (bf16[32,1024]{1,0:T(8,128)(2,1)}, bf16[32,1024]{1,0:T(8,128)(2,1)S(1)}, u32[]{:S(2)}, u32[]{:S(2)}) collective-permute-start(bf16[32,1024]{1,0:T(8,128)(2,1)} %bitcast.6), channel_id=1, source_target_pairs={{0,6},{2,4},{4,2},{6,0},{8,14},{10,12},{12,10},{14,8},{1,7},{3,5},... | collective-permute-start | bytes 196616 | tf_op jit(solution)/shard_map/ppermute | solution.py:126
  6.8 0.4 %collective-permute-start.3 = (bf16[32,1024]{1,0:T(8,128)(2,1)}, bf16[32,1024]{1,0:T(8,128)(2,1)S(1)}, u32[]{:S(2)}, u32[]{:S(2)}) collective-permute-start(bf16[32,1024]{1,0:T(8,128)(2,1)} %bitcast.7), channel_id=1, source_target_pairs={{0,2},{2,0},{4,6},{6,4},{8,10},{10,8},{12,14},{14,12},{1,3},{3,1},... | collective-permute-start | bytes 196616 | tf_op jit(solution)/shard_map/ppermute | solution.py:126
  7.2 1.4 %collective-permute-start.2 = (bf16[32,1024]{1,0:T(8,128)(2,1)}, bf16[32,1024]{1,0:T(8,128)(2,1)S(1)}, u32[]{:S(2)}, u32[]{:S(2)}) collective-permute-start(bf16[32,1024]{1,0:T(8,128)(2,1)} %bitcast.8), channel_id=1, source_target_pairs={{0,4},{2,6},{4,0},{6,2},{8,12},{10,14},{12,8},{14,10},{1,5},{3,7},... | collective-permute-start | bytes 196616 | tf_op jit(solution)/shard_map/ppermute | solution.py:126
  8.5 0.0 collective-permute-done.1.refs_2_
  8.6 1.5 %collective-permute-start.6 = (bf16[32,1024]{1,0:T(8,128)(2,1)S(1)}, bf16[32,1024]{1,0:T(8,128)(2,1)S(1)}, u32[]{:S(2)}, u32[]{:S(2)}) collective-permute-start(bf16[32,1024]{1,0:T(8,128)(2,1)S(1)} %collective-permute-done.1.refs_2_), channel_id=1, source_target_pairs={{0,2},{2,0},{4,6},{6,4},{8,10},{10,8},{12,14},{14,12},{1,3},{3,1},... | collective-permute-start | bytes 196616 | tf_op jit(solution)/shard_map/ppermute | solution.py:126
  10.0 1.0 %collective-permute-done.refs_1_ = bf16[32,1024]{1,0:T(8,128)(2,1)S(1)} collective-permute-done((bf16[32,1024]{1,0:T(8,128)(2,1)}, bf16[32,1024]{1,0:T(8,128)(2,1)S(1)}, u32[]{:S(2)}, u32[]{:S(2)}) %collective-permute-start) | collective-permute-done | bytes 65568 | tf_op jit(solution)/shard_map/ppermute | solution.py:126
  11.0 1.5 %collective-permute-start.5 = (bf16[32,1024]{1,0:T(8,128)(2,1)S(1)}, bf16[32,1024]{1,0:T(8,128)(2,1)S(1)}, u32[]{:S(2)}, u32[]{:S(2)}) collective-permute-start(bf16[32,1024]{1,0:T(8,128)(2,1)S(1)} %collective-permute-done.refs_1_), channel_id=1, source_target_pairs={{0,2},{2,0},{4,6},{6,4},{8,10},{10,8},{12,14},{14,12},{1,3},{3,1},... | collective-permute-start | bytes 196616 | tf_op jit(solution)/shard_map/ppermute | solution.py:126
  12.5 0.0 copy-start.2
  12.5 0.7 %copy-done.2 = f32[1,32,32]{2,1,0:T(8,128)S(1)} copy-done((f32[1,32,32]{2,1,0:T(8,128)S(1)}, f32[1,32,32]{2,1,0:T(8,128)}, u32[]{:S(2)}) %copy-start.2) | copy-done | bytes 4120
  13.2 0.0 copy-start.3
  13.2 0.7 %copy-done.3 = f32[1,32,32]{2,1,0:T(8,128)S(1)} copy-done((f32[1,32,32]{2,1,0:T(8,128)S(1)}, f32[1,32,32]{2,1,0:T(8,128)}, u32[]{:S(2)}) %copy-start.3) | copy-done | bytes 4120
  14.0 0.0 copy-start.4
  14.0 0.7 %copy-done.4 = f32[1,32,32]{2,1,0:T(8,128)S(1)} copy-done((f32[1,32,32]{2,1,0:T(8,128)S(1)}, f32[1,32,32]{2,1,0:T(8,128)}, u32[]{:S(2)}) %copy-start.4) | copy-done | bytes 4120
  14.7 4.3 %curvature.1.refs_8_ = bf16[1024,1024]{1,0:T(8,128)(2,1)S(1)} custom-call(f32[1,32,32]{2,1,0:T(8,128)S(1)} %copy-done.2, f32[1,32,32]{2,1,0:T(8,128)S(1)} %copy-done.3, f32[1,32,32]{2,1,0:T(8,128)S(1)} %copy-done.4), custom_call_target="tpu_custom_call" | custom-call | flops 2147483648 | bytes 2097152 | tf_op jit(solution)/shard_map/curvature/pallas_call | solution.py:46
  19.0 0.0 collective-permute-done.4.refs_5_
  19.0 0.0 collective-permute-done.3.refs_4_
  19.0 0.0 collective-permute-done.2.refs_3_
  19.0 0.0 collective-permute-done.6.refs_7_
  19.1 0.0 collective-permute-done.5.refs_6_
  19.1 0.0 copy-done.1
  19.1 0.0 copy-done
  19.1 2.1 %outgoing.1 = (bf16[256,1024]{1,0:T(8,128)(2,1)S(1)}, bf16[1024,256]{1,0:T(8,128)(2,1)S(1)}) custom-call(bf16[32,1024]{1,0:T(8,128)(2,1)S(1)} %bitcast.9, bf16[32,1024]{1,0:T(8,128)(2,1)S(1)} %collective-permute-done.refs_1_, bf16[32,1024]{1,0:T(8,128)(2,1)S(1)} %collective-permute-done.1.refs_2_, bf16[32,1024]{1,0:T(8,128)(2,1)S(1)} %collective-permute-done.2.refs_3_, ...), custom_call_target="tpu_custom_call" | custom-call | flops 1073741824 | bytes 2097152 | tf_op jit(solution)/shard_map/outgoing/pallas_call | solution.py:88
  21.2 0.1 collective-permute-start.7
  21.3 1.3 %own_scores.1 = f32[1024,256]{1,0:T(8,128)S(1)} custom-call(bf16[256,1024]{1,0:T(8,128)(2,1)S(1)} %get-tuple-element.7.w_ref, bf16[2048,1024]{1,0:T(8,128)(2,1)S(1)} %bitcast.3), custom_call_target="tpu_custom_call" | custom-call | flops 536870912 | bytes 2097152 | tf_op jit(solution)/shard_map/own_scores/pallas_call | solution.py:114
  22.6 0.5 %collective-permute-done.7 = bf16[1024,256]{1,0:T(8,128)(2,1)S(1)} collective-permute-done((bf16[1024,256]{1,0:T(8,128)(2,1)S(1)}, bf16[1024,256]{1,0:T(8,128)(2,1)S(1)}, u32[]{:S(2)}, u32[]{:S(2)}) %collective-permute-start.7) | collective-permute-done | bytes 524320 | tf_op jit(solution)/shard_map/ppermute | solution.py:141
  23.2 0.9 %add_convert_fusion = bf16[1024,256]{1,0:T(8,128)(2,1)} fusion(f32[1024,256]{1,0:T(8,128)S(1)} %own_scores.1, bf16[1024,256]{1,0:T(8,128)(2,1)S(1)} %collective-permute-done.7), kind=kLoop, calls=%fused_computation | loop fusion | flops 786432 | bytes 2097152 | tf_op jit(solution)/shard_map/convert_element_type | solution.py:143
Async XLA Ops:
  0.0 19.1 %copy-start.1 = (bf16[32,1,1024]{2,0,1:T(8,128)(2,1)S(1)}, bf16[32,1,1024]{2,0,1:T(8,128)(2,1)}, u32[]{:S(2)}) copy-start(bf16[32,1,1024]{2,0,1:T(8,128)(2,1)} %param.6) | copy-start | bytes 196612
  0.0 19.1 %copy-start = (bf16[2048,1,1024]{2,0,1:T(8,128)(2,1)S(1)}, bf16[2048,1,1024]{2,0,1:T(8,128)(2,1)}, u32[]{:S(2)}) copy-start(bf16[2048,1,1024]{2,0,1:T(8,128)(2,1)} %param.5) | copy-start | bytes 12582916
  0.0 8.5 %collective-permute-start.1 = (bf16[32,1024]{1,0:T(8,128)(2,1)}, bf16[32,1024]{1,0:T(8,128)(2,1)S(1)}, u32[]{:S(2)}, u32[]{:S(2)}) collective-permute-start(bf16[32,1024]{1,0:T(8,128)(2,1)} %bitcast.4), channel_id=1, source_target_pairs={{0,12},{2,14},{4,8},{6,10},{8,4},{10,6},{12,0},{14,2},{1,13},{3,15... | collective-permute-start | bytes 196616 | tf_op jit(solution)/shard_map/ppermute | solution.py:126
  5.1 6.0 %collective-permute-start = (bf16[32,1024]{1,0:T(8,128)(2,1)}, bf16[32,1024]{1,0:T(8,128)(2,1)S(1)}, u32[]{:S(2)}, u32[]{:S(2)}) collective-permute-start(bf16[32,1024]{1,0:T(8,128)(2,1)} %bitcast.5), channel_id=1, source_target_pairs={{0,8},{2,10},{4,12},{6,14},{8,0},{10,2},{12,4},{14,6},{1,9},{3,11}... | collective-permute-start | bytes 196616 | tf_op jit(solution)/shard_map/ppermute | solution.py:126
  5.1 14.0 %collective-permute-start.4 = (bf16[32,1024]{1,0:T(8,128)(2,1)}, bf16[32,1024]{1,0:T(8,128)(2,1)S(1)}, u32[]{:S(2)}, u32[]{:S(2)}) collective-permute-start(bf16[32,1024]{1,0:T(8,128)(2,1)} %bitcast.6), channel_id=1, source_target_pairs={{0,6},{2,4},{4,2},{6,0},{8,14},{10,12},{12,10},{14,8},{1,7},{3,5},... | collective-permute-start | bytes 196616 | tf_op jit(solution)/shard_map/ppermute | solution.py:126
  6.8 12.3 %collective-permute-start.3 = (bf16[32,1024]{1,0:T(8,128)(2,1)}, bf16[32,1024]{1,0:T(8,128)(2,1)S(1)}, u32[]{:S(2)}, u32[]{:S(2)}) collective-permute-start(bf16[32,1024]{1,0:T(8,128)(2,1)} %bitcast.7), channel_id=1, source_target_pairs={{0,2},{2,0},{4,6},{6,4},{8,10},{10,8},{12,14},{14,12},{1,3},{3,1},... | collective-permute-start | bytes 196616 | tf_op jit(solution)/shard_map/ppermute | solution.py:126
  7.2 11.9 %collective-permute-start.2 = (bf16[32,1024]{1,0:T(8,128)(2,1)}, bf16[32,1024]{1,0:T(8,128)(2,1)S(1)}, u32[]{:S(2)}, u32[]{:S(2)}) collective-permute-start(bf16[32,1024]{1,0:T(8,128)(2,1)} %bitcast.8), channel_id=1, source_target_pairs={{0,4},{2,6},{4,0},{6,2},{8,12},{10,14},{12,8},{14,10},{1,5},{3,7},... | collective-permute-start | bytes 196616 | tf_op jit(solution)/shard_map/ppermute | solution.py:126
  8.6 10.5 %collective-permute-start.6 = (bf16[32,1024]{1,0:T(8,128)(2,1)S(1)}, bf16[32,1024]{1,0:T(8,128)(2,1)S(1)}, u32[]{:S(2)}, u32[]{:S(2)}) collective-permute-start(bf16[32,1024]{1,0:T(8,128)(2,1)S(1)} %collective-permute-done.1.refs_2_), channel_id=1, source_target_pairs={{0,2},{2,0},{4,6},{6,4},{8,10},{10,8},{12,14},{14,12},{1,3},{3,1},... | collective-permute-start | bytes 196616 | tf_op jit(solution)/shard_map/ppermute | solution.py:126
  11.0 8.0 %collective-permute-start.5 = (bf16[32,1024]{1,0:T(8,128)(2,1)S(1)}, bf16[32,1024]{1,0:T(8,128)(2,1)S(1)}, u32[]{:S(2)}, u32[]{:S(2)}) collective-permute-start(bf16[32,1024]{1,0:T(8,128)(2,1)S(1)} %collective-permute-done.refs_1_), channel_id=1, source_target_pairs={{0,2},{2,0},{4,6},{6,4},{8,10},{10,8},{12,14},{14,12},{1,3},{3,1},... | collective-permute-start | bytes 196616 | tf_op jit(solution)/shard_map/ppermute | solution.py:126
  12.5 0.7 %copy-start.2 = (f32[1,32,32]{2,1,0:T(8,128)S(1)}, f32[1,32,32]{2,1,0:T(8,128)}, u32[]{:S(2)}) copy-start(f32[1,32,32]{2,1,0:T(8,128)} %basis_in_ref.1) | copy-start | bytes 12292
  13.2 0.7 %copy-start.3 = (f32[1,32,32]{2,1,0:T(8,128)S(1)}, f32[1,32,32]{2,1,0:T(8,128)}, u32[]{:S(2)}) copy-start(f32[1,32,32]{2,1,0:T(8,128)} %basis_out_ref.1) | copy-start | bytes 12292
  14.0 0.7 %copy-start.4 = (f32[1,32,32]{2,1,0:T(8,128)S(1)}, f32[1,32,32]{2,1,0:T(8,128)}, u32[]{:S(2)}) copy-start(f32[1,32,32]{2,1,0:T(8,128)} %eigen_ref.1) | copy-start | bytes 12292
  21.2 2.0 %collective-permute-start.7 = (bf16[1024,256]{1,0:T(8,128)(2,1)S(1)}, bf16[1024,256]{1,0:T(8,128)(2,1)S(1)}, u32[]{:S(2)}, u32[]{:S(2)}) collective-permute-start(bf16[1024,256]{1,0:T(8,128)(2,1)S(1)} %get-tuple-element.8), channel_id=1, source_target_pairs={{0,1},{1,0},{2,3},{3,2},{4,5},{5,4},{6,7},{7,6},{8,9},{9,8},{10,11... | collective-permute-start | bytes 1572872 | tf_op jit(solution)/shard_map/ppermute | solution.py:141

commit v2 on v0

v2 whole, which is shorter than its diff:
```python
import functools

import jax
import jax.numpy as jnp
from jax import lax
from jax.experimental import pallas as pl
from jax.experimental.pallas import tpu as pltpu
from jax.sharding import PartitionSpec as P

F32, BF16 = jnp.float32, jnp.bfloat16
VMEM = pl.BlockSpec(memory_space=pltpu.VMEM)
HBM = pl.BlockSpec(memory_space=pl.ANY)
HIGH = lax.Precision.HIGHEST
NT = (((1,), (1,)), ((), ()))
PARAMS = pltpu.CompilerParams(vmem_limit_bytes=24 * 1024 * 1024)


def estimate(flops, bytes_accessed):
    return pl.CostEstimate(flops=flops, bytes_accessed=bytes_accessed, transcendentals=0)


def kron_kernel(in_hbm, out_hbm, eigen_hbm, kron_ref, inverse_ref, basis_in, basis_out, eigen, sems):
    pairs = ((in_hbm, basis_in), (out_hbm, basis_out), (eigen_hbm, eigen))
    copies = [pltpu.make_async_copy(*pair, sems.at[i]) for i, pair in enumerate(pairs)]
    for copy in copies:
        copy.start()
    kout, kin = basis_out.shape[1], basis_in.shape[1]
    grad = kout * kin
    lane_out = lax.broadcasted_iota(jnp.int32, (kout, grad), 1) // kin
    repeat = (lax.broadcasted_iota(jnp.int32, (kout, grad), 0) == lane_out).astype(F32)
    lane_in = lax.broadcasted_iota(jnp.int32, (kin, grad), 1) % kin
    tile = (lax.broadcasted_iota(jnp.int32, (kin, grad), 0) == lane_in).astype(F32)
    for copy in copies:
        copy.wait()
    tiled_in = jnp.dot(basis_in[0], tile, precision=HIGH, preferred_element_type=F32)
    spread_out = jnp.dot(basis_out[0], repeat, precision=HIGH, preferred_element_type=F32)
    tiled_eigen = jnp.dot(eigen[0], tile, precision=HIGH, preferred_element_type=F32)
    inverse_ref[...] = 1.0 / (jnp.sum(tiled_eigen * repeat, axis=0, keepdims=True) + 0.1)
    for b in range(kout):
        kron_ref[pl.ds(b * kin, kin), :] = (spread_out[b:b + 1, :] * tiled_in).astype(BF16)


def kron_bases(basis_in, basis_out, eigenvalues):
    grad = basis_in.shape[1] * basis_out.shape[1]
    return pl.pallas_call(
        kron_kernel,
        out_shape=tuple(jax.ShapeDtypeStruct(*x) for x in (((grad, grad), BF16), ((1, grad), F32))),
        in_specs=[HBM] * 3,
        out_specs=(VMEM,) * 2,
        scratch_shapes=[pltpu.VMEM(x.shape, F32) for x in (basis_in, basis_out, eigenvalues)] + [pltpu.SemaphoreType.DMA((3,))],
        compiler_params=PARAMS,
        cost_estimate=estimate(4 * grad**3, 0),
        name="kron_bases",
    )(*(pltpu.with_memory_space_constraint(x, pltpu.HBM) for x in (basis_in, basis_out, eigenvalues)))


def fill_rows(masks, blocks, kron_ref, inverse_ref, w_ref, rows_ref):
    size = blocks[0].shape[0]
    for i, block in enumerate(blocks):
        rows_ref[pl.ds(i * size, size), :] = block[...]
    total = len(blocks) * size
    step = min(total, 256)
    for i in range(total // step):
        rows = pl.ds(i * step, step)
        rotated = jnp.dot(rows_ref[rows, :], kron_ref[...], preferred_element_type=F32)
        scaled = (rotated * inverse_ref[...]).astype(BF16)
        rows_ref[rows, :] = lax.dot_general(scaled, kron_ref[...], NT, preferred_element_type=F32).astype(BF16)
    me = lax.axis_index("pb")
    for i, mask in enumerate(masks):
        at = pl.multiple_of((me ^ mask) * size, size) if len(masks) > 1 else 0
        w_ref[pl.ds(at, size), :] = rows_ref[pl.ds(i * size, size), :]


def score_half(layer, q_ref, w_ref, out_ref):
    half, step = out_ref.shape[0], min(w_ref.shape[0], 256)
    rows = pl.ds(pl.multiple_of(layer * half, half), half)
    for i in range(w_ref.shape[0] // step):
        cols = slice(i * step, (i + 1) * step)
        product = lax.dot_general(q_ref[rows, :], w_ref[cols, :], NT, preferred_element_type=F32)
        out_ref[:, cols] = product.astype(out_ref.dtype)


def early_kernel(masks, *refs):
    *blocks, kron_ref, inverse_ref, w_ref, rows_ref = refs
    fill_rows(masks, blocks, kron_ref, inverse_ref, w_ref, rows_ref)


def late_kernel(masks, *refs):
    *blocks, kron_ref, inverse_ref, _, q_ref, w_ref, out_ref, rows_ref = refs
    if blocks:
        fill_rows(masks, blocks, kron_ref, inverse_ref, w_ref, rows_ref)
    score_half(1 - lax.axis_index("layer"), q_ref, w_ref, out_ref)


def own_kernel(w_ref, q_ref, out_ref):
    score_half(lax.axis_index("layer"), q_ref, w_ref, out_ref)


def early_rows(masks, blocks, kron, inverse, train):
    rows, grad = sum(block.shape[0] for block in blocks), kron.shape[0]
    return pl.pallas_call(
        functools.partial(early_kernel, masks),
        out_shape=jax.ShapeDtypeStruct((train, grad), BF16),
        in_specs=[VMEM] * (len(blocks) + 2),
        out_specs=VMEM,
        scratch_shapes=[pltpu.VMEM((rows, grad), BF16)],
        compiler_params=PARAMS,
        cost_estimate=estimate(0, 0),
        name="early_rows",
    )(*blocks, kron, inverse)


def outgoing_scores(masks, blocks, kron, inverse, w, queries):
    rows, (train, grad), half = sum(block.shape[0] for block in blocks), w.shape, queries.shape[0] // 2
    return pl.pallas_call(
        functools.partial(late_kernel, masks),
        out_shape=(jax.ShapeDtypeStruct((train, grad), BF16), jax.ShapeDtypeStruct((half, train), BF16)),
        in_specs=[VMEM] * (len(blocks) + 4),
        out_specs=(VMEM, VMEM),
        input_output_aliases={len(blocks) + 2: 0},
        scratch_shapes=[pltpu.VMEM((max(rows, 32), grad), BF16)],
        compiler_params=PARAMS,
        cost_estimate=estimate(2 * train * grad * half, 2 * half * grad),
        name="outgoing_scores",
    )(*blocks, kron, inverse, w, queries)


def own_scores(w, queries):
    (train, grad), half = w.shape, queries.shape[0] // 2
    return pl.pallas_call(
        own_kernel,
        out_shape=jax.ShapeDtypeStruct((half, train), F32),
        in_specs=[VMEM, VMEM],
        out_specs=VMEM,
        compiler_params=PARAMS,
        cost_estimate=estimate(2 * train * grad * half, 2 * half * grad),
        name="own_scores",
    )(w, queries)


def exchange(x, n, mask):
    return lax.ppermute(x, "pb", [(i, i ^ mask) for i in range(n)])


def on_device(n, query_grads, train_grads, basis_in, basis_out, eigenvalues):
    train = train_grads.reshape(train_grads.shape[0], -1)
    queries = query_grads.reshape(query_grads.shape[0], -1)
    if n == 8:
        far = [exchange(train, n, mask) for mask in (4, 6)]
        near = [exchange(train, n, mask) for mask in (2, 1, 3)]
        early, late = [train] + far + near, [exchange(block, n, 1) for block in far]
        early_masks, late_masks = (0, 4, 6, 2, 1, 3), (5, 7)
        basis_in, basis_out, eigenvalues, _ = lax.optimization_barrier((basis_in, basis_out, eigenvalues, far[0]))
    else:
        early, late = [lax.all_gather(train, "pb", axis=0, tiled=True)], []
        early_masks, late_masks = (0,), ()
    kron, inverse = kron_bases(basis_in, basis_out, eigenvalues)
    w = early_rows(early_masks, early, kron, inverse, n * train.shape[0])
    w, sent = outgoing_scores(late_masks, late, kron, inverse, w, queries)
    received = lax.ppermute(sent, "layer", [(0, 1), (1, 0)])
    return (own_scores(w, queries) + received.astype(F32)).astype(BF16)


def solution(mesh):
    placed = (
        P(("grp", "pb"), "layer", None),
        P(("grp", "pb"), "layer", None),
        P("layer", None, None),
        P("layer", None, None),
        P("layer", None, None),
    )
    return jax.shard_map(
        functools.partial(on_device, mesh.shape["pb"]),
        mesh=mesh,
        in_specs=placed,
        out_specs=P(("grp", "pb", "layer"), None),
        check_vma=False,
    )
```

time: 91 us -> 20.2 us (0.22)
  blocking collectives: 33 us -> 0 us
  matrix products: 16.9 us -> 0 us
  between operations: 13.4 us -> 0.07 us
  starting transfers between devices: 0.01 us -> 11.5 us
  local copies, waits for them, and re-layouts: 11.4 us -> 0.01 us
  waiting for transfers between devices: 9.82 us -> 2.05 us
  Pallas kernels: 0 us -> 5.51 us
  other arithmetic: 6 us -> 0.91 us
    all_gather x1 -> x0, blocking collectives: 33 us -> none  [on_device(): piece = lax.all_gather(train_grads, 'pb', axis=0, tiled=True)]
    dot_general x2 -> x0, matrix products: 16.9 us -> none  [the longest x1 12.4 us: precondition(): jnp.einsum('qlh,lgh->qlg', scaled, kron, preferred_element_type=jnp.float32)]
    ppermute x0 -> x8, starting transfers between devices: none -> 11.5 us  [the longest x7 11.4 us: exchange(): return lax.ppermute(x, 'pb', [(i, i ^ mask) for i in range(n)])]
    convert_element_type x1 -> x0, local copies, waits for them, and re-layouts: 11.4 us -> none  [precondition(): kron = whole.reshape(layers, kout * kin, kout * kin).astype(jnp.bfloat16)]
    reduce_scatter x1 -> x0, waiting for transfers between devices: 9.81 us -> none  [on_device(): lax.psum_scatter(partial_scores.astype(jnp.bfloat16), 'layer', scatter_di...]
    pallas_call x0 -> x4, Pallas kernels: none -> 5.51 us  [the longest x1 1.86 us: outgoing_scores(): pl.pallas_call(functools.partial(late_kernel, masks), out_shape=(jax.Shap...]
    convert_element_type x1, other arithmetic: 6 us -> 0.91 us  [on_device(): return (own_scores(w, queries) + received.astype(F32)).astype(BF16)]
    ppermute x0 -> x8, waiting for transfers between devices: none -> 2.05 us  [the longest x1 1.15 us: on_device(): received = lax.ppermute(sent, 'layer', [(0, 1), (1, 0)])]
  transfers between devices with their start and end apart: 1 -> 8, of which waited for: 1 -> 3; matrix products, arithmetic and copies ran while one was open for 0% -> 0% of each run, Pallas kernels for 0% -> 18%
where the time goes in v2:
time: 20.2 us; the launch traced here: 20.1 us
  starting transfers between devices  11.5 us (57%)
  Pallas kernels  5.51 us (27%)
  waiting for transfers between devices  2.05 us (10%)
  other arithmetic  0.91 us (5%)
    ppermute x7, starting transfers between devices, exchange(): return lax.ppermute(x, 'pb', [(i, i ^ mask) for i in range(n)])  11.4 us
    pallas_call x1, Pallas kernels, outgoing_scores(): pl.pallas_call(functools.partial(late_kernel, masks), out_shape=(jax.Shap...  1.86 us
    pallas_call x1, Pallas kernels, kron_bases(): pl.pallas_call(kron_kernel, out_shape=tuple((jax.ShapeDtypeStruct(*x) for...  1.64 us
    pallas_call x1, Pallas kernels, early_rows(): pl.pallas_call(functools.partial(early_kernel, masks), out_shape=jax.Shap...  1.27 us
    ppermute x1, waiting for transfers between devices, on_device(): received = lax.ppermute(sent, 'layer', [(0, 1), (1, 0)])  1.15 us
    convert_element_type x1, other arithmetic, on_device(): return (own_scores(w, queries) + received.astype(F32)).astype(BF16)  0.91 us
    ppermute x7, waiting for transfers between devices, exchange(): return lax.ppermute(x, 'pb', [(i, i ^ mask) for i in range(n)])  0.9 us
    pallas_call x1, Pallas kernels, own_scores(): pl.pallas_call(own_kernel, out_shape=jax.ShapeDtypeStruct((half, train),...  0.74 us
  transfers between devices with their start and end apart: 8, of which 3 were waited for; matrix products, arithmetic and copies ran while one was open for 0% of the time, Pallas kernels for 18%

profile of v2, /device:TPU:0, one launch (start us, length us, event | category | flops | bytes accessed | tf_op | source)
XLA Modules:
  0.0 20.1 jit_solution(1691477501445343462)
XLA Ops:
  0.0 0.0 copy-start.1
  0.0 4.0 %collective-permute-start = (bf16[32,1024]{1,0:T(8,128)(2,1)}, bf16[32,1024]{1,0:T(8,128)(2,1)S(1)}, u32[]{:S(2)}, u32[]{:S(2)}) collective-permute-start(bf16[32,1024]{1,0:T(8,128)(2,1)} %bitcast.4), channel_id=1, source_target_pairs={{0,8},{2,10},{4,12},{6,14},{8,0},{10,2},{12,4},{14,6},{1,9},{3,11}... | collective-permute-start | bytes 196616 | tf_op jit(solution)/shard_map/ppermute | solution.py:142
  4.0 1.3 %collective-permute-start.2 = (bf16[32,1024]{1,0:T(8,128)(2,1)}, bf16[32,1024]{1,0:T(8,128)(2,1)S(1)}, u32[]{:S(2)}, u32[]{:S(2)}) collective-permute-start(bf16[32,1024]{1,0:T(8,128)(2,1)} %bitcast.5), channel_id=1, source_target_pairs={{0,12},{2,14},{4,8},{6,10},{8,4},{10,6},{12,0},{14,2},{1,13},{3,15... | collective-permute-start | bytes 196616 | tf_op jit(solution)/shard_map/ppermute | solution.py:142
  5.4 1.2 %collective-permute-start.6 = (bf16[32,1024]{1,0:T(8,128)(2,1)}, bf16[32,1024]{1,0:T(8,128)(2,1)S(1)}, u32[]{:S(2)}, u32[]{:S(2)}) collective-permute-start(bf16[32,1024]{1,0:T(8,128)(2,1)} %bitcast.6), channel_id=1, source_target_pairs={{0,6},{2,4},{4,2},{6,0},{8,14},{10,12},{12,10},{14,8},{1,7},{3,5},... | collective-permute-start | bytes 196616 | tf_op jit(solution)/shard_map/ppermute | solution.py:142
  6.5 0.5 %collective-permute-start.5 = (bf16[32,1024]{1,0:T(8,128)(2,1)}, bf16[32,1024]{1,0:T(8,128)(2,1)S(1)}, u32[]{:S(2)}, u32[]{:S(2)}) collective-permute-start(bf16[32,1024]{1,0:T(8,128)(2,1)} %bitcast.7), channel_id=1, source_target_pairs={{0,2},{2,0},{4,6},{6,4},{8,10},{10,8},{12,14},{14,12},{1,3},{3,1},... | collective-permute-start | bytes 196616 | tf_op jit(solution)/shard_map/ppermute | solution.py:142
  7.1 1.8 %collective-permute-start.4 = (bf16[32,1024]{1,0:T(8,128)(2,1)}, bf16[32,1024]{1,0:T(8,128)(2,1)S(1)}, u32[]{:S(2)}, u32[]{:S(2)}) collective-permute-start(bf16[32,1024]{1,0:T(8,128)(2,1)} %bitcast.8), channel_id=1, source_target_pairs={{0,4},{2,6},{4,0},{6,2},{8,12},{10,14},{12,8},{14,10},{1,5},{3,7},... | collective-permute-start | bytes 196616 | tf_op jit(solution)/shard_map/ppermute | solution.py:142
  8.9 0.0 collective-permute-done.refs_1_
  8.9 1.7 %collective-permute-start.1 = (bf16[32,1024]{1,0:T(8,128)(2,1)S(1)}, bf16[32,1024]{1,0:T(8,128)(2,1)S(1)}, u32[]{:S(2)}, u32[]{:S(2)}) collective-permute-start(bf16[32,1024]{1,0:T(8,128)(2,1)S(1)} %collective-permute-done.refs_1_), channel_id=1, source_target_pairs={{0,2},{2,0},{4,6},{6,4},{8,10},{10,8},{12,14},{14,12},{1,3},{3,1},... | collective-permute-start | bytes 196616 | tf_op jit(solution)/shard_map/ppermute | solution.py:142
  10.6 0.5 %collective-permute-done.2.refs_2_ = bf16[32,1024]{1,0:T(8,128)(2,1)S(1)} collective-permute-done((bf16[32,1024]{1,0:T(8,128)(2,1)}, bf16[32,1024]{1,0:T(8,128)(2,1)S(1)}, u32[]{:S(2)}, u32[]{:S(2)}) %collective-permute-start.2) | collective-permute-done | bytes 65568 | tf_op jit(solution)/shard_map/ppermute | solution.py:142
  11.0 0.9 %collective-permute-start.3 = (bf16[32,1024]{1,0:T(8,128)(2,1)S(1)}, bf16[32,1024]{1,0:T(8,128)(2,1)S(1)}, u32[]{:S(2)}, u32[]{:S(2)}) collective-permute-start(bf16[32,1024]{1,0:T(8,128)(2,1)S(1)} %collective-permute-done.2.refs_2_), channel_id=1, source_target_pairs={{0,2},{2,0},{4,6},{6,4},{8,10},{10,8},{12,14},{14,12},{1,3},{3,1},... | collective-permute-start | bytes 196616 | tf_op jit(solution)/shard_map/ppermute | solution.py:142
  11.9 0.0 copy-start
  11.9 1.6 %kron_bases.1 = (bf16[1024,1024]{1,0:T(8,128)(2,1)S(1)}, f32[1,1024]{1,0:T(1,128)S(1)}) custom-call(f32[1,32,32]{2,1,0:T(8,128)} %in_hbm, f32[1,32,32]{2,1,0:T(8,128)} %out_hbm, f32[1,32,32]{2,1,0:T(8,128)} %eigen_hbm), custom_call_target="tpu_custom_call" | custom-call | flops 4294967296 | tf_op jit(solution)/shard_map/kron_bases/pallas_call | solution.py:45
  13.6 0.0 collective-permute-done.6.refs_5_
  13.6 0.0 collective-permute-done.5.refs_4_
  13.6 0.0 collective-permute-done.4.refs_3_
  13.6 0.0 copy-done.1
  13.6 1.3 %early_rows.1.refs_4_ = bf16[256,1024]{1,0:T(8,128)(2,1)S(1)} custom-call(bf16[32,1024]{1,0:T(8,128)(2,1)S(1)} %bitcast.9, bf16[32,1024]{1,0:T(8,128)(2,1)S(1)} %collective-permute-done.refs_1_, bf16[32,1024]{1,0:T(8,128)(2,1)S(1)} %collective-permute-done.2.refs_2_, bf16[32,1024]{1,0:T(8,128)(2,1)S(1)} %collective-permute-done.4.refs_3_, ...), custom_call_target="tpu_custom_call" | custom-call | tf_op jit(solution)/shard_map/early_rows/pallas_call | solution.py:101
  14.9 0.4 %collective-permute-done.3.refs_1_ = bf16[32,1024]{1,0:T(8,128)(2,1)S(1)} collective-permute-done((bf16[32,1024]{1,0:T(8,128)(2,1)S(1)}, bf16[32,1024]{1,0:T(8,128)(2,1)S(1)}, u32[]{:S(2)}, u32[]{:S(2)}) %collective-permute-start.3) | collective-permute-done | bytes 65568 | tf_op jit(solution)/shard_map/ppermute | solution.py:142
  15.3 0.0 collective-permute-done.1.refs_0_
  15.3 0.0 copy-done
  15.3 1.9 %outgoing_scores.1 = (bf16[256,1024]{1,0:T(8,128)(2,1)S(1)}, bf16[1024,256]{1,0:T(8,128)(2,1)S(1)}) custom-call(bf16[32,1024]{1,0:T(8,128)(2,1)S(1)} %collective-permute-done.1.refs_0_, bf16[32,1024]{1,0:T(8,128)(2,1)S(1)} %collective-permute-done.3.refs_1_, ...), custom_call_target="tpu_custom_call", output_to_operand_aliasing={{0}: (4, {})} | custom-call | flops 536870912 | bytes 2097152 | tf_op jit(solution)/shard_map/outgoing_scores/pallas_call | solution.py:115
  17.2 0.1 collective-permute-start.7
  17.3 0.7 %own_scores.1 = f32[1024,256]{1,0:T(8,128)S(1)} custom-call(bf16[256,1024]{1,0:T(8,128)(2,1)S(1)} %get-tuple-element.17.w_ref, bf16[2048,1024]{1,0:T(8,128)(2,1)S(1)} %bitcast.3), custom_call_target="tpu_custom_call" | custom-call | flops 536870912 | bytes 2097152 | tf_op jit(solution)/shard_map/own_scores/pallas_call | solution.py:130
  18.0 1.1 %collective-permute-done.7 = bf16[1024,256]{1,0:T(8,128)(2,1)S(1)} collective-permute-done((bf16[1024,256]{1,0:T(8,128)(2,1)S(1)}, bf16[1024,256]{1,0:T(8,128)(2,1)S(1)}, u32[]{:S(2)}, u32[]{:S(2)}) %collective-permute-start.7) | collective-permute-done | bytes 524320 | tf_op jit(solution)/shard_map/ppermute | solution.py:160
  19.1 0.9 %add_convert_fusion = bf16[1024,256]{1,0:T(8,128)(2,1)} fusion(f32[1024,256]{1,0:T(8,128)S(1)} %own_scores.1, bf16[1024,256]{1,0:T(8,128)(2,1)S(1)} %collective-permute-done.7), kind=kLoop, calls=%fused_computation | loop fusion | flops 786432 | bytes 2097152 | tf_op jit(solution)/shard_map/convert_element_type | solution.py:161
Async XLA Ops:
  0.0 13.6 %copy-start.1 = (bf16[32,1,1024]{2,0,1:T(8,128)(2,1)S(1)}, bf16[32,1,1024]{2,0,1:T(8,128)(2,1)}, u32[]{:S(2)}) copy-start(bf16[32,1,1024]{2,0,1:T(8,128)(2,1)} %param.6) | copy-start | bytes 196612
  0.0 8.9 %collective-permute-start = (bf16[32,1024]{1,0:T(8,128)(2,1)}, bf16[32,1024]{1,0:T(8,128)(2,1)S(1)}, u32[]{:S(2)}, u32[]{:S(2)}) collective-permute-start(bf16[32,1024]{1,0:T(8,128)(2,1)} %bitcast.4), channel_id=1, source_target_pairs={{0,8},{2,10},{4,12},{6,14},{8,0},{10,2},{12,4},{14,6},{1,9},{3,11}... | collective-permute-start | bytes 196616 | tf_op jit(solution)/shard_map/ppermute | solution.py:142
  4.0 7.0 %collective-permute-start.2 = (bf16[32,1024]{1,0:T(8,128)(2,1)}, bf16[32,1024]{1,0:T(8,128)(2,1)S(1)}, u32[]{:S(2)}, u32[]{:S(2)}) collective-permute-start(bf16[32,1024]{1,0:T(8,128)(2,1)} %bitcast.5), channel_id=1, source_target_pairs={{0,12},{2,14},{4,8},{6,10},{8,4},{10,6},{12,0},{14,2},{1,13},{3,15... | collective-permute-start | bytes 196616 | tf_op jit(solution)/shard_map/ppermute | solution.py:142
  5.4 8.2 %collective-permute-start.6 = (bf16[32,1024]{1,0:T(8,128)(2,1)}, bf16[32,1024]{1,0:T(8,128)(2,1)S(1)}, u32[]{:S(2)}, u32[]{:S(2)}) collective-permute-start(bf16[32,1024]{1,0:T(8,128)(2,1)} %bitcast.6), channel_id=1, source_target_pairs={{0,6},{2,4},{4,2},{6,0},{8,14},{10,12},{12,10},{14,8},{1,7},{3,5},... | collective-permute-start | bytes 196616 | tf_op jit(solution)/shard_map/ppermute | solution.py:142
  6.5 7.0 %collective-permute-start.5 = (bf16[32,1024]{1,0:T(8,128)(2,1)}, bf16[32,1024]{1,0:T(8,128)(2,1)S(1)}, u32[]{:S(2)}, u32[]{:S(2)}) collective-permute-start(bf16[32,1024]{1,0:T(8,128)(2,1)} %bitcast.7), channel_id=1, source_target_pairs={{0,2},{2,0},{4,6},{6,4},{8,10},{10,8},{12,14},{14,12},{1,3},{3,1},... | collective-permute-start | bytes 196616 | tf_op jit(solution)/shard_map/ppermute | solution.py:142
  7.1 6.5 %collective-permute-start.4 = (bf16[32,1024]{1,0:T(8,128)(2,1)}, bf16[32,1024]{1,0:T(8,128)(2,1)S(1)}, u32[]{:S(2)}, u32[]{:S(2)}) collective-permute-start(bf16[32,1024]{1,0:T(8,128)(2,1)} %bitcast.8), channel_id=1, source_target_pairs={{0,4},{2,6},{4,0},{6,2},{8,12},{10,14},{12,8},{14,10},{1,5},{3,7},... | collective-permute-start | bytes 196616 | tf_op jit(solution)/shard_map/ppermute | solution.py:142
  8.9 6.4 %collective-permute-start.1 = (bf16[32,1024]{1,0:T(8,128)(2,1)S(1)}, bf16[32,1024]{1,0:T(8,128)(2,1)S(1)}, u32[]{:S(2)}, u32[]{:S(2)}) collective-permute-start(bf16[32,1024]{1,0:T(8,128)(2,1)S(1)} %collective-permute-done.refs_1_), channel_id=1, source_target_pairs={{0,2},{2,0},{4,6},{6,4},{8,10},{10,8},{12,14},{14,12},{1,3},{3,1},... | collective-permute-start | bytes 196616 | tf_op jit(solution)/shard_map/ppermute | solution.py:142
  11.0 4.3 %collective-permute-start.3 = (bf16[32,1024]{1,0:T(8,128)(2,1)S(1)}, bf16[32,1024]{1,0:T(8,128)(2,1)S(1)}, u32[]{:S(2)}, u32[]{:S(2)}) collective-permute-start(bf16[32,1024]{1,0:T(8,128)(2,1)S(1)} %collective-permute-done.2.refs_2_), channel_id=1, source_target_pairs={{0,2},{2,0},{4,6},{6,4},{8,10},{10,8},{12,14},{14,12},{1,3},{3,1},... | collective-permute-start | bytes 196616 | tf_op jit(solution)/shard_map/ppermute | solution.py:142
  11.9 3.4 %copy-start = (bf16[2048,1,1024]{2,0,1:T(8,128)(2,1)S(1)}, bf16[2048,1,1024]{2,0,1:T(8,128)(2,1)}, u32[]{:S(2)}) copy-start(bf16[2048,1,1024]{2,0,1:T(8,128)(2,1)} %param.5) | copy-start | bytes 12582916
  17.2 2.0 %collective-permute-start.7 = (bf16[1024,256]{1,0:T(8,128)(2,1)S(1)}, bf16[1024,256]{1,0:T(8,128)(2,1)S(1)}, u32[]{:S(2)}, u32[]{:S(2)}) collective-permute-start(bf16[1024,256]{1,0:T(8,128)(2,1)S(1)} %get-tuple-element.18), channel_id=1, source_target_pairs={{0,1},{1,0},{2,3},{3,2},{4,5},{5,4},{6,7},{7,6},{8,9},{9,8},{10,11... | collective-permute-start | bytes 1572872 | tf_op jit(solution)/shard_map/ppermute | solution.py:160

commit v3 on v2

v3 whole, which is shorter than its diff:
```python
import functools

import jax
import jax.numpy as jnp
from jax import lax
from jax.experimental import pallas as pl
from jax.experimental.pallas import tpu as pltpu
from jax.sharding import PartitionSpec as P

F32, BF16 = jnp.float32, jnp.bfloat16
VMEM = pl.BlockSpec(memory_space=pltpu.VMEM)
HBM = pl.BlockSpec(memory_space=pl.ANY)
HIGH = lax.Precision.HIGHEST
NT = (((1,), (1,)), ((), ()))
PARAMS = pltpu.CompilerParams(vmem_limit_bytes=24 * 1024 * 1024)


def estimate(flops, bytes_accessed):
    return pl.CostEstimate(flops=flops, bytes_accessed=bytes_accessed, transcendentals=0)


def kron_kernel(in_hbm, out_hbm, eigen_hbm, kron_ref, inverse_ref, basis_in, basis_out, eigen, sems):
    pairs = ((in_hbm, basis_in), (out_hbm, basis_out), (eigen_hbm, eigen))
    copies = [pltpu.make_async_copy(*pair, sems.at[i]) for i, pair in enumerate(pairs)]
    for copy in copies:
        copy.start()
    kout, kin = basis_out.shape[1], basis_in.shape[1]
    grad = kout * kin
    lane_out = lax.broadcasted_iota(jnp.int32, (kout, grad), 1) // kin
    repeat = (lax.broadcasted_iota(jnp.int32, (kout, grad), 0) == lane_out).astype(F32)
    lane_in = lax.broadcasted_iota(jnp.int32, (kin, grad), 1) % kin
    tile = (lax.broadcasted_iota(jnp.int32, (kin, grad), 0) == lane_in).astype(F32)
    for copy in copies:
        copy.wait()
    tiled_in = jnp.dot(basis_in[0], tile, precision=HIGH, preferred_element_type=F32)
    spread_out = jnp.dot(basis_out[0], repeat, precision=HIGH, preferred_element_type=F32)
    tiled_eigen = jnp.dot(eigen[0], tile, precision=HIGH, preferred_element_type=F32)
    inverse_ref[...] = 1.0 / (jnp.sum(tiled_eigen * repeat, axis=0, keepdims=True) + 0.1)
    for b in range(kout):
        kron_ref[pl.ds(b * kin, kin), :] = (spread_out[b:b + 1, :] * tiled_in).astype(BF16)


def kron_bases(basis_in, basis_out, eigenvalues):
    grad = basis_in.shape[1] * basis_out.shape[1]
    return pl.pallas_call(
        kron_kernel,
        out_shape=tuple(jax.ShapeDtypeStruct(*x) for x in (((grad, grad), BF16), ((1, grad), F32))),
        in_specs=[HBM] * 3,
        out_specs=(VMEM,) * 2,
        scratch_shapes=[pltpu.VMEM(x.shape, F32) for x in (basis_in, basis_out, eigenvalues)] + [pltpu.SemaphoreType.DMA((3,))],
        compiler_params=PARAMS,
        cost_estimate=estimate(4 * grad**3, 0),
        name="kron_bases",
    )(*(pltpu.with_memory_space_constraint(x, pltpu.HBM) for x in (basis_in, basis_out, eigenvalues)))


def precondition_kernel(*refs):
    *blocks, kron_ref, inverse_ref, w_ref = refs
    size, total = blocks[0].shape[0], w_ref.shape[0]
    for i, block in enumerate(blocks):
        w_ref[pl.ds(i * size, size), :] = block[...]
    step = min(total, 256)
    for i in range(total // step):
        rows = pl.ds(i * step, step)
        rotated = jnp.dot(w_ref[rows, :], kron_ref[...], preferred_element_type=F32)
        scaled = (rotated * inverse_ref[...]).astype(BF16)
        w_ref[rows, :] = lax.dot_general(scaled, kron_ref[...], NT, preferred_element_type=F32).astype(BF16)


def precondition(blocks, kron, inverse, name):
    rows, grad = sum(block.shape[0] for block in blocks), kron.shape[0]
    return pl.pallas_call(
        precondition_kernel,
        out_shape=jax.ShapeDtypeStruct((rows, grad), BF16),
        in_specs=[VMEM] * (len(blocks) + 2),
        out_specs=VMEM,
        compiler_params=PARAMS,
        cost_estimate=estimate(0, 0),
        name=name,
    )(*blocks, kron, inverse)


def arrange(masks, groups, w_ref):
    me, size = lax.axis_index("pb"), w_ref.shape[0] // len(masks)
    i = 0
    for group in groups:
        for row in range(0, group.shape[0], size):
            at = pl.multiple_of((me ^ masks[i]) * size, size) if len(masks) > 1 else 0
            w_ref[pl.ds(at, size), :] = group[pl.ds(row, size), :]
            i += 1


def first_kernel(masks, *refs):
    *groups, q_ref, out_ref, w_ref = refs
    arrange(masks, groups, w_ref)
    half, step = out_ref.shape[0], min(w_ref.shape[0], 256)
    own = pl.ds(pl.multiple_of(lax.axis_index("layer") * half, half), half)
    for i in range(w_ref.shape[0] // step):
        cols = slice(i * step, (i + 1) * step)
        out_ref[:, cols] = lax.dot_general(q_ref[own, :], w_ref[cols, :], NT, preferred_element_type=F32)


def last_kernel(masks, *refs):
    *groups, q_ref, first_ref, out_hbm, w_ref, out_ref, sems = refs
    arrange(masks, groups, w_ref)
    half, step, parts = first_ref.shape[0], min(w_ref.shape[0], 256), sems.shape[0]
    start, rows = lax.axis_index("layer") * half, half // parts
    copies = []
    for r in range(parts):
        own = pl.ds(pl.multiple_of(start + r * rows, rows), rows)
        here = pl.ds(r * rows, rows)
        for i in range(w_ref.shape[0] // step):
            cols = slice(i * step, (i + 1) * step)
            second = lax.dot_general(q_ref[own, :], w_ref[cols, :], NT, preferred_element_type=F32)
            out_ref[here, cols] = (first_ref[here, cols] + second).astype(BF16)
        copies.append(pltpu.make_async_copy(out_ref.at[here], out_hbm.at[here], sems.at[r]))
        copies[-1].start()
    for copy in copies:
        copy.wait()


def first_scores(masks, groups, queries):
    train, grad = sum(group.shape[0] for group in groups), queries.shape[1]
    half = queries.shape[0] // 2
    return pl.pallas_call(
        functools.partial(first_kernel, masks),
        out_shape=jax.ShapeDtypeStruct((half, train), F32),
        in_specs=[VMEM] * (len(groups) + 1),
        out_specs=VMEM,
        scratch_shapes=[pltpu.VMEM((train, grad), BF16)],
        compiler_params=PARAMS,
        cost_estimate=estimate(2 * train * grad * half, 2 * half * grad),
        name="first_scores",
    )(*groups, queries)


def last_scores(masks, groups, queries, first):
    train, grad = sum(group.shape[0] for group in groups), queries.shape[1]
    half = queries.shape[0] // 2
    return pl.pallas_call(
        functools.partial(last_kernel, masks),
        out_shape=jax.ShapeDtypeStruct((half, train), BF16),
        in_specs=[VMEM] * (len(groups) + 2),
        out_specs=HBM,
        scratch_shapes=[pltpu.VMEM((train, grad), BF16), pltpu.VMEM((half, train), BF16), pltpu.SemaphoreType.DMA((2,))],
        compiler_params=PARAMS,
        cost_estimate=estimate(2 * train * grad * half, 2 * half * grad),
        name="last_scores",
    )(*groups, queries, first)


def exchange(x, n, mask):
    return lax.ppermute(x, "pb", [(i, i ^ mask) for i in range(n)])


def other_layer(x):
    return lax.ppermute(x, "layer", [(0, 1), (1, 0)])


def on_device(n, query_grads, train_grads, basis_in, basis_out, eigenvalues):
    train = train_grads.reshape(train_grads.shape[0], -1)
    queries = query_grads.reshape(query_grads.shape[0], -1)
    other_queries = other_layer(queries)
    if n == 8:
        far = [exchange(train, n, mask) for mask in (4, 6)]
        last, _ = lax.optimization_barrier((train, other_queries))
        second, _ = lax.optimization_barrier((far[1], other_queries))
        near = [exchange(block, n, mask) for block, mask in ((train, 3), (train, 1), (last, 2))]
        groups, masks = [[train] + far + near, [exchange(block, n, 1) for block in (far[0], second)]], (0, 4, 6, 3, 1, 2, 5, 7)
        basis_in, basis_out, eigenvalues, _ = lax.optimization_barrier((basis_in, basis_out, eigenvalues, far[0]))
    else:
        groups, masks = [[lax.all_gather(train, "pb", axis=0, tiled=True)]], (0,)
    kron, inverse = kron_bases(basis_in, basis_out, eigenvalues)
    own = [precondition(groups[0], kron, inverse, "early_rows")]
    if len(groups) > 1:
        own[0], *late = lax.optimization_barrier([own[0]] + groups[1])
        own.append(precondition(late, kron, inverse, "late_rows"))
    other = [other_layer(w) for w in own]
    return last_scores(masks, other, other_queries, first_scores(masks, own, queries))


def solution(mesh):
    placed = (
        P(("grp", "pb"), "layer", None),
        P(("grp", "pb"), "layer", None),
        P("layer", None, None),
        P("layer", None, None),
        P("layer", None, None),
    )
    return jax.shard_map(
        functools.partial(on_device, mesh.shape["pb"]),
        mesh=mesh,
        in_specs=placed,
        out_specs=P(("grp", "pb", "layer"), None),
        check_vma=False,
    )
```

time: 20.2 us -> 21 us (1.040)
  other arithmetic: 0.91 us -> 0 us
  Pallas kernels: 5.51 us -> 6.25 us
  waiting for transfers between devices: 2.05 us -> 2.66 us
  starting transfers between devices: 11.5 us -> 11.8 us
    ppermute x7, waiting for transfers between devices: 0.9 us -> 2.46 us  [exchange(): return lax.ppermute(x, 'pb', [(i, i ^ mask) for i in range(n)])]
    ppermute x1 -> x3, starting transfers between devices: 0.07 us -> 1.02 us  [other_layer(): return lax.ppermute(x, 'layer', [(0, 1), (1, 0)])]
    ppermute x1 -> x3, waiting for transfers between devices: 1.15 us -> 0.2 us  [other_layer(): return lax.ppermute(x, 'layer', [(0, 1), (1, 0)])]
    convert_element_type x1 -> x0, other arithmetic: 0.91 us -> none  [on_device(): return (own_scores(w, queries) + received.astype(F32)).astype(BF16)]
    pallas_call x3 -> x4, Pallas kernels: 3.87 us -> 4.76 us  [the longest x2 2.39 us: precondition(): pl.pallas_call(precondition_kernel, out_shape=jax.ShapeDtypeStruct((rows,...]
    ppermute x7, starting transfers between devices: 11.4 us -> 10.8 us  [exchange(): return lax.ppermute(x, 'pb', [(i, i ^ mask) for i in range(n)])]
  transfers between devices with their start and end apart: 8 -> 10, of which waited for: 3 -> 4; matrix products, arithmetic and copies ran while one was open for 0% -> 0% of each run, Pallas kernels for 18% -> 22%
where the time goes in v3:
time: 21 us; the launch traced here: 20.8 us
  starting transfers between devices  11.8 us (56%)
  Pallas kernels  6.25 us (30%)
  waiting for transfers between devices  2.66 us (13%)
    ppermute x7, starting transfers between devices, exchange(): return lax.ppermute(x, 'pb', [(i, i ^ mask) for i in range(n)])  10.8 us
    ppermute x7, waiting for transfers between devices, exchange(): return lax.ppermute(x, 'pb', [(i, i ^ mask) for i in range(n)])  2.46 us
    pallas_call x2, Pallas kernels, precondition(): pl.pallas_call(precondition_kernel, out_shape=jax.ShapeDtypeStruct((rows,...  2.39 us
    pallas_call x1, Pallas kernels, last_scores(): pl.pallas_call(functools.partial(last_kernel, masks), out_shape=jax.Shape...  1.6 us
    pallas_call x1, Pallas kernels, kron_bases(): pl.pallas_call(kron_kernel, out_shape=tuple((jax.ShapeDtypeStruct(*x) for...  1.49 us
    ppermute x3, starting transfers between devices, other_layer(): return lax.ppermute(x, 'layer', [(0, 1), (1, 0)])  1.02 us
    pallas_call x1, Pallas kernels, first_scores(): pl.pallas_call(functools.partial(first_kernel, masks), out_shape=jax.Shap...  0.78 us
  transfers between devices with their start and end apart: 10, of which 4 were waited for; matrix products, arithmetic and copies ran while one was open for 0% of the time, Pallas kernels for 22%

profile of v3, /device:TPU:0, one launch (start us, length us, event | category | flops | bytes accessed | tf_op | source)
XLA Modules:
  0.0 20.8 jit_solution(9101061960022382689)
XLA Ops:
  0.0 0.5 %collective-permute-start.4 = (bf16[2048,1024]{1,0:T(8,128)(2,1)}, bf16[2048,1024]{1,0:T(8,128)(2,1)S(1)}, u32[]{:S(2)}, u32[]{:S(2)}) collective-permute-start(bf16[2048,1024]{1,0:T(8,128)(2,1)} %bitcast.2), channel_id=1, source_target_pairs={{0,1},{1,0},{2,3},{3,2},{4,5},{5,4},{6,7},{7,6},{8,9},{9,8},{10,11... | collective-permute-start | bytes 12582920 | tf_op jit(solution)/shard_map/ppermute | solution.py:157
  0.5 0.0 copy-start.1
  0.5 3.6 %collective-permute-start = (bf16[32,1024]{1,0:T(8,128)(2,1)}, bf16[32,1024]{1,0:T(8,128)(2,1)S(1)}, u32[]{:S(2)}, u32[]{:S(2)}) collective-permute-start(bf16[32,1024]{1,0:T(8,128)(2,1)} %bitcast.4), channel_id=1, source_target_pairs={{0,8},{2,10},{4,12},{6,14},{8,0},{10,2},{12,4},{14,6},{1,9},{3,11}... | collective-permute-start | bytes 196616 | tf_op jit(solution)/shard_map/ppermute | solution.py:153
  4.1 1.3 %collective-permute-start.1 = (bf16[32,1024]{1,0:T(8,128)(2,1)}, bf16[32,1024]{1,0:T(8,128)(2,1)S(1)}, u32[]{:S(2)}, u32[]{:S(2)}) collective-permute-start(bf16[32,1024]{1,0:T(8,128)(2,1)} %bitcast.5), channel_id=1, source_target_pairs={{0,12},{2,14},{4,8},{6,10},{8,4},{10,6},{12,0},{14,2},{1,13},{3,15... | collective-permute-start | bytes 196616 | tf_op jit(solution)/shard_map/ppermute | solution.py:153
  5.5 1.2 %collective-permute-start.2 = (bf16[32,1024]{1,0:T(8,128)(2,1)}, bf16[32,1024]{1,0:T(8,128)(2,1)S(1)}, u32[]{:S(2)}, u32[]{:S(2)}) collective-permute-start(bf16[32,1024]{1,0:T(8,128)(2,1)} %bitcast.6), channel_id=1, source_target_pairs={{0,6},{2,4},{4,2},{6,0},{8,14},{10,12},{12,10},{14,8},{1,7},{3,5},... | collective-permute-start | bytes 196616 | tf_op jit(solution)/shard_map/ppermute | solution.py:153
  6.6 0.5 %collective-permute-start.3 = (bf16[32,1024]{1,0:T(8,128)(2,1)}, bf16[32,1024]{1,0:T(8,128)(2,1)S(1)}, u32[]{:S(2)}, u32[]{:S(2)}) collective-permute-start(bf16[32,1024]{1,0:T(8,128)(2,1)} %bitcast.7), channel_id=1, source_target_pairs={{0,2},{2,0},{4,6},{6,4},{8,10},{10,8},{12,14},{14,12},{1,3},{3,1},... | collective-permute-start | bytes 196616 | tf_op jit(solution)/shard_map/ppermute | solution.py:153
  7.1 1.5 %collective-permute-done.refs_1_ = bf16[32,1024]{1,0:T(8,128)(2,1)S(1)} collective-permute-done((bf16[32,1024]{1,0:T(8,128)(2,1)}, bf16[32,1024]{1,0:T(8,128)(2,1)S(1)}, u32[]{:S(2)}, u32[]{:S(2)}) %collective-permute-start) | collective-permute-done | bytes 65568 | tf_op jit(solution)/shard_map/ppermute | solution.py:153
  8.7 1.5 %collective-permute-start.6 = (bf16[32,1024]{1,0:T(8,128)(2,1)S(1)}, bf16[32,1024]{1,0:T(8,128)(2,1)S(1)}, u32[]{:S(2)}, u32[]{:S(2)}) collective-permute-start(bf16[32,1024]{1,0:T(8,128)(2,1)S(1)} %collective-permute-done.refs_1_), channel_id=1, source_target_pairs={{0,2},{2,0},{4,6},{6,4},{8,10},{10,8},{12,14},{14,12},{1,3},{3,1},... | collective-permute-start | bytes 196616 | tf_op jit(solution)/shard_map/ppermute | solution.py:153
  10.2 0.0 collective-permute-done.4.refs_2_
  10.2 2.0 %collective-permute-start.5 = (bf16[32,1024]{1,0:T(8,128)(2,1)}, bf16[32,1024]{1,0:T(8,128)(2,1)S(1)}, u32[]{:S(2)}, u32[]{:S(2)}) collective-permute-start(bf16[32,1024]{1,0:T(8,128)(2,1)} %bitcast.8), channel_id=1, source_target_pairs={{0,4},{2,6},{4,0},{6,2},{8,12},{10,14},{12,8},{14,10},{1,5},{3,7},... | collective-permute-start | bytes 196616 | tf_op jit(solution)/shard_map/ppermute | solution.py:153
  12.2 0.0 collective-permute-done.1.refs_2_
  12.2 0.5 %collective-permute-start.7 = (bf16[32,1024]{1,0:T(8,128)(2,1)S(1)}, bf16[32,1024]{1,0:T(8,128)(2,1)S(1)}, u32[]{:S(2)}, u32[]{:S(2)}) collective-permute-start(bf16[32,1024]{1,0:T(8,128)(2,1)S(1)} %collective-permute-done.1.refs_2_), channel_id=1, source_target_pairs={{0,2},{2,0},{4,6},{6,4},{8,10},{10,8},{12,14},{14,12},{1,3},{3,1},... | collective-permute-start | bytes 196616 | tf_op jit(solution)/shard_map/ppermute | solution.py:153
  12.8 1.5 %kron_bases.1 = (bf16[1024,1024]{1,0:T(8,128)(2,1)S(1)}, f32[1,1024]{1,0:T(1,128)S(1)}) custom-call(f32[1,32,32]{2,1,0:T(8,128)} %in_hbm, f32[1,32,32]{2,1,0:T(8,128)} %out_hbm, f32[1,32,32]{2,1,0:T(8,128)} %eigen_hbm), custom_call_target="tpu_custom_call" | custom-call | flops 4294967296 | tf_op jit(solution)/shard_map/kron_bases/pallas_call | solution.py:45
  14.3 0.0 copy-start
  14.3 0.0 collective-permute-done.2.refs_3_
  14.3 0.0 collective-permute-done.3.refs_4_
  14.3 0.4 %collective-permute-done.5.refs_5_ = bf16[32,1024]{1,0:T(8,128)(2,1)S(1)} collective-permute-done((bf16[32,1024]{1,0:T(8,128)(2,1)}, bf16[32,1024]{1,0:T(8,128)(2,1)S(1)}, u32[]{:S(2)}, u32[]{:S(2)}) %collective-permute-start.5) | collective-permute-done | bytes 65568 | tf_op jit(solution)/shard_map/ppermute | solution.py:153
  14.7 0.0 copy-done.1
  14.7 1.3 %early_rows.1.refs_0_ = bf16[192,1024]{1,0:T(8,128)(2,1)S(1)} custom-call(bf16[32,1024]{1,0:T(8,128)(2,1)S(1)} %bitcast.9, bf16[32,1024]{1,0:T(8,128)(2,1)S(1)} %collective-permute-done.refs_1_, bf16[32,1024]{1,0:T(8,128)(2,1)S(1)} %collective-permute-done.1.refs_2_, bf16[32,1024]{1,0:T(8,128)(2,1)S(1)} %collective-permute-done.2.refs_3_, ...), custom_call_target="tpu_custom_call" | custom-call | tf_op jit(solution)/shard_map/early_rows/pallas_call | solution.py:72
  16.0 0.0 collective-permute-done.6.refs_0_
  16.0 0.5 %collective-permute-done.7.refs_1_ = bf16[32,1024]{1,0:T(8,128)(2,1)S(1)} collective-permute-done((bf16[32,1024]{1,0:T(8,128)(2,1)S(1)}, bf16[32,1024]{1,0:T(8,128)(2,1)S(1)}, u32[]{:S(2)}, u32[]{:S(2)}) %collective-permute-start.7) | collective-permute-done | bytes 65568 | tf_op jit(solution)/shard_map/ppermute | solution.py:153
  16.5 0.0 collective-permute-start.8
  16.5 1.1 %late_rows.1.refs_1_ = bf16[64,1024]{1,0:T(8,128)(2,1)S(1)} custom-call(bf16[32,1024]{1,0:T(8,128)(2,1)S(1)} %collective-permute-done.6.refs_0_, bf16[32,1024]{1,0:T(8,128)(2,1)S(1)} %collective-permute-done.7.refs_1_, bf16[1024,1024]{1,0:T(8,128)(2,1)S(1)} %get-tuple-element.19.refs_6_.refs_2_, f32[1,1024]{1,0:T(1,128)S(1)} %get-tuple-element.20.refs_7_.refs_3_), custom_call_target="tpu_custom_call" | custom-call | tf_op jit(solution)/shard_map/late_rows/pallas_call | solution.py:72
  17.6 0.6 %collective-permute-start.9 = (bf16[64,1024]{1,0:T(8,128)(2,1)S(1)}, bf16[64,1024]{1,0:T(8,128)(2,1)S(1)}, u32[]{:S(2)}, u32[]{:S(2)}) collective-permute-start(bf16[64,1024]{1,0:T(8,128)(2,1)S(1)} %late_rows.1.refs_1_), channel_id=1, source_target_pairs={{0,1},{1,0},{2,3},{3,2},{4,5},{5,4},{6,7},{7,6},{8,9},{9,8},{10,11... | collective-permute-start | bytes 393224 | tf_op jit(solution)/shard_map/ppermute | solution.py:157
  18.2 0.0 copy-done
  18.2 0.8 %first_scores.1.refs_3_ = f32[1024,256]{1,0:T(8,128)S(1)} custom-call(bf16[192,1024]{1,0:T(8,128)(2,1)S(1)} %early_rows.1.refs_0_, bf16[64,1024]{1,0:T(8,128)(2,1)S(1)} %late_rows.1.refs_1_, bf16[2048,1024]{1,0:T(8,128)(2,1)S(1)} %bitcast.3), custom_call_target="tpu_custom_call" | custom-call | flops 536870912 | bytes 2097152 | tf_op jit(solution)/shard_map/first_scores/pallas_call | solution.py:125
  19.0 0.2 collective-permute-done.9.refs_1_
  19.2 0.0 collective-permute-done.8.refs_0_
  19.2 1.6 %last_scores.1 = bf16[1024,256]{1,0:T(8,128)(2,1)} custom-call(bf16[192,1024]{1,0:T(8,128)(2,1)S(1)} %collective-permute-done.8.refs_0_, bf16[64,1024]{1,0:T(8,128)(2,1)S(1)} %collective-permute-done.9.refs_1_, bf16[2048,1024]{1,0:T(8,128)(2,1)S(1)} %collective-permute-done.4.refs_2_, f32[1024,256]{1,0:T(8,128)S(1)} %first_scores.1.refs_3_), custom_call_target="tpu_custom_call" | custom-call | flops 536870912 | bytes 2097152 | tf_op jit(solution)/shard_map/last_scores/pallas_call | solution.py:140
Async XLA Ops:
  0.0 10.2 %collective-permute-start.4 = (bf16[2048,1024]{1,0:T(8,128)(2,1)}, bf16[2048,1024]{1,0:T(8,128)(2,1)S(1)}, u32[]{:S(2)}, u32[]{:S(2)}) collective-permute-start(bf16[2048,1024]{1,0:T(8,128)(2,1)} %bitcast.2), channel_id=1, source_target_pairs={{0,1},{1,0},{2,3},{3,2},{4,5},{5,4},{6,7},{7,6},{8,9},{9,8},{10,11... | collective-permute-start | bytes 12582920 | tf_op jit(solution)/shard_map/ppermute | solution.py:157
  0.5 14.2 %copy-start.1 = (bf16[32,1,1024]{2,0,1:T(8,128)(2,1)S(1)}, bf16[32,1,1024]{2,0,1:T(8,128)(2,1)}, u32[]{:S(2)}) copy-start(bf16[32,1,1024]{2,0,1:T(8,128)(2,1)} %param.6) | copy-start | bytes 196612
  0.5 8.2 %collective-permute-start = (bf16[32,1024]{1,0:T(8,128)(2,1)}, bf16[32,1024]{1,0:T(8,128)(2,1)S(1)}, u32[]{:S(2)}, u32[]{:S(2)}) collective-permute-start(bf16[32,1024]{1,0:T(8,128)(2,1)} %bitcast.4), channel_id=1, source_target_pairs={{0,8},{2,10},{4,12},{6,14},{8,0},{10,2},{12,4},{14,6},{1,9},{3,11}... | collective-permute-start | bytes 196616 | tf_op jit(solution)/shard_map/ppermute | solution.py:153
  4.1 8.1 %collective-permute-start.1 = (bf16[32,1024]{1,0:T(8,128)(2,1)}, bf16[32,1024]{1,0:T(8,128)(2,1)S(1)}, u32[]{:S(2)}, u32[]{:S(2)}) collective-permute-start(bf16[32,1024]{1,0:T(8,128)(2,1)} %bitcast.5), channel_id=1, source_target_pairs={{0,12},{2,14},{4,8},{6,10},{8,4},{10,6},{12,0},{14,2},{1,13},{3,15... | collective-permute-start | bytes 196616 | tf_op jit(solution)/shard_map/ppermute | solution.py:153
  5.5 8.8 %collective-permute-start.2 = (bf16[32,1024]{1,0:T(8,128)(2,1)}, bf16[32,1024]{1,0:T(8,128)(2,1)S(1)}, u32[]{:S(2)}, u32[]{:S(2)}) collective-permute-start(bf16[32,1024]{1,0:T(8,128)(2,1)} %bitcast.6), channel_id=1, source_target_pairs={{0,6},{2,4},{4,2},{6,0},{8,14},{10,12},{12,10},{14,8},{1,7},{3,5},... | collective-permute-start | bytes 196616 | tf_op jit(solution)/shard_map/ppermute | solution.py:153
  6.6 7.7 %collective-permute-start.3 = (bf16[32,1024]{1,0:T(8,128)(2,1)}, bf16[32,1024]{1,0:T(8,128)(2,1)S(1)}, u32[]{:S(2)}, u32[]{:S(2)}) collective-permute-start(bf16[32,1024]{1,0:T(8,128)(2,1)} %bitcast.7), channel_id=1, source_target_pairs={{0,2},{2,0},{4,6},{6,4},{8,10},{10,8},{12,14},{14,12},{1,3},{3,1},... | collective-permute-start | bytes 196616 | tf_op jit(solution)/shard_map/ppermute | solution.py:153
  8.7 7.3 %collective-permute-start.6 = (bf16[32,1024]{1,0:T(8,128)(2,1)S(1)}, bf16[32,1024]{1,0:T(8,128)(2,1)S(1)}, u32[]{:S(2)}, u32[]{:S(2)}) collective-permute-start(bf16[32,1024]{1,0:T(8,128)(2,1)S(1)} %collective-permute-done.refs_1_), channel_id=1, source_target_pairs={{0,2},{2,0},{4,6},{6,4},{8,10},{10,8},{12,14},{14,12},{1,3},{3,1},... | collective-permute-start | bytes 196616 | tf_op jit(solution)/shard_map/ppermute | solution.py:153
  10.2 4.5 %collective-permute-start.5 = (bf16[32,1024]{1,0:T(8,128)(2,1)}, bf16[32,1024]{1,0:T(8,128)(2,1)S(1)}, u32[]{:S(2)}, u32[]{:S(2)}) collective-permute-start(bf16[32,1024]{1,0:T(8,128)(2,1)} %bitcast.8), channel_id=1, source_target_pairs={{0,4},{2,6},{4,0},{6,2},{8,12},{10,14},{12,8},{14,10},{1,5},{3,7},... | collective-permute-start | bytes 196616 | tf_op jit(solution)/shard_map/ppermute | solution.py:153
  12.2 4.3 %collective-permute-start.7 = (bf16[32,1024]{1,0:T(8,128)(2,1)S(1)}, bf16[32,1024]{1,0:T(8,128)(2,1)S(1)}, u32[]{:S(2)}, u32[]{:S(2)}) collective-permute-start(bf16[32,1024]{1,0:T(8,128)(2,1)S(1)} %collective-permute-done.1.refs_2_), channel_id=1, source_target_pairs={{0,2},{2,0},{4,6},{6,4},{8,10},{10,8},{12,14},{14,12},{1,3},{3,1},... | collective-permute-start | bytes 196616 | tf_op jit(solution)/shard_map/ppermute | solution.py:153
  14.3 3.9 %copy-start = (bf16[2048,1,1024]{2,0,1:T(8,128)(2,1)S(1)}, bf16[2048,1,1024]{2,0,1:T(8,128)(2,1)}, u32[]{:S(2)}) copy-start(bf16[2048,1,1024]{2,0,1:T(8,128)(2,1)} %param.5) | copy-start | bytes 12582916
  16.5 2.7 %collective-permute-start.8 = (bf16[192,1024]{1,0:T(8,128)(2,1)S(1)}, bf16[192,1024]{1,0:T(8,128)(2,1)S(1)}, u32[]{:S(2)}, u32[]{:S(2)}) collective-permute-start(bf16[192,1024]{1,0:T(8,128)(2,1)S(1)} %early_rows.1.refs_0_), channel_id=1, source_target_pairs={{0,1},{1,0},{2,3},{3,2},{4,5},{5,4},{6,7},{7,6},{8,9},{9,8},{10,11... | collective-permute-start | bytes 1179656 | tf_op jit(solution)/shard_map/ppermute | solution.py:157
  17.6 1.6 %collective-permute-start.9 = (bf16[64,1024]{1,0:T(8,128)(2,1)S(1)}, bf16[64,1024]{1,0:T(8,128)(2,1)S(1)}, u32[]{:S(2)}, u32[]{:S(2)}) collective-permute-start(bf16[64,1024]{1,0:T(8,128)(2,1)S(1)} %late_rows.1.refs_1_), channel_id=1, source_target_pairs={{0,1},{1,0},{2,3},{3,2},{4,5},{5,4},{6,7},{7,6},{8,9},{9,8},{10,11... | collective-permute-start | bytes 393224 | tf_op jit(solution)/shard_map/ppermute | solution.py:157

commit v4 on v2

--- a/solution.py
+++ b/solution.py
@@ -19,7 +19,7 @@
     return pl.CostEstimate(flops=flops, bytes_accessed=bytes_accessed, transcendentals=0)
 
 
-def kron_kernel(in_hbm, out_hbm, eigen_hbm, kron_ref, inverse_ref, basis_in, basis_out, eigen, sems):
+def kron_kernel(in_hbm, out_hbm, eigen_hbm, kron_ref, turned_ref, inverse_ref, basis_in, basis_out, eigen, sems):
     pairs = ((in_hbm, basis_in), (out_hbm, basis_out), (eigen_hbm, eigen))
     copies = [pltpu.make_async_copy(*pair, sems.at[i]) for i, pair in enumerate(pairs)]
     for copy in copies:
@@ -32,29 +32,33 @@
     tile = (lax.broadcasted_iota(jnp.int32, (kin, grad), 0) == lane_in).astype(F32)
     for copy in copies:
         copy.wait()
-    tiled_in = jnp.dot(basis_in[0], tile, precision=HIGH, preferred_element_type=F32)
-    spread_out = jnp.dot(basis_out[0], repeat, precision=HIGH, preferred_element_type=F32)
-    tiled_eigen = jnp.dot(eigen[0], tile, precision=HIGH, preferred_element_type=F32)
+    inner = jnp.concatenate([basis_in[0], basis_in[0].T, eigen[0]], axis=0)
+    outer = jnp.concatenate([basis_out[0], basis_out[0].T], axis=0)
+    tiled = jnp.dot(inner, tile, precision=HIGH, preferred_element_type=F32)
+    spread = jnp.dot(outer, repeat, precision=HIGH, preferred_element_type=F32)
+    tiled_in, turned_in, tiled_eigen = tiled[:kin], tiled[kin:2 * kin], tiled[2 * kin:]
     inverse_ref[...] = 1.0 / (jnp.sum(tiled_eigen * repeat, axis=0, keepdims=True) + 0.1)
     for b in range(kout):
-        kron_ref[pl.ds(b * kin, kin), :] = (spread_out[b:b + 1, :] * tiled_in).astype(BF16)
+        kron_ref[pl.ds(b * kin, kin), :] = (spread[b:b + 1, :] * tiled_in).astype(BF16)
+        turned_ref[pl.ds(b * kin, kin), :] = (spread[kout + b:kout + b + 1, :] * turned_in).astype(BF16)
 
 
 def kron_bases(basis_in, basis_out, eigenvalues):
     grad = basis_in.shape[1] * basis_out.shape[1]
+    args = [pltpu.with_memory_space_constraint(x, pltpu.HBM) for x in (basis_in, basis_out, eigenvalues)]
     return pl.pallas_call(
         kron_kernel,
-        out_shape=tuple(jax.ShapeDtypeStruct(*x) for x in (((grad, grad), BF16), ((1, grad), F32))),
+        out_shape=tuple(jax.ShapeDtypeStruct(*x) for x in (((grad, grad), BF16), ((grad, grad), BF16), ((1, grad), F32))),
         in_specs=[HBM] * 3,
-        out_specs=(VMEM,) * 2,
-        scratch_shapes=[pltpu.VMEM(x.shape, F32) for x in (basis_in, basis_out, eigenvalues)] + [pltpu.SemaphoreType.DMA((3,))],
+        out_specs=(VMEM,) * 3,
+        scratch_shapes=[pltpu.VMEM(x.shape, F32) for x in args] + [pltpu.SemaphoreType.DMA((3,))],
         compiler_params=PARAMS,
         cost_estimate=estimate(4 * grad**3, 0),
         name="kron_bases",
-    )(*(pltpu.with_memory_space_constraint(x, pltpu.HBM) for x in (basis_in, basis_out, eigenvalues)))
-
-
-def fill_rows(masks, blocks, kron_ref, inverse_ref, w_ref, rows_ref):
+    )(*args)
+
+
+def fill_rows(masks, blocks, kron_ref, turned_ref, inverse_ref, w_ref, rows_ref):
     size = blocks[0].shape[0]
     for i, block in enumerate(blocks):
         rows_ref[pl.ds(i * size, size), :] = block[...]
@@ -64,7 +68,7 @@
         rows = pl.ds(i * step, step)
         rotated = jnp.dot(rows_ref[rows, :], kron_ref[...], preferred_element_type=F32)
         scaled = (rotated * inverse_ref[...]).astype(BF16)
-        rows_ref[rows, :] = lax.dot_general(scaled, kron_ref[...], NT, preferred_element_type=F32).astype(BF16)
+        rows_ref[rows, :] = jnp.dot(scaled, turned_ref[...], preferred_element_type=F32).astype(BF16)
     me = lax.axis_index("pb")
     for i, mask in enumerate(masks):
         at = pl.multiple_of((me ^ mask) * size, size) if len(masks) > 1 else 0
@@ -81,14 +85,14 @@
 
 
 def early_kernel(masks, *refs):
-    *blocks, kron_ref, inverse_ref, w_ref, rows_ref = refs
-    fill_rows(masks, blocks, kron_ref, inverse_ref, w_ref, rows_ref)
+    *blocks, kron_ref, turned_ref, inverse_ref, w_ref, rows_ref = refs
+    fill_rows(masks, blocks, kron_ref, turned_ref, inverse_ref, w_ref, rows_ref)
 
 
 def late_kernel(masks, *refs):
-    *blocks, kron_ref, inverse_ref, _, q_ref, w_ref, out_ref, rows_ref = refs
+    *blocks, kron_ref, turned_ref, inverse_ref, _, q_ref, w_ref, out_ref, rows_ref = refs
     if blocks:
-        fill_rows(masks, blocks, kron_ref, inverse_ref, w_ref, rows_ref)
+        fill_rows(masks, blocks, kron_ref, turned_ref, inverse_ref, w_ref, rows_ref)
     score_half(1 - lax.axis_index("layer"), q_ref, w_ref, out_ref)
 
 
@@ -96,33 +100,33 @@
     score_half(lax.axis_index("layer"), q_ref, w_ref, out_ref)
 
 
-def early_rows(masks, blocks, kron, inverse, train):
-    rows, grad = sum(block.shape[0] for block in blocks), kron.shape[0]
+def early_rows(masks, blocks, bases, train):
+    rows, grad = sum(block.shape[0] for block in blocks), bases[0].shape[0]
     return pl.pallas_call(
         functools.partial(early_kernel, masks),
         out_shape=jax.ShapeDtypeStruct((train, grad), BF16),
-        in_specs=[VMEM] * (len(blocks) + 2),
+        in_specs=[VMEM] * (len(blocks) + 3),
         out_specs=VMEM,
         scratch_shapes=[pltpu.VMEM((rows, grad), BF16)],
         compiler_params=PARAMS,
         cost_estimate=estimate(0, 0),
         name="early_rows",
-    )(*blocks, kron, inverse)
-
-
-def outgoing_scores(masks, blocks, kron, inverse, w, queries):
+    )(*blocks, *bases)
+
+
+def outgoing_scores(masks, blocks, bases, w, queries):
     rows, (train, grad), half = sum(block.shape[0] for block in blocks), w.shape, queries.shape[0] // 2
     return pl.pallas_call(
         functools.partial(late_kernel, masks),
         out_shape=(jax.ShapeDtypeStruct((train, grad), BF16), jax.ShapeDtypeStruct((half, train), BF16)),
-        in_specs=[VMEM] * (len(blocks) + 4),
+        in_specs=[VMEM] * (len(blocks) + 5),
         out_specs=(VMEM, VMEM),
-        input_output_aliases={len(blocks) + 2: 0},
+        input_output_aliases={len(blocks) + 3: 0},
         scratch_shapes=[pltpu.VMEM((max(rows, 32), grad), BF16)],
         compiler_params=PARAMS,
         cost_estimate=estimate(2 * train * grad * half, 2 * half * grad),
         name="outgoing_scores",
-    )(*blocks, kron, inverse, w, queries)
+    )(*blocks, *bases, w, queries)
 
 
 def own_scores(w, queries):
@@ -136,6 +140,31 @@
         cost_estimate=estimate(2 * train * grad * half, 2 * half * grad),
         name="own_scores",
     )(w, queries)
+
+
+def add_kernel(own_ref, received_ref, out_hbm, out_ref, sems):
+    rows = own_ref.shape[0] // sems.shape[0]
+    copies = []
+    for i in range(sems.shape[0]):
+        here = pl.ds(i * rows, rows)
+        out_ref[here, :] = (own_ref[here, :] + received_ref[here, :].astype(F32)).astype(BF16)
+        copies.append(pltpu.make_async_copy(out_ref.at[here], out_hbm.at[here], sems.at[i]))
+        copies[-1].start()
+    for copy in copies:
+        copy.wait()
+
+
+def add_scores(own, received):
+    return pl.pallas_call(
+        add_kernel,
+        out_shape=jax.ShapeDtypeStruct(own.shape, BF16),
+        in_specs=[VMEM, VMEM],
+        out_specs=HBM,
+        scratch_shapes=[pltpu.VMEM(own.shape, BF16), pltpu.SemaphoreType.DMA((4,))],
+        compiler_params=PARAMS,
+        cost_estimate=estimate(0, 0),
+        name="add_scores",
+    )(own, received)
 
 
 def exchange(x, n, mask):
@@ -154,11 +183,11 @@
     else:
         early, late = [lax.all_gather(train, "pb", axis=0, tiled=True)], []
         early_masks, late_masks = (0,), ()
-    kron, inverse = kron_bases(basis_in, basis_out, eigenvalues)
-    w = early_rows(early_masks, early, kron, inverse, n * train.shape[0])
-    w, sent = outgoing_scores(late_masks, late, kron, inverse, w, queries)
+    bases = kron_bases(basis_in, basis_out, eigenvalues)
+    w = early_rows(early_masks, early, bases, n * train.shape[0])
+    w, sent = outgoing_scores(late_masks, late, bases, w, queries)
     received = lax.ppermute(sent, "layer", [(0, 1), (1, 0)])
-    return (own_scores(w, queries) + received.astype(F32)).astype(BF16)
+    return add_scores(own_scores(w, queries), received)
 
 
 def solution(mesh):

time: 20.2 us -> 20.9 us (1.035)
  local copies, waits for them, and re-layouts: 0.01 us -> 0.98 us
  other arithmetic: 0.91 us -> 0 us
  Pallas kernels: 5.51 us -> 6.3 us
  waiting for transfers between devices: 2.05 us -> 1.83 us
    unnamed x4, local copies, waits for them, and re-layouts: 0.01 us -> 0.98 us
    convert_element_type x1 -> x0, other arithmetic: 0.91 us -> none  [on_device(): return (own_scores(w, queries) + received.astype(F32)).astype(BF16)]
    pallas_call x0 -> x1, Pallas kernels: none -> 0.85 us  [add_scores(): pl.pallas_call(add_kernel, out_shape=jax.ShapeDtypeStruct(own.shape, BF16...]
    pallas_call x1, Pallas kernels: 1.64 us -> 2.11 us  [kron_bases(): pl.pallas_call(kron_kernel, out_shape=tuple((jax.ShapeDtypeStruct(*x) for...]
    pallas_call x1, Pallas kernels: 1.27 us -> 0.99 us  [early_rows(): pl.pallas_call(functools.partial(early_kernel, masks), out_shape=jax.Shap...]
    pallas_call x1, Pallas kernels: 1.86 us -> 1.6 us  [outgoing_scores(): pl.pallas_call(functools.partial(late_kernel, masks), out_shape=(jax.Shap...]
    ppermute x7, waiting for transfers between devices: 0.9 us -> 0.68 us  [exchange(): return lax.ppermute(x, 'pb', [(i, i ^ mask) for i in range(n)])]
  transfers between devices with their start and end apart: 8 -> 8, of which waited for: 3 -> 3; matrix products, arithmetic and copies ran while one was open for 0% -> 0% of each run, Pallas kernels for 18% -> 19%
where the time goes in v4:
time: 20.9 us; the launch traced here: 20.7 us
  starting transfers between devices  11.5 us (55%)
  Pallas kernels  6.3 us (30%)
  waiting for transfers between devices  1.83 us (9%)
  local copies, waits for them, and re-layouts  0.98 us (5%)
    ppermute x7, starting transfers between devices, exchange(): return lax.ppermute(x, 'pb', [(i, i ^ mask) for i in range(n)])  11.4 us
    pallas_call x1, Pallas kernels, kron_bases(): pl.pallas_call(kron_kernel, out_shape=tuple((jax.ShapeDtypeStruct(*x) for...  2.11 us
    pallas_call x1, Pallas kernels, outgoing_scores(): pl.pallas_call(functools.partial(late_kernel, masks), out_shape=(jax.Shap...  1.6 us
    ppermute x1, waiting for transfers between devices, on_device(): received = lax.ppermute(sent, 'layer', [(0, 1), (1, 0)])  1.15 us
    pallas_call x1, Pallas kernels, early_rows(): pl.pallas_call(functools.partial(early_kernel, masks), out_shape=jax.Shap...  0.99 us
    unnamed x4, local copies, waits for them, and re-layouts  0.98 us
    pallas_call x1, Pallas kernels, add_scores(): pl.pallas_call(add_kernel, out_shape=jax.ShapeDtypeStruct(own.shape, BF16...  0.85 us
    pallas_call x1, Pallas kernels, own_scores(): pl.pallas_call(own_kernel, out_shape=jax.ShapeDtypeStruct((half, train),...  0.74 us
  transfers between devices with their start and end apart: 8, of which 3 were waited for; matrix products, arithmetic and copies ran while one was open for 0% of the time, Pallas kernels for 19%

profile of v4, /device:TPU:0, one launch (start us, length us, event | category | flops | bytes accessed | tf_op | source)
XLA Modules:
  0.0 20.7 jit_solution(7628595441479253640)
XLA Ops:
  0.0 0.0 copy-start.1
  0.0 4.0 %collective-permute-start = (bf16[32,1024]{1,0:T(8,128)(2,1)}, bf16[32,1024]{1,0:T(8,128)(2,1)S(1)}, u32[]{:S(2)}, u32[]{:S(2)}) collective-permute-start(bf16[32,1024]{1,0:T(8,128)(2,1)} %bitcast.4), channel_id=1, source_target_pairs={{0,8},{2,10},{4,12},{6,14},{8,0},{10,2},{12,4},{14,6},{1,9},{3,11}... | collective-permute-start | bytes 196616 | tf_op jit(solution)/shard_map/ppermute | solution.py:171
  4.0 1.3 %collective-permute-start.2 = (bf16[32,1024]{1,0:T(8,128)(2,1)}, bf16[32,1024]{1,0:T(8,128)(2,1)S(1)}, u32[]{:S(2)}, u32[]{:S(2)}) collective-permute-start(bf16[32,1024]{1,0:T(8,128)(2,1)} %bitcast.5), channel_id=1, source_target_pairs={{0,12},{2,14},{4,8},{6,10},{8,4},{10,6},{12,0},{14,2},{1,13},{3,15... | collective-permute-start | bytes 196616 | tf_op jit(solution)/shard_map/ppermute | solution.py:171
  5.4 1.2 %collective-permute-start.6 = (bf16[32,1024]{1,0:T(8,128)(2,1)}, bf16[32,1024]{1,0:T(8,128)(2,1)S(1)}, u32[]{:S(2)}, u32[]{:S(2)}) collective-permute-start(bf16[32,1024]{1,0:T(8,128)(2,1)} %bitcast.6), channel_id=1, source_target_pairs={{0,6},{2,4},{4,2},{6,0},{8,14},{10,12},{12,10},{14,8},{1,7},{3,5},... | collective-permute-start | bytes 196616 | tf_op jit(solution)/shard_map/ppermute | solution.py:171
  6.5 0.5 %collective-permute-start.5 = (bf16[32,1024]{1,0:T(8,128)(2,1)}, bf16[32,1024]{1,0:T(8,128)(2,1)S(1)}, u32[]{:S(2)}, u32[]{:S(2)}) collective-permute-start(bf16[32,1024]{1,0:T(8,128)(2,1)} %bitcast.7), channel_id=1, source_target_pairs={{0,2},{2,0},{4,6},{6,4},{8,10},{10,8},{12,14},{14,12},{1,3},{3,1},... | collective-permute-start | bytes 196616 | tf_op jit(solution)/shard_map/ppermute | solution.py:171
  7.1 1.8 %collective-permute-start.4 = (bf16[32,1024]{1,0:T(8,128)(2,1)}, bf16[32,1024]{1,0:T(8,128)(2,1)S(1)}, u32[]{:S(2)}, u32[]{:S(2)}) collective-permute-start(bf16[32,1024]{1,0:T(8,128)(2,1)} %bitcast.8), channel_id=1, source_target_pairs={{0,4},{2,6},{4,0},{6,2},{8,12},{10,14},{12,8},{14,10},{1,5},{3,7},... | collective-permute-start | bytes 196616 | tf_op jit(solution)/shard_map/ppermute | solution.py:171
  8.9 0.0 collective-permute-done.refs_1_
  8.9 1.7 %collective-permute-start.1 = (bf16[32,1024]{1,0:T(8,128)(2,1)S(1)}, bf16[32,1024]{1,0:T(8,128)(2,1)S(1)}, u32[]{:S(2)}, u32[]{:S(2)}) collective-permute-start(bf16[32,1024]{1,0:T(8,128)(2,1)S(1)} %collective-permute-done.refs_1_), channel_id=1, source_target_pairs={{0,2},{2,0},{4,6},{6,4},{8,10},{10,8},{12,14},{14,12},{1,3},{3,1},... | collective-permute-start | bytes 196616 | tf_op jit(solution)/shard_map/ppermute | solution.py:171
  10.6 0.5 %collective-permute-done.2.refs_2_ = bf16[32,1024]{1,0:T(8,128)(2,1)S(1)} collective-permute-done((bf16[32,1024]{1,0:T(8,128)(2,1)}, bf16[32,1024]{1,0:T(8,128)(2,1)S(1)}, u32[]{:S(2)}, u32[]{:S(2)}) %collective-permute-start.2) | collective-permute-done | bytes 65568 | tf_op jit(solution)/shard_map/ppermute | solution.py:171
  11.0 0.9 %collective-permute-start.3 = (bf16[32,1024]{1,0:T(8,128)(2,1)S(1)}, bf16[32,1024]{1,0:T(8,128)(2,1)S(1)}, u32[]{:S(2)}, u32[]{:S(2)}) collective-permute-start(bf16[32,1024]{1,0:T(8,128)(2,1)S(1)} %collective-permute-done.2.refs_2_), channel_id=1, source_target_pairs={{0,2},{2,0},{4,6},{6,4},{8,10},{10,8},{12,14},{14,12},{1,3},{3,1},... | collective-permute-start | bytes 196616 | tf_op jit(solution)/shard_map/ppermute | solution.py:171
  11.9 2.1 %kron_bases.1 = (bf16[1024,1024]{1,0:T(8,128)(2,1)S(1)}, bf16[1024,1024]{1,0:T(8,128)(2,1)S(1)}, f32[1,1024]{1,0:T(1,128)S(1)}) custom-call(f32[1,32,32]{2,1,0:T(8,128)} %in_hbm, f32[1,32,32]{2,1,0:T(8,128)} %out_hbm, f32[1,32,32]{2,1,0:T(8,128)} %eigen_hbm), custom_call_target="tpu_custom_call" | custom-call | flops 4294967296 | tf_op jit(solution)/shard_map/kron_bases/pallas_call | solution.py:49
  14.0 0.0 collective-permute-done.6.refs_5_
  14.0 0.0 collective-permute-done.5.refs_4_
  14.1 0.0 collective-permute-done.4.refs_3_
  14.1 0.0 copy-done.1
  14.1 0.0 copy-start
  14.1 1.0 %early_rows.1.refs_5_ = bf16[256,1024]{1,0:T(8,128)(2,1)S(1)} custom-call(bf16[32,1024]{1,0:T(8,128)(2,1)S(1)} %bitcast.9, bf16[32,1024]{1,0:T(8,128)(2,1)S(1)} %collective-permute-done.refs_1_, bf16[32,1024]{1,0:T(8,128)(2,1)S(1)} %collective-permute-done.2.refs_2_, bf16[32,1024]{1,0:T(8,128)(2,1)S(1)} %collective-permute-done.4.refs_3_, ...), custom_call_target="tpu_custom_call" | custom-call | tf_op jit(solution)/shard_map/early_rows/pallas_call | solution.py:105
  15.1 0.2 collective-permute-done.3.refs_1_
  15.3 0.0 collective-permute-done.1.refs_0_
  15.3 1.0 %copy-done = bf16[2048,1,1024]{2,0,1:T(8,128)(2,1)S(1)} copy-done((bf16[2048,1,1024]{2,0,1:T(8,128)(2,1)S(1)}, bf16[2048,1,1024]{2,0,1:T(8,128)(2,1)}, u32[]{:S(2)}) %copy-start) | copy-done | bytes 4194328
  16.3 1.6 %outgoing_scores.1 = (bf16[256,1024]{1,0:T(8,128)(2,1)S(1)}, bf16[1024,256]{1,0:T(8,128)(2,1)S(1)}) custom-call(bf16[32,1024]{1,0:T(8,128)(2,1)S(1)} %collective-permute-done.1.refs_0_, bf16[32,1024]{1,0:T(8,128)(2,1)S(1)} %collective-permute-done.3.refs_1_, ...), custom_call_target="tpu_custom_call", output_to_operand_aliasing={{0}: (5, {})} | custom-call | flops 536870912 | bytes 2097152 | tf_op jit(solution)/shard_map/outgoing_scores/pallas_call | solution.py:119
  17.9 0.1 collective-permute-start.7
  18.0 0.7 %own_scores.1.own_ref = f32[1024,256]{1,0:T(8,128)S(1)} custom-call(bf16[256,1024]{1,0:T(8,128)(2,1)S(1)} %get-tuple-element.19.w_ref, bf16[2048,1024]{1,0:T(8,128)(2,1)S(1)} %bitcast.3), custom_call_target="tpu_custom_call" | custom-call | flops 536870912 | bytes 2097152 | tf_op jit(solution)/shard_map/own_scores/pallas_call | solution.py:134
  18.7 1.2 %collective-permute-done.7.received_ref = bf16[1024,256]{1,0:T(8,128)(2,1)S(1)} collective-permute-done((bf16[1024,256]{1,0:T(8,128)(2,1)S(1)}, bf16[1024,256]{1,0:T(8,128)(2,1)S(1)}, u32[]{:S(2)}, u32[]{:S(2)}) %collective-permute-start.7) | collective-permute-done | bytes 524320 | tf_op jit(solution)/shard_map/ppermute | solution.py:189
  19.9 0.9 %add_scores.1 = bf16[1024,256]{1,0:T(8,128)(2,1)} custom-call(f32[1024,256]{1,0:T(8,128)S(1)} %own_scores.1.own_ref, bf16[1024,256]{1,0:T(8,128)(2,1)S(1)} %collective-permute-done.7.received_ref), custom_call_target="tpu_custom_call" | custom-call | tf_op jit(solution)/shard_map/add_scores/pallas_call | solution.py:158
Async XLA Ops:
  0.0 14.1 %copy-start.1 = (bf16[32,1,1024]{2,0,1:T(8,128)(2,1)S(1)}, bf16[32,1,1024]{2,0,1:T(8,128)(2,1)}, u32[]{:S(2)}) copy-start(bf16[32,1,1024]{2,0,1:T(8,128)(2,1)} %param.6) | copy-start | bytes 196612
  0.0 8.9 %collective-permute-start = (bf16[32,1024]{1,0:T(8,128)(2,1)}, bf16[32,1024]{1,0:T(8,128)(2,1)S(1)}, u32[]{:S(2)}, u32[]{:S(2)}) collective-permute-start(bf16[32,1024]{1,0:T(8,128)(2,1)} %bitcast.4), channel_id=1, source_target_pairs={{0,8},{2,10},{4,12},{6,14},{8,0},{10,2},{12,4},{14,6},{1,9},{3,11}... | collective-permute-start | bytes 196616 | tf_op jit(solution)/shard_map/ppermute | solution.py:171
  4.0 7.0 %collective-permute-start.2 = (bf16[32,1024]{1,0:T(8,128)(2,1)}, bf16[32,1024]{1,0:T(8,128)(2,1)S(1)}, u32[]{:S(2)}, u32[]{:S(2)}) collective-permute-start(bf16[32,1024]{1,0:T(8,128)(2,1)} %bitcast.5), channel_id=1, source_target_pairs={{0,12},{2,14},{4,8},{6,10},{8,4},{10,6},{12,0},{14,2},{1,13},{3,15... | collective-permute-start | bytes 196616 | tf_op jit(solution)/shard_map/ppermute | solution.py:171
  5.4 8.6 %collective-permute-start.6 = (bf16[32,1024]{1,0:T(8,128)(2,1)}, bf16[32,1024]{1,0:T(8,128)(2,1)S(1)}, u32[]{:S(2)}, u32[]{:S(2)}) collective-permute-start(bf16[32,1024]{1,0:T(8,128)(2,1)} %bitcast.6), channel_id=1, source_target_pairs={{0,6},{2,4},{4,2},{6,0},{8,14},{10,12},{12,10},{14,8},{1,7},{3,5},... | collective-permute-start | bytes 196616 | tf_op jit(solution)/shard_map/ppermute | solution.py:171
  6.5 7.5 %collective-permute-start.5 = (bf16[32,1024]{1,0:T(8,128)(2,1)}, bf16[32,1024]{1,0:T(8,128)(2,1)S(1)}, u32[]{:S(2)}, u32[]{:S(2)}) collective-permute-start(bf16[32,1024]{1,0:T(8,128)(2,1)} %bitcast.7), channel_id=1, source_target_pairs={{0,2},{2,0},{4,6},{6,4},{8,10},{10,8},{12,14},{14,12},{1,3},{3,1},... | collective-permute-start | bytes 196616 | tf_op jit(solution)/shard_map/ppermute | solution.py:171
  7.1 7.0 %collective-permute-start.4 = (bf16[32,1024]{1,0:T(8,128)(2,1)}, bf16[32,1024]{1,0:T(8,128)(2,1)S(1)}, u32[]{:S(2)}, u32[]{:S(2)}) collective-permute-start(bf16[32,1024]{1,0:T(8,128)(2,1)} %bitcast.8), channel_id=1, source_target_pairs={{0,4},{2,6},{4,0},{6,2},{8,12},{10,14},{12,8},{14,10},{1,5},{3,7},... | collective-permute-start | bytes 196616 | tf_op jit(solution)/shard_map/ppermute | solution.py:171
  8.9 6.4 %collective-permute-start.1 = (bf16[32,1024]{1,0:T(8,128)(2,1)S(1)}, bf16[32,1024]{1,0:T(8,128)(2,1)S(1)}, u32[]{:S(2)}, u32[]{:S(2)}) collective-permute-start(bf16[32,1024]{1,0:T(8,128)(2,1)S(1)} %collective-permute-done.refs_1_), channel_id=1, source_target_pairs={{0,2},{2,0},{4,6},{6,4},{8,10},{10,8},{12,14},{14,12},{1,3},{3,1},... | collective-permute-start | bytes 196616 | tf_op jit(solution)/shard_map/ppermute | solution.py:171
  11.0 4.3 %collective-permute-start.3 = (bf16[32,1024]{1,0:T(8,128)(2,1)S(1)}, bf16[32,1024]{1,0:T(8,128)(2,1)S(1)}, u32[]{:S(2)}, u32[]{:S(2)}) collective-permute-start(bf16[32,1024]{1,0:T(8,128)(2,1)S(1)} %collective-permute-done.2.refs_2_), channel_id=1, source_target_pairs={{0,2},{2,0},{4,6},{6,4},{8,10},{10,8},{12,14},{14,12},{1,3},{3,1},... | collective-permute-start | bytes 196616 | tf_op jit(solution)/shard_map/ppermute | solution.py:171
  14.1 2.2 %copy-start = (bf16[2048,1,1024]{2,0,1:T(8,128)(2,1)S(1)}, bf16[2048,1,1024]{2,0,1:T(8,128)(2,1)}, u32[]{:S(2)}) copy-start(bf16[2048,1,1024]{2,0,1:T(8,128)(2,1)} %param.5) | copy-start | bytes 12582916
  17.9 2.0 %collective-permute-start.7 = (bf16[1024,256]{1,0:T(8,128)(2,1)S(1)}, bf16[1024,256]{1,0:T(8,128)(2,1)S(1)}, u32[]{:S(2)}, u32[]{:S(2)}) collective-permute-start(bf16[1024,256]{1,0:T(8,128)(2,1)S(1)} %get-tuple-element.20), channel_id=1, source_target_pairs={{0,1},{1,0},{2,3},{3,2},{4,5},{5,4},{6,7},{7,6},{8,9},{9,8},{10,11... | collective-permute-start | bytes 1572872 | tf_op jit(solution)/shard_map/ppermute | solution.py:189

commit v5 on v4

--- a/solution.py
+++ b/solution.py
@@ -10,7 +10,6 @@
 F32, BF16 = jnp.float32, jnp.bfloat16
 VMEM = pl.BlockSpec(memory_space=pltpu.VMEM)
 HBM = pl.BlockSpec(memory_space=pl.ANY)
-HIGH = lax.Precision.HIGHEST
 NT = (((1,), (1,)), ((), ()))
 PARAMS = pltpu.CompilerParams(vmem_limit_bytes=24 * 1024 * 1024)
 
@@ -19,43 +18,59 @@
     return pl.CostEstimate(flops=flops, bytes_accessed=bytes_accessed, transcendentals=0)
 
 
-def kron_kernel(in_hbm, out_hbm, eigen_hbm, kron_ref, turned_ref, inverse_ref, basis_in, basis_out, eigen, sems):
-    pairs = ((in_hbm, basis_in), (out_hbm, basis_out), (eigen_hbm, eigen))
-    copies = [pltpu.make_async_copy(*pair, sems.at[i]) for i, pair in enumerate(pairs)]
-    for copy in copies:
-        copy.start()
+def selector_kernel(kin, chosen_ref):
+    kout, grad = chosen_ref.shape[0] - kin, chosen_ref.shape[1]
+    lane = lax.broadcasted_iota(jnp.int32, (kout, grad), 1)
+    chosen_ref[:kout, :] = (lax.broadcasted_iota(jnp.int32, (kout, grad), 0) == lane // kin).astype(F32).astype(BF16)
+    lane = lax.broadcasted_iota(jnp.int32, (kin, grad), 1)
+    chosen_ref[kout:, :] = (lax.broadcasted_iota(jnp.int32, (kin, grad), 0) == lane % kin).astype(F32).astype(BF16)
+
+
+def selectors(kout, kin):
+    return pl.pallas_call(
+        functools.partial(selector_kernel, kin),
+        out_shape=jax.ShapeDtypeStruct((kout + kin, kout * kin), BF16),
+        out_specs=VMEM,
+        compiler_params=PARAMS,
+        cost_estimate=estimate(2 * (kout * kin)**3, 0),
+        name="selectors",
+    )()
+
+
+def select(matrices, chosen):
+    rest, parts = jnp.concatenate(matrices, axis=0), []
+    for _ in range(3):
+        parts.append(rest.astype(BF16))
+        rest = rest - parts[-1].astype(F32)
+    product = jnp.dot(jnp.concatenate(parts, axis=0), chosen, preferred_element_type=F32)
+    rows = rest.shape[0]
+    return product[:rows] + product[rows:2 * rows] + product[2 * rows:]
+
+
+def kron_kernel(basis_in, basis_out, eigen, chosen_ref, _, kron_ref, turned_ref, inverse_ref):
     kout, kin = basis_out.shape[1], basis_in.shape[1]
-    grad = kout * kin
-    lane_out = lax.broadcasted_iota(jnp.int32, (kout, grad), 1) // kin
-    repeat = (lax.broadcasted_iota(jnp.int32, (kout, grad), 0) == lane_out).astype(F32)
-    lane_in = lax.broadcasted_iota(jnp.int32, (kin, grad), 1) % kin
-    tile = (lax.broadcasted_iota(jnp.int32, (kin, grad), 0) == lane_in).astype(F32)
-    for copy in copies:
-        copy.wait()
-    inner = jnp.concatenate([basis_in[0], basis_in[0].T, eigen[0]], axis=0)
-    outer = jnp.concatenate([basis_out[0], basis_out[0].T], axis=0)
-    tiled = jnp.dot(inner, tile, precision=HIGH, preferred_element_type=F32)
-    spread = jnp.dot(outer, repeat, precision=HIGH, preferred_element_type=F32)
+    repeat, tile = chosen_ref[:kout, :], chosen_ref[kout:, :]
+    tiled = select([basis_in[0], basis_in[0].T, eigen[0]], tile)
+    spread = select([basis_out[0], basis_out[0].T], repeat)
     tiled_in, turned_in, tiled_eigen = tiled[:kin], tiled[kin:2 * kin], tiled[2 * kin:]
-    inverse_ref[...] = 1.0 / (jnp.sum(tiled_eigen * repeat, axis=0, keepdims=True) + 0.1)
+    inverse_ref[...] = 1.0 / (jnp.sum(tiled_eigen * repeat.astype(F32), axis=0, keepdims=True) + 0.1)
     for b in range(kout):
         kron_ref[pl.ds(b * kin, kin), :] = (spread[b:b + 1, :] * tiled_in).astype(BF16)
-        turned_ref[pl.ds(b * kin, kin), :] = (spread[kout + b:kout + b + 1, :] * turned_in).astype(BF16)
-
-
-def kron_bases(basis_in, basis_out, eigenvalues):
-    grad = basis_in.shape[1] * basis_out.shape[1]
-    args = [pltpu.with_memory_space_constraint(x, pltpu.HBM) for x in (basis_in, basis_out, eigenvalues)]
+    for a in range(kout):
+        turned_ref[pl.ds(a * kin, kin), :] = (spread[kout + a:kout + a + 1, :] * turned_in).astype(BF16)
+
+
+def kron_bases(basis_in, basis_out, eigenvalues, chosen, queries):
+    grad = chosen.shape[1]
     return pl.pallas_call(
         kron_kernel,
         out_shape=tuple(jax.ShapeDtypeStruct(*x) for x in (((grad, grad), BF16), ((grad, grad), BF16), ((1, grad), F32))),
-        in_specs=[HBM] * 3,
+        in_specs=[VMEM] * 5,
         out_specs=(VMEM,) * 3,
-        scratch_shapes=[pltpu.VMEM(x.shape, F32) for x in args] + [pltpu.SemaphoreType.DMA((3,))],
         compiler_params=PARAMS,
         cost_estimate=estimate(4 * grad**3, 0),
         name="kron_bases",
-    )(*args)
+    )(basis_in, basis_out, eigenvalues, chosen, queries)
 
 
 def fill_rows(masks, blocks, kron_ref, turned_ref, inverse_ref, w_ref, rows_ref):
@@ -174,16 +189,17 @@
 def on_device(n, query_grads, train_grads, basis_in, basis_out, eigenvalues):
     train = train_grads.reshape(train_grads.shape[0], -1)
     queries = query_grads.reshape(query_grads.shape[0], -1)
+    chosen = selectors(basis_out.shape[1], basis_in.shape[1])
     if n == 8:
-        far = [exchange(train, n, mask) for mask in (4, 6)]
-        near = [exchange(train, n, mask) for mask in (2, 1, 3)]
+        far = [exchange(train, n, mask) for mask in (6, 4)]
+        behind, chosen = lax.optimization_barrier((train, chosen))
+        near = [exchange(behind, n, mask) for mask in (2, 1, 3)]
         early, late = [train] + far + near, [exchange(block, n, 1) for block in far]
-        early_masks, late_masks = (0, 4, 6, 2, 1, 3), (5, 7)
-        basis_in, basis_out, eigenvalues, _ = lax.optimization_barrier((basis_in, basis_out, eigenvalues, far[0]))
+        early_masks, late_masks = (0, 6, 4, 2, 1, 3), (7, 5)
     else:
         early, late = [lax.all_gather(train, "pb", axis=0, tiled=True)], []
         early_masks, late_masks = (0,), ()
-    bases = kron_bases(basis_in, basis_out, eigenvalues)
+    bases = kron_bases(basis_in, basis_out, eigenvalues, chosen, queries)
     w = early_rows(early_masks, early, bases, n * train.shape[0])
     w, sent = outgoing_scores(late_masks, late, bases, w, queries)
     received = lax.ppermute(sent, "layer", [(0, 1), (1, 0)])

time: 20.9 us -> 19.9 us (0.952)
  Pallas kernels: 6.3 us -> 5.33 us
  local copies, waits for them, and re-layouts: 0.98 us -> 0.02 us
  waiting for transfers between devices: 1.83 us -> 2.64 us
    pallas_call x1, Pallas kernels: 2.11 us -> 1.12 us  [kron_bases(): pl.pallas_call(kron_kernel, out_shape=tuple((jax.ShapeDtypeStruct(*x) for...]
    unnamed x4 -> x10, local copies, waits for them, and re-layouts: 0.98 us -> 0.02 us
    ppermute x7, waiting for transfers between devices: 0.68 us -> 1.48 us  [exchange(): return lax.ppermute(x, 'pb', [(i, i ^ mask) for i in range(n)])]
  transfers between devices with their start and end apart: 8 -> 8, of which waited for: 3 -> 3; matrix products, arithmetic and copies ran while one was open for 0% -> 0% of each run, Pallas kernels for 19% -> 15%
where the time goes in v5:
time: 19.9 us; the launch traced here: 19.7 us
  starting transfers between devices  11.6 us (58%)
  Pallas kernels  5.33 us (27%)
  waiting for transfers between devices  2.64 us (13%)
    ppermute x7, starting transfers between devices, exchange(): return lax.ppermute(x, 'pb', [(i, i ^ mask) for i in range(n)])  11.6 us
    pallas_call x1, Pallas kernels, outgoing_scores(): pl.pallas_call(functools.partial(late_kernel, masks), out_shape=(jax.Shap...  1.61 us
    ppermute x7, waiting for transfers between devices, exchange(): return lax.ppermute(x, 'pb', [(i, i ^ mask) for i in range(n)])  1.48 us
    ppermute x1, waiting for transfers between devices, on_device(): received = lax.ppermute(sent, 'layer', [(0, 1), (1, 0)])  1.15 us
    pallas_call x1, Pallas kernels, kron_bases(): pl.pallas_call(kron_kernel, out_shape=tuple((jax.ShapeDtypeStruct(*x) for...  1.12 us
    pallas_call x1, Pallas kernels, early_rows(): pl.pallas_call(functools.partial(early_kernel, masks), out_shape=jax.Shap...  1 us
    pallas_call x1, Pallas kernels, add_scores(): pl.pallas_call(add_kernel, out_shape=jax.ShapeDtypeStruct(own.shape, BF16...  0.85 us
    pallas_call x1, Pallas kernels, own_scores(): pl.pallas_call(own_kernel, out_shape=jax.ShapeDtypeStruct((half, train),...  0.74 us
  transfers between devices with their start and end apart: 8, of which 3 were waited for; matrix products, arithmetic and copies ran while one was open for 0% of the time, Pallas kernels for 15%

profile of v5, /device:TPU:0, one launch (start us, length us, event | category | flops | bytes accessed | tf_op | source)
XLA Modules:
  0.0 19.7 jit_solution(12466010464108413438)
XLA Ops:
  0.0 0.0 copy-start.1
  0.0 0.0 copy-start
  0.0 0.0 copy-start.2
  0.0 0.0 copy-start.3
  0.0 0.0 copy-start.4
  0.0 4.1 %collective-permute-start.2 = (bf16[32,1024]{1,0:T(8,128)(2,1)}, bf16[32,1024]{1,0:T(8,128)(2,1)S(1)}, u32[]{:S(2)}, u32[]{:S(2)}) collective-permute-start(bf16[32,1024]{1,0:T(8,128)(2,1)} %bitcast.5), channel_id=1, source_target_pairs={{0,8},{2,10},{4,12},{6,14},{8,0},{10,2},{12,4},{14,6},{1,9},{3,11}... | collective-permute-start | bytes 196616 | tf_op jit(solution)/shard_map/ppermute | solution.py:186
  4.1 1.3 %collective-permute-start = (bf16[32,1024]{1,0:T(8,128)(2,1)}, bf16[32,1024]{1,0:T(8,128)(2,1)S(1)}, u32[]{:S(2)}, u32[]{:S(2)}) collective-permute-start(bf16[32,1024]{1,0:T(8,128)(2,1)} %bitcast.6), channel_id=1, source_target_pairs={{0,12},{2,14},{4,8},{6,10},{8,4},{10,6},{12,0},{14,2},{1,13},{3,15... | collective-permute-start | bytes 196616 | tf_op jit(solution)/shard_map/ppermute | solution.py:186
  5.5 0.0 copy-done.1
  5.5 1.2 %collective-permute-start.6 = (bf16[32,1024]{1,0:T(8,128)(2,1)S(1)}, bf16[32,1024]{1,0:T(8,128)(2,1)S(1)}, u32[]{:S(2)}, u32[]{:S(2)}) collective-permute-start(bf16[32,1024]{1,0:T(8,128)(2,1)S(1)} %bitcast.7), channel_id=1, source_target_pairs={{0,6},{2,4},{4,2},{6,0},{8,14},{10,12},{12,10},{14,8},{1,7},{3,5},... | collective-permute-start | bytes 196616 | tf_op jit(solution)/shard_map/ppermute | solution.py:186
  6.7 0.5 %collective-permute-start.5 = (bf16[32,1024]{1,0:T(8,128)(2,1)S(1)}, bf16[32,1024]{1,0:T(8,128)(2,1)S(1)}, u32[]{:S(2)}, u32[]{:S(2)}) collective-permute-start(bf16[32,1024]{1,0:T(8,128)(2,1)S(1)} %bitcast.8), channel_id=1, source_target_pairs={{0,2},{2,0},{4,6},{6,4},{8,10},{10,8},{12,14},{14,12},{1,3},{3,1},... | collective-permute-start | bytes 196616 | tf_op jit(solution)/shard_map/ppermute | solution.py:186
  7.3 1.8 %collective-permute-start.4 = (bf16[32,1024]{1,0:T(8,128)(2,1)S(1)}, bf16[32,1024]{1,0:T(8,128)(2,1)S(1)}, u32[]{:S(2)}, u32[]{:S(2)}) collective-permute-start(bf16[32,1024]{1,0:T(8,128)(2,1)S(1)} %bitcast.9), channel_id=1, source_target_pairs={{0,4},{2,6},{4,0},{6,2},{8,12},{10,14},{12,8},{14,10},{1,5},{3,7},... | collective-permute-start | bytes 196616 | tf_op jit(solution)/shard_map/ppermute | solution.py:186
  9.1 0.0 collective-permute-done.2.refs_2_
  9.1 1.6 %collective-permute-start.3 = (bf16[32,1024]{1,0:T(8,128)(2,1)S(1)}, bf16[32,1024]{1,0:T(8,128)(2,1)S(1)}, u32[]{:S(2)}, u32[]{:S(2)}) collective-permute-start(bf16[32,1024]{1,0:T(8,128)(2,1)S(1)} %collective-permute-done.2.refs_2_), channel_id=1, source_target_pairs={{0,2},{2,0},{4,6},{6,4},{8,10},{10,8},{12,14},{14,12},{1,3},{3,1},... | collective-permute-start | bytes 196616 | tf_op jit(solution)/shard_map/ppermute | solution.py:186
  10.6 0.4 %collective-permute-done.refs_1_ = bf16[32,1024]{1,0:T(8,128)(2,1)S(1)} collective-permute-done((bf16[32,1024]{1,0:T(8,128)(2,1)}, bf16[32,1024]{1,0:T(8,128)(2,1)S(1)}, u32[]{:S(2)}, u32[]{:S(2)}) %collective-permute-start) | collective-permute-done | bytes 65568 | tf_op jit(solution)/shard_map/ppermute | solution.py:186
  11.0 1.0 %collective-permute-start.1 = (bf16[32,1024]{1,0:T(8,128)(2,1)S(1)}, bf16[32,1024]{1,0:T(8,128)(2,1)S(1)}, u32[]{:S(2)}, u32[]{:S(2)}) collective-permute-start(bf16[32,1024]{1,0:T(8,128)(2,1)S(1)} %collective-permute-done.refs_1_), channel_id=1, source_target_pairs={{0,2},{2,0},{4,6},{6,4},{8,10},{10,8},{12,14},{14,12},{1,3},{3,1},... | collective-permute-start | bytes 196616 | tf_op jit(solution)/shard_map/ppermute | solution.py:186
  12.0 0.0 copy-done
  12.0 0.0 copy-done.2
  12.0 0.0 copy-done.3
  12.0 0.0 copy-done.4
  12.0 1.1 %kron_bases.1 = (bf16[1024,1024]{1,0:T(8,128)(2,1)S(1)}, bf16[1024,1024]{1,0:T(8,128)(2,1)S(1)}, f32[1,1024]{1,0:T(1,128)S(1)}) custom-call(f32[1,32,32]{2,1,0:T(8,128)S(1)} %copy-done.2, f32[1,32,32]{2,1,0:T(8,128)S(1)} %copy-done.3, f32[1,32,32]{2,1,0:T(8,128)S(1)} %copy-done.4, bf16[64,1024]{1,0:T(8,128)(2,1)S(1)} %selectors.1.chosen_ref, ...), custom_call_target="tpu_custom_call" | custom-call | flops 4294967296 | tf_op jit(solution)/shard_map/kron_bases/pallas_call | solution.py:65
  13.1 0.0 collective-permute-done.6.refs_5_
  13.2 0.0 collective-permute-done.5.refs_4_
  13.2 0.0 collective-permute-done.4.refs_3_
  13.2 1.0 %early_rows.1.refs_5_ = bf16[256,1024]{1,0:T(8,128)(2,1)S(1)} custom-call(bf16[32,1024]{1,0:T(8,128)(2,1)S(1)} %bitcast.10, bf16[32,1024]{1,0:T(8,128)(2,1)S(1)} %collective-permute-done.refs_1_, bf16[32,1024]{1,0:T(8,128)(2,1)S(1)} %collective-permute-done.2.refs_2_, bf16[32,1024]{1,0:T(8,128)(2,1)S(1)} %collective-permute-done.4.refs_3_, ...), custom_call_target="tpu_custom_call" | custom-call | tf_op jit(solution)/shard_map/early_rows/pallas_call | solution.py:120
  14.2 0.0 collective-permute-done.3.refs_1_
  14.2 1.1 %collective-permute-done.1.refs_0_ = bf16[32,1024]{1,0:T(8,128)(2,1)S(1)} collective-permute-done((bf16[32,1024]{1,0:T(8,128)(2,1)S(1)}, bf16[32,1024]{1,0:T(8,128)(2,1)S(1)}, u32[]{:S(2)}, u32[]{:S(2)}) %collective-permute-start.1) | collective-permute-done | bytes 65568 | tf_op jit(solution)/shard_map/ppermute | solution.py:186
  15.3 1.6 %outgoing_scores.1 = (bf16[256,1024]{1,0:T(8,128)(2,1)S(1)}, bf16[1024,256]{1,0:T(8,128)(2,1)S(1)}) custom-call(bf16[32,1024]{1,0:T(8,128)(2,1)S(1)} %collective-permute-done.1.refs_0_, bf16[32,1024]{1,0:T(8,128)(2,1)S(1)} %collective-permute-done.3.refs_1_, ...), custom_call_target="tpu_custom_call", output_to_operand_aliasing={{0}: (5, {})} | custom-call | flops 536870912 | bytes 2097152 | tf_op jit(solution)/shard_map/outgoing_scores/pallas_call | solution.py:134
  16.9 0.1 collective-permute-start.7
  17.0 0.7 %own_scores.1.own_ref = f32[1024,256]{1,0:T(8,128)S(1)} custom-call(bf16[256,1024]{1,0:T(8,128)(2,1)S(1)} %get-tuple-element.17.w_ref, bf16[2048,1024]{1,0:T(8,128)(2,1)S(1)} %bitcast.4), custom_call_target="tpu_custom_call" | custom-call | flops 536870912 | bytes 2097152 | tf_op jit(solution)/shard_map/own_scores/pallas_call | solution.py:149
  17.7 1.2 %collective-permute-done.7.received_ref = bf16[1024,256]{1,0:T(8,128)(2,1)S(1)} collective-permute-done((bf16[1024,256]{1,0:T(8,128)(2,1)S(1)}, bf16[1024,256]{1,0:T(8,128)(2,1)S(1)}, u32[]{:S(2)}, u32[]{:S(2)}) %collective-permute-start.7) | collective-permute-done | bytes 524320 | tf_op jit(solution)/shard_map/ppermute | solution.py:205
  18.9 0.9 %add_scores.1 = bf16[1024,256]{1,0:T(8,128)(2,1)} custom-call(f32[1024,256]{1,0:T(8,128)S(1)} %own_scores.1.own_ref, bf16[1024,256]{1,0:T(8,128)(2,1)S(1)} %collective-permute-done.7.received_ref), custom_call_target="tpu_custom_call" | custom-call | tf_op jit(solution)/shard_map/add_scores/pallas_call | solution.py:173
  (1 shorter events, 0.0 us)
Async XLA Ops:
  0.0 5.5 %copy-start.1 = (bf16[32,1,1024]{2,0,1:T(8,128)(2,1)S(1)}, bf16[32,1,1024]{2,0,1:T(8,128)(2,1)}, u32[]{:S(2)}) copy-start(bf16[32,1,1024]{2,0,1:T(8,128)(2,1)} %param.6) | copy-start | bytes 196612
  0.0 12.0 %copy-start = (bf16[2048,1,1024]{2,0,1:T(8,128)(2,1)S(1)}, bf16[2048,1,1024]{2,0,1:T(8,128)(2,1)}, u32[]{:S(2)}) copy-start(bf16[2048,1,1024]{2,0,1:T(8,128)(2,1)} %param.5) | copy-start | bytes 12582916
  0.0 12.0 %copy-start.2 = (f32[1,32,32]{2,1,0:T(8,128)S(1)}, f32[1,32,32]{2,1,0:T(8,128)}, u32[]{:S(2)}) copy-start(f32[1,32,32]{2,1,0:T(8,128)} %basis_in.1) | copy-start | bytes 12292
  0.0 12.0 %copy-start.3 = (f32[1,32,32]{2,1,0:T(8,128)S(1)}, f32[1,32,32]{2,1,0:T(8,128)}, u32[]{:S(2)}) copy-start(f32[1,32,32]{2,1,0:T(8,128)} %basis_out.1) | copy-start | bytes 12292
  0.0 12.0 %copy-start.4 = (f32[1,32,32]{2,1,0:T(8,128)S(1)}, f32[1,32,32]{2,1,0:T(8,128)}, u32[]{:S(2)}) copy-start(f32[1,32,32]{2,1,0:T(8,128)} %eigen.1) | copy-start | bytes 12292
  0.0 9.1 %collective-permute-start.2 = (bf16[32,1024]{1,0:T(8,128)(2,1)}, bf16[32,1024]{1,0:T(8,128)(2,1)S(1)}, u32[]{:S(2)}, u32[]{:S(2)}) collective-permute-start(bf16[32,1024]{1,0:T(8,128)(2,1)} %bitcast.5), channel_id=1, source_target_pairs={{0,8},{2,10},{4,12},{6,14},{8,0},{10,2},{12,4},{14,6},{1,9},{3,11}... | collective-permute-start | bytes 196616 | tf_op jit(solution)/shard_map/ppermute | solution.py:186
  4.1 6.9 %collective-permute-start = (bf16[32,1024]{1,0:T(8,128)(2,1)}, bf16[32,1024]{1,0:T(8,128)(2,1)S(1)}, u32[]{:S(2)}, u32[]{:S(2)}) collective-permute-start(bf16[32,1024]{1,0:T(8,128)(2,1)} %bitcast.6), channel_id=1, source_target_pairs={{0,12},{2,14},{4,8},{6,10},{8,4},{10,6},{12,0},{14,2},{1,13},{3,15... | collective-permute-start | bytes 196616 | tf_op jit(solution)/shard_map/ppermute | solution.py:186
  5.5 7.6 %collective-permute-start.6 = (bf16[32,1024]{1,0:T(8,128)(2,1)S(1)}, bf16[32,1024]{1,0:T(8,128)(2,1)S(1)}, u32[]{:S(2)}, u32[]{:S(2)}) collective-permute-start(bf16[32,1024]{1,0:T(8,128)(2,1)S(1)} %bitcast.7), channel_id=1, source_target_pairs={{0,6},{2,4},{4,2},{6,0},{8,14},{10,12},{12,10},{14,8},{1,7},{3,5},... | collective-permute-start | bytes 196616 | tf_op jit(solution)/shard_map/ppermute | solution.py:186
  6.7 6.4 %collective-permute-start.5 = (bf16[32,1024]{1,0:T(8,128)(2,1)S(1)}, bf16[32,1024]{1,0:T(8,128)(2,1)S(1)}, u32[]{:S(2)}, u32[]{:S(2)}) collective-permute-start(bf16[32,1024]{1,0:T(8,128)(2,1)S(1)} %bitcast.8), channel_id=1, source_target_pairs={{0,2},{2,0},{4,6},{6,4},{8,10},{10,8},{12,14},{14,12},{1,3},{3,1},... | collective-permute-start | bytes 196616 | tf_op jit(solution)/shard_map/ppermute | solution.py:186
  7.3 5.9 %collective-permute-start.4 = (bf16[32,1024]{1,0:T(8,128)(2,1)S(1)}, bf16[32,1024]{1,0:T(8,128)(2,1)S(1)}, u32[]{:S(2)}, u32[]{:S(2)}) collective-permute-start(bf16[32,1024]{1,0:T(8,128)(2,1)S(1)} %bitcast.9), channel_id=1, source_target_pairs={{0,4},{2,6},{4,0},{6,2},{8,12},{10,14},{12,8},{14,10},{1,5},{3,7},... | collective-permute-start | bytes 196616 | tf_op jit(solution)/shard_map/ppermute | solution.py:186
  9.1 5.1 %collective-permute-start.3 = (bf16[32,1024]{1,0:T(8,128)(2,1)S(1)}, bf16[32,1024]{1,0:T(8,128)(2,1)S(1)}, u32[]{:S(2)}, u32[]{:S(2)}) collective-permute-start(bf16[32,1024]{1,0:T(8,128)(2,1)S(1)} %collective-permute-done.2.refs_2_), channel_id=1, source_target_pairs={{0,2},{2,0},{4,6},{6,4},{8,10},{10,8},{12,14},{14,12},{1,3},{3,1},... | collective-permute-start | bytes 196616 | tf_op jit(solution)/shard_map/ppermute | solution.py:186
  11.0 4.3 %collective-permute-start.1 = (bf16[32,1024]{1,0:T(8,128)(2,1)S(1)}, bf16[32,1024]{1,0:T(8,128)(2,1)S(1)}, u32[]{:S(2)}, u32[]{:S(2)}) collective-permute-start(bf16[32,1024]{1,0:T(8,128)(2,1)S(1)} %collective-permute-done.refs_1_), channel_id=1, source_target_pairs={{0,2},{2,0},{4,6},{6,4},{8,10},{10,8},{12,14},{14,12},{1,3},{3,1},... | collective-permute-start | bytes 196616 | tf_op jit(solution)/shard_map/ppermute | solution.py:186
  16.9 2.0 %collective-permute-start.7 = (bf16[1024,256]{1,0:T(8,128)(2,1)S(1)}, bf16[1024,256]{1,0:T(8,128)(2,1)S(1)}, u32[]{:S(2)}, u32[]{:S(2)}) collective-permute-start(bf16[1024,256]{1,0:T(8,128)(2,1)S(1)} %get-tuple-element.18), channel_id=1, source_target_pairs={{0,1},{1,0},{2,3},{3,2},{4,5},{5,4},{6,7},{7,6},{8,9},{9,8},{10,11... | collective-permute-start | bytes 1572872 | tf_op jit(solution)/shard_map/ppermute | solution.py:205

commit v6 on v3

v6 whole, which is shorter than its diff:
```python
import functools

import jax
import jax.numpy as jnp
from jax import lax
from jax.experimental import pallas as pl
from jax.experimental.pallas import tpu as pltpu
from jax.sharding import PartitionSpec as P

F32, BF16 = jnp.float32, jnp.bfloat16
VMEM = pl.BlockSpec(memory_space=pltpu.VMEM)
HBM = pl.BlockSpec(memory_space=pl.ANY)
NT = (((1,), (1,)), ((), ()))
PARAMS = pltpu.CompilerParams(vmem_limit_bytes=24 * 1024 * 1024)


def estimate(flops, bytes_accessed):
    return pl.CostEstimate(flops=flops, bytes_accessed=bytes_accessed, transcendentals=0)


def selector_kernel(kin, chosen_ref):
    kout, grad = chosen_ref.shape[0] - kin, chosen_ref.shape[1]
    lane = lax.broadcasted_iota(jnp.int32, (kout, grad), 1)
    chosen_ref[:kout, :] = (lax.broadcasted_iota(jnp.int32, (kout, grad), 0) == lane // kin).astype(F32).astype(BF16)
    lane = lax.broadcasted_iota(jnp.int32, (kin, grad), 1)
    chosen_ref[kout:, :] = (lax.broadcasted_iota(jnp.int32, (kin, grad), 0) == lane % kin).astype(F32).astype(BF16)


def selectors(kout, kin):
    return pl.pallas_call(
        functools.partial(selector_kernel, kin),
        out_shape=jax.ShapeDtypeStruct((kout + kin, kout * kin), BF16),
        out_specs=VMEM,
        compiler_params=PARAMS,
        cost_estimate=estimate(2 * (kout * kin)**3, 0),
        name="selectors",
    )()


def select(matrices, chosen):
    rest, parts = jnp.concatenate(matrices, axis=0), []
    for _ in range(3):
        parts.append(rest.astype(BF16))
        rest = rest - parts[-1].astype(F32)
    product = jnp.dot(jnp.concatenate(parts, axis=0), chosen, preferred_element_type=F32)
    rows = rest.shape[0]
    return product[:rows] + product[rows:2 * rows] + product[2 * rows:]


def kron_kernel(basis_in, basis_out, eigen, chosen_ref, _, kron_ref, turned_ref, inverse_ref):
    kout, kin = basis_out.shape[1], basis_in.shape[1]
    repeat, tile = chosen_ref[:kout, :], chosen_ref[kout:, :]
    tiled = select([basis_in[0], basis_in[0].T, eigen[0]], tile)
    spread = select([basis_out[0], basis_out[0].T], repeat)
    tiled_in, turned_in, tiled_eigen = tiled[:kin], tiled[kin:2 * kin], tiled[2 * kin:]
    inverse_ref[...] = 1.0 / (jnp.sum(tiled_eigen * repeat.astype(F32), axis=0, keepdims=True) + 0.1)
    for b in range(kout):
        kron_ref[pl.ds(b * kin, kin), :] = (spread[b:b + 1, :] * tiled_in).astype(BF16)
    for a in range(kout):
        turned_ref[pl.ds(a * kin, kin), :] = (spread[kout + a:kout + a + 1, :] * turned_in).astype(BF16)


def kron_bases(basis_in, basis_out, eigenvalues, chosen, queries):
    grad = chosen.shape[1]
    return pl.pallas_call(
        kron_kernel,
        out_shape=tuple(jax.ShapeDtypeStruct(*x) for x in (((grad, grad), BF16), ((grad, grad), BF16), ((1, grad), F32))),
        in_specs=[VMEM] * 5,
        out_specs=(VMEM,) * 3,
        compiler_params=PARAMS,
        cost_estimate=estimate(grad**3 // 2, 0),
        name="kron_bases",
    )(basis_in, basis_out, eigenvalues, chosen, queries)


def precondition_kernel(*refs):
    *blocks, kron_ref, turned_ref, inverse_ref, w_ref = refs
    size, total = blocks[0].shape[0], w_ref.shape[0]
    for i, block in enumerate(blocks):
        w_ref[pl.ds(i * size, size), :] = block[...]
    step = min(total, 256)
    for i in range(total // step):
        rows = pl.ds(i * step, step)
        rotated = jnp.dot(w_ref[rows, :], kron_ref[...], preferred_element_type=F32)
        scaled = (rotated * inverse_ref[...]).astype(BF16)
        w_ref[rows, :] = jnp.dot(scaled, turned_ref[...], preferred_element_type=F32).astype(BF16)


def precondition(blocks, bases, name):
    rows, grad = sum(block.shape[0] for block in blocks), bases[0].shape[0]
    return pl.pallas_call(
        precondition_kernel,
        out_shape=jax.ShapeDtypeStruct((rows, grad), BF16),
        in_specs=[VMEM] * (len(blocks) + 3),
        out_specs=VMEM,
        compiler_params=PARAMS,
        cost_estimate=estimate((0 if name == "early_rows" else int(19.5 * grad**3)), 0),
        name=name,
    )(*blocks, *bases)


def arrange(masks, groups, w_ref):
    me, size = lax.axis_index("pb"), w_ref.shape[0] // len(masks)
    i = 0
    for group in groups:
        for row in range(0, group.shape[0], size):
            at = pl.multiple_of((me ^ masks[i]) * size, size) if len(masks) > 1 else 0
            w_ref[pl.ds(at, size), :] = group[pl.ds(row, size), :]
            i += 1


def first_kernel(masks, *refs):
    *groups, q_ref, out_ref, w_ref = refs
    arrange(masks, groups, w_ref)
    half, step = out_ref.shape[0], min(w_ref.shape[0], 256)
    own = pl.ds(pl.multiple_of(lax.axis_index("layer") * half, half), half)
    for i in range(w_ref.shape[0] // step):
        cols = slice(i * step, (i + 1) * step)
        out_ref[:, cols] = lax.dot_general(q_ref[own, :], w_ref[cols, :], NT, preferred_element_type=F32)


def last_kernel(masks, *refs):
    *groups, q_ref, first_ref, out_hbm, w_ref, out_ref, sems = refs
    arrange(masks, groups, w_ref)
    half, step, parts = first_ref.shape[0], min(w_ref.shape[0], 256), sems.shape[0]
    rows = half // parts
    copies = []
    for r in range(parts):
        here = pl.ds(r * rows, rows)
        for i in range(w_ref.shape[0] // step):
            cols = slice(i * step, (i + 1) * step)
            second = lax.dot_general(q_ref[here, :], w_ref[cols, :], NT, preferred_element_type=F32)
            out_ref[here, cols] = (first_ref[here, cols] + second).astype(BF16)
        copies.append(pltpu.make_async_copy(out_ref.at[here], out_hbm.at[here], sems.at[r]))
        copies[-1].start()
    for copy in copies:
        copy.wait()


def first_scores(masks, groups, queries):
    train, grad = sum(group.shape[0] for group in groups), queries.shape[1]
    half = queries.shape[0] // 2
    return pl.pallas_call(
        functools.partial(first_kernel, masks),
        out_shape=jax.ShapeDtypeStruct((half, train), F32),
        in_specs=[VMEM] * (len(groups) + 1),
        out_specs=VMEM,
        scratch_shapes=[pltpu.VMEM((train, grad), BF16)],
        compiler_params=PARAMS,
        cost_estimate=estimate(2 * train * grad * half, 2 * half * grad),
        name="first_scores",
    )(*groups, queries)


def last_scores(masks, groups, queries, first):
    train, grad = sum(group.shape[0] for group in groups), queries.shape[1]
    half = queries.shape[0]
    return pl.pallas_call(
        functools.partial(last_kernel, masks),
        out_shape=jax.ShapeDtypeStruct((half, train), BF16),
        in_specs=[VMEM] * (len(groups) + 2),
        out_specs=HBM,
        scratch_shapes=[pltpu.VMEM((train, grad), BF16), pltpu.VMEM((half, train), BF16), pltpu.SemaphoreType.DMA((2,))],
        compiler_params=PARAMS,
        cost_estimate=estimate(2 * train * grad * half, 2 * half * grad),
        name="last_scores",
    )(*groups, queries, first)


def theirs_kernel(q_ref, theirs_ref):
    half = theirs_ref.shape[0]
    start, rows = (1 - lax.axis_index("layer")) * half, min(half, 256)
    for i in range(half // rows):
        there = pl.ds(pl.multiple_of(start + i * rows, rows), rows)
        theirs_ref[pl.ds(i * rows, rows), :] = q_ref[there, :]


def other_half(queries):
    rows, grad = queries.shape
    return pl.pallas_call(
        theirs_kernel,
        out_shape=jax.ShapeDtypeStruct((rows // 2, grad), BF16),
        in_specs=[VMEM],
        out_specs=VMEM,
        compiler_params=PARAMS,
        cost_estimate=estimate(4 * grad**3, 0),
        name="other_half",
    )(queries)


def exchange(x, n, mask):
    return lax.ppermute(x, "pb", [(i, i ^ mask) for i in range(n)])


def other_layer(x):
    return lax.ppermute(x, "layer", [(0, 1), (1, 0)])


def on_device(n, query_grads, train_grads, basis_in, basis_out, eigenvalues):
    train = train_grads.reshape(train_grads.shape[0], -1)
    queries = query_grads.reshape(query_grads.shape[0], -1)
    chosen = selectors(basis_out.shape[1], basis_in.shape[1])
    if n == 8:
        far = [exchange(train, n, mask) for mask in (4, 6)]
        behind, chosen = lax.optimization_barrier((train, chosen))
        near = [exchange(behind, n, mask) for mask in (2, 1, 3)]
        groups, masks = [[train] + far + near, [exchange(block, n, 1) for block in far]], (0, 4, 6, 2, 1, 3, 5, 7)
        loose, *_ = lax.optimization_barrier([queries] + [])
        sent = other_half(loose)
        sent, *_ = lax.optimization_barrier([sent] + near[1:2])
    else:
        groups, masks = [[lax.all_gather(train, "pb", axis=0, tiled=True)]], (0,)
        sent = other_half(queries)
    other_queries = other_layer(sent)
    bases = kron_bases(basis_in, basis_out, eigenvalues, chosen, queries)
    own = [precondition(groups[0], bases, "early_rows")]
    if len(groups) > 1:
        own[0], *groups[1] = lax.optimization_barrier([own[0]] + groups[1])
        own.append(precondition(groups[1], bases, "late_rows"))
    other = [other_layer(w) for w in own]
    return last_scores(masks, other, other_queries, first_scores(masks, own, queries))


def solution(mesh):
    placed = (
        P(("grp", "pb"), "layer", None),
        P(("grp", "pb"), "layer", None),
        P("layer", None, None),
        P("layer", None, None),
        P("layer", None, None),
    )
    return jax.shard_map(
        functools.partial(on_device, mesh.shape["pb"]),
        mesh=mesh,
        in_specs=placed,
        out_specs=P(("grp", "pb", "layer"), None),
        check_vma=False,
    )
```

time: 21 us -> 19 us (0.905)
  waiting for transfers between devices: 2.66 us -> 0.7 us
  Pallas kernels: 6.25 us -> 5.53 us
  starting transfers between devices: 11.8 us -> 12.5 us
    ppermute x7, waiting for transfers between devices: 2.46 us -> 0.5 us  [exchange(): return lax.ppermute(x, 'pb', [(i, i ^ mask) for i in range(n)])]
    ppermute x7, starting transfers between devices: 10.8 us -> 11.9 us  [exchange(): return lax.ppermute(x, 'pb', [(i, i ^ mask) for i in range(n)])]
    pallas_call x2, Pallas kernels: 2.39 us -> 1.85 us  [precondition(): pl.pallas_call(precondition_kernel, out_shape=jax.ShapeDtypeStruct((rows,...]
    ppermute x3, starting transfers between devices: 1.02 us -> 0.65 us  [other_layer(): return lax.ppermute(x, 'layer', [(0, 1), (1, 0)])]
    pallas_call x1, Pallas kernels: 1.49 us -> 1.13 us  [kron_bases(): pl.pallas_call(kron_kernel, out_shape=tuple((jax.ShapeDtypeStruct(*x) for...]
  transfers between devices with their start and end apart: 10 -> 10, of which waited for: 4 -> 2; matrix products, arithmetic and copies ran while one was open for 0% -> 0% of each run, Pallas kernels for 22% -> 21%
where the time goes in v6:
time: 19 us; the launch traced here: 18.9 us
  starting transfers between devices  12.5 us (66%)
  Pallas kernels  5.53 us (29%)
  waiting for transfers between devices  0.7 us (4%)
    ppermute x7, starting transfers between devices, exchange(): return lax.ppermute(x, 'pb', [(i, i ^ mask) for i in range(n)])  11.9 us
    pallas_call x2, Pallas kernels, precondition(): pl.pallas_call(precondition_kernel, out_shape=jax.ShapeDtypeStruct((rows,...  1.85 us
    pallas_call x1, Pallas kernels, last_scores(): pl.pallas_call(functools.partial(last_kernel, masks), out_shape=jax.Shape...  1.61 us
    pallas_call x1, Pallas kernels, kron_bases(): pl.pallas_call(kron_kernel, out_shape=tuple((jax.ShapeDtypeStruct(*x) for...  1.13 us
    pallas_call x1, Pallas kernels, first_scores(): pl.pallas_call(functools.partial(first_kernel, masks), out_shape=jax.Shap...  0.78 us
    ppermute x3, starting transfers between devices, other_layer(): return lax.ppermute(x, 'layer', [(0, 1), (1, 0)])  0.65 us
    ppermute x7, waiting for transfers between devices, exchange(): return lax.ppermute(x, 'pb', [(i, i ^ mask) for i in range(n)])  0.5 us
  transfers between devices with their start and end apart: 10, of which 2 were waited for; matrix products, arithmetic and copies ran while one was open for 0% of the time, Pallas kernels for 21%

profile of v6, /device:TPU:0, one launch (start us, length us, event | category | flops | bytes accessed | tf_op | source)
XLA Modules:
  0.0 18.9 jit_solution(8353714103929077962)
XLA Ops:
  0.0 0.0 copy-start.1
  0.0 0.0 copy-start
  0.0 4.0 %collective-permute-start = (bf16[32,1024]{1,0:T(8,128)(2,1)}, bf16[32,1024]{1,0:T(8,128)(2,1)S(1)}, u32[]{:S(2)}, u32[]{:S(2)}) collective-permute-start(bf16[32,1024]{1,0:T(8,128)(2,1)} %bitcast.5), channel_id=1, source_target_pairs={{0,8},{2,10},{4,12},{6,14},{8,0},{10,2},{12,4},{14,6},{1,9},{3,11}... | collective-permute-start | bytes 196616 | tf_op jit(solution)/shard_map/ppermute | solution.py:192
  4.0 1.3 %collective-permute-start.1 = (bf16[32,1024]{1,0:T(8,128)(2,1)}, bf16[32,1024]{1,0:T(8,128)(2,1)S(1)}, u32[]{:S(2)}, u32[]{:S(2)}) collective-permute-start(bf16[32,1024]{1,0:T(8,128)(2,1)} %bitcast.6), channel_id=1, source_target_pairs={{0,12},{2,14},{4,8},{6,10},{8,4},{10,6},{12,0},{14,2},{1,13},{3,15... | collective-permute-start | bytes 196616 | tf_op jit(solution)/shard_map/ppermute | solution.py:192
  5.4 0.0 copy-done.1
  5.4 0.3 %collective-permute-start.2 = (bf16[32,1024]{1,0:T(8,128)(2,1)S(1)}, bf16[32,1024]{1,0:T(8,128)(2,1)S(1)}, u32[]{:S(2)}, u32[]{:S(2)}) collective-permute-start(bf16[32,1024]{1,0:T(8,128)(2,1)S(1)} %bitcast.7), channel_id=1, source_target_pairs={{0,4},{2,6},{4,0},{6,2},{8,12},{10,14},{12,8},{14,10},{1,5},{3,7},... | collective-permute-start | bytes 196616 | tf_op jit(solution)/shard_map/ppermute | solution.py:192
  5.7 1.5 %collective-permute-start.3 = (bf16[32,1024]{1,0:T(8,128)(2,1)S(1)}, bf16[32,1024]{1,0:T(8,128)(2,1)S(1)}, u32[]{:S(2)}, u32[]{:S(2)}) collective-permute-start(bf16[32,1024]{1,0:T(8,128)(2,1)S(1)} %bitcast.8), channel_id=1, source_target_pairs={{0,2},{2,0},{4,6},{6,4},{8,10},{10,8},{12,14},{14,12},{1,3},{3,1},... | collective-permute-start | bytes 196616 | tf_op jit(solution)/shard_map/ppermute | solution.py:192
  7.2 1.8 %collective-permute-start.4 = (bf16[32,1024]{1,0:T(8,128)(2,1)S(1)}, bf16[32,1024]{1,0:T(8,128)(2,1)S(1)}, u32[]{:S(2)}, u32[]{:S(2)}) collective-permute-start(bf16[32,1024]{1,0:T(8,128)(2,1)S(1)} %bitcast.9), channel_id=1, source_target_pairs={{0,6},{2,4},{4,2},{6,0},{8,14},{10,12},{12,10},{14,8},{1,7},{3,5},... | collective-permute-start | bytes 196616 | tf_op jit(solution)/shard_map/ppermute | solution.py:192
  9.0 0.0 copy-start.2
  9.0 0.0 copy-start.3
  9.0 0.0 copy-start.4
  9.0 0.0 collective-permute-done.refs_1_
  9.0 1.6 %collective-permute-start.5 = (bf16[32,1024]{1,0:T(8,128)(2,1)S(1)}, bf16[32,1024]{1,0:T(8,128)(2,1)S(1)}, u32[]{:S(2)}, u32[]{:S(2)}) collective-permute-start(bf16[32,1024]{1,0:T(8,128)(2,1)S(1)} %collective-permute-done.refs_1_), channel_id=1, source_target_pairs={{0,2},{2,0},{4,6},{6,4},{8,10},{10,8},{12,14},{14,12},{1,3},{3,1},... | collective-permute-start | bytes 196616 | tf_op jit(solution)/shard_map/ppermute | solution.py:192
  10.6 0.0 collective-permute-done.1.refs_2_
  10.6 1.4 %collective-permute-start.6 = (bf16[32,1024]{1,0:T(8,128)(2,1)S(1)}, bf16[32,1024]{1,0:T(8,128)(2,1)S(1)}, u32[]{:S(2)}, u32[]{:S(2)}) collective-permute-start(bf16[32,1024]{1,0:T(8,128)(2,1)S(1)} %collective-permute-done.1.refs_2_), channel_id=1, source_target_pairs={{0,2},{2,0},{4,6},{6,4},{8,10},{10,8},{12,14},{14,12},{1,3},{3,1},... | collective-permute-start | bytes 196616 | tf_op jit(solution)/shard_map/ppermute | solution.py:192
  11.9 0.0 copy-done
  11.9 0.1 other_half.1
  12.1 0.0 collective-permute-done.3.refs_4_
  12.1 0.1 collective-permute-start.9
  12.2 0.0 copy-done.2
  12.2 0.0 copy-done.3
  12.2 0.0 copy-done.4
  12.2 1.1 %kron_bases.1 = (bf16[1024,1024]{1,0:T(8,128)(2,1)S(1)}, bf16[1024,1024]{1,0:T(8,128)(2,1)S(1)}, f32[1,1024]{1,0:T(1,128)S(1)}) custom-call(f32[1,32,32]{2,1,0:T(8,128)S(1)} %copy-done.2, f32[1,32,32]{2,1,0:T(8,128)S(1)} %copy-done.3, f32[1,32,32]{2,1,0:T(8,128)S(1)} %copy-done.4, bf16[64,1024]{1,0:T(8,128)(2,1)S(1)} %selectors.1.chosen_ref, ...), custom_call_target="tpu_custom_call" | custom-call | flops 536870912 | tf_op jit(solution)/shard_map/kron_bases/pallas_call | solution.py:65
  13.3 0.0 collective-permute-done.2.refs_3_
  13.3 0.0 collective-permute-done.4.refs_5_
  13.3 1.0 %early_rows.1.refs_0_ = bf16[192,1024]{1,0:T(8,128)(2,1)S(1)} custom-call(bf16[32,1024]{1,0:T(8,128)(2,1)S(1)} %bitcast.10, bf16[32,1024]{1,0:T(8,128)(2,1)S(1)} %collective-permute-done.refs_1_, bf16[32,1024]{1,0:T(8,128)(2,1)S(1)} %collective-permute-done.1.refs_2_, bf16[32,1024]{1,0:T(8,128)(2,1)S(1)} %collective-permute-done.2.refs_3_, ...), custom_call_target="tpu_custom_call" | custom-call | tf_op jit(solution)/shard_map/early_rows/pallas_call | solution.py:91
  14.3 0.0 collective-permute-done.5.refs_0_
  14.4 0.5 %collective-permute-done.6.refs_1_ = bf16[32,1024]{1,0:T(8,128)(2,1)S(1)} collective-permute-done((bf16[32,1024]{1,0:T(8,128)(2,1)S(1)}, bf16[32,1024]{1,0:T(8,128)(2,1)S(1)}, u32[]{:S(2)}, u32[]{:S(2)}) %collective-permute-start.6) | collective-permute-done | bytes 65568 | tf_op jit(solution)/shard_map/ppermute | solution.py:192
  14.8 0.1 collective-permute-start.7
  14.9 0.9 %late_rows.1.refs_1_ = bf16[64,1024]{1,0:T(8,128)(2,1)S(1)} custom-call(bf16[32,1024]{1,0:T(8,128)(2,1)S(1)} %collective-permute-done.5.refs_0_, bf16[32,1024]{1,0:T(8,128)(2,1)S(1)} %collective-permute-done.6.refs_1_, bf16[1024,1024]{1,0:T(8,128)(2,1)S(1)} %get-tuple-element.16.refs_6_.refs_2_, bf16[1024,1024]{1,0:T(8,128)(2,1)S(1)} %get-tuple-element.17.refs_7_.refs_3_, ...), custom_call_target="tpu_custom_call" | custom-call | flops 20937965568 | tf_op jit(solution)/shard_map/late_rows/pallas_call | solution.py:91
  15.8 0.5 %collective-permute-start.8 = (bf16[64,1024]{1,0:T(8,128)(2,1)S(1)}, bf16[64,1024]{1,0:T(8,128)(2,1)S(1)}, u32[]{:S(2)}, u32[]{:S(2)}) collective-permute-start(bf16[64,1024]{1,0:T(8,128)(2,1)S(1)} %late_rows.1.refs_1_), channel_id=1, source_target_pairs={{0,1},{1,0},{2,3},{3,2},{4,5},{5,4},{6,7},{7,6},{8,9},{9,8},{10,11... | collective-permute-start | bytes 393224 | tf_op jit(solution)/shard_map/ppermute | solution.py:196
  16.3 0.8 %first_scores.1.refs_3_ = f32[1024,256]{1,0:T(8,128)S(1)} custom-call(bf16[192,1024]{1,0:T(8,128)(2,1)S(1)} %early_rows.1.refs_0_, bf16[64,1024]{1,0:T(8,128)(2,1)S(1)} %late_rows.1.refs_1_, bf16[2048,1024]{1,0:T(8,128)(2,1)S(1)} %bitcast.4), custom_call_target="tpu_custom_call" | custom-call | flops 536870912 | bytes 2097152 | tf_op jit(solution)/shard_map/first_scores/pallas_call | solution.py:143
  17.1 0.2 %collective-permute-done.8.refs_1_ = bf16[64,1024]{1,0:T(8,128)(2,1)S(1)} collective-permute-done((bf16[64,1024]{1,0:T(8,128)(2,1)S(1)}, bf16[64,1024]{1,0:T(8,128)(2,1)S(1)}, u32[]{:S(2)}, u32[]{:S(2)}) %collective-permute-start.8) | collective-permute-done | bytes 131104 | tf_op jit(solution)/shard_map/ppermute | solution.py:196
  17.3 0.0 collective-permute-done.7.refs_0_
  17.3 0.0 collective-permute-done.9.refs_2_
  17.3 1.6 %last_scores.1 = bf16[1024,256]{1,0:T(8,128)(2,1)} custom-call(bf16[192,1024]{1,0:T(8,128)(2,1)S(1)} %collective-permute-done.7.refs_0_, bf16[64,1024]{1,0:T(8,128)(2,1)S(1)} %collective-permute-done.8.refs_1_, bf16[1024,1024]{1,0:T(8,128)(2,1)S(1)} %collective-permute-done.9.refs_2_, f32[1024,256]{1,0:T(8,128)S(1)} %first_scores.1.refs_3_), custom_call_target="tpu_custom_call" | custom-call | flops 536870912 | bytes 2097152 | tf_op jit(solution)/shard_map/last_scores/pallas_call | solution.py:158
  (1 shorter events, 0.0 us)
Async XLA Ops:
  0.0 5.4 %copy-start.1 = (bf16[32,1,1024]{2,0,1:T(8,128)(2,1)S(1)}, bf16[32,1,1024]{2,0,1:T(8,128)(2,1)}, u32[]{:S(2)}) copy-start(bf16[32,1,1024]{2,0,1:T(8,128)(2,1)} %param.6) | copy-start | bytes 196612
  0.0 11.9 %copy-start = (bf16[2048,1,1024]{2,0,1:T(8,128)(2,1)S(1)}, bf16[2048,1,1024]{2,0,1:T(8,128)(2,1)}, u32[]{:S(2)}) copy-start(bf16[2048,1,1024]{2,0,1:T(8,128)(2,1)} %param.5) | copy-start | bytes 12582916
  0.0 9.0 %collective-permute-start = (bf16[32,1024]{1,0:T(8,128)(2,1)}, bf16[32,1024]{1,0:T(8,128)(2,1)S(1)}, u32[]{:S(2)}, u32[]{:S(2)}) collective-permute-start(bf16[32,1024]{1,0:T(8,128)(2,1)} %bitcast.5), channel_id=1, source_target_pairs={{0,8},{2,10},{4,12},{6,14},{8,0},{10,2},{12,4},{14,6},{1,9},{3,11}... | collective-permute-start | bytes 196616 | tf_op jit(solution)/shard_map/ppermute | solution.py:192
  4.0 6.5 %collective-permute-start.1 = (bf16[32,1024]{1,0:T(8,128)(2,1)}, bf16[32,1024]{1,0:T(8,128)(2,1)S(1)}, u32[]{:S(2)}, u32[]{:S(2)}) collective-permute-start(bf16[32,1024]{1,0:T(8,128)(2,1)} %bitcast.6), channel_id=1, source_target_pairs={{0,12},{2,14},{4,8},{6,10},{8,4},{10,6},{12,0},{14,2},{1,13},{3,15... | collective-permute-start | bytes 196616 | tf_op jit(solution)/shard_map/ppermute | solution.py:192
  5.4 7.9 %collective-permute-start.2 = (bf16[32,1024]{1,0:T(8,128)(2,1)S(1)}, bf16[32,1024]{1,0:T(8,128)(2,1)S(1)}, u32[]{:S(2)}, u32[]{:S(2)}) collective-permute-start(bf16[32,1024]{1,0:T(8,128)(2,1)S(1)} %bitcast.7), channel_id=1, source_target_pairs={{0,4},{2,6},{4,0},{6,2},{8,12},{10,14},{12,8},{14,10},{1,5},{3,7},... | collective-permute-start | bytes 196616 | tf_op jit(solution)/shard_map/ppermute | solution.py:192
  5.7 6.3 %collective-permute-start.3 = (bf16[32,1024]{1,0:T(8,128)(2,1)S(1)}, bf16[32,1024]{1,0:T(8,128)(2,1)S(1)}, u32[]{:S(2)}, u32[]{:S(2)}) collective-permute-start(bf16[32,1024]{1,0:T(8,128)(2,1)S(1)} %bitcast.8), channel_id=1, source_target_pairs={{0,2},{2,0},{4,6},{6,4},{8,10},{10,8},{12,14},{14,12},{1,3},{3,1},... | collective-permute-start | bytes 196616 | tf_op jit(solution)/shard_map/ppermute | solution.py:192
  7.2 6.1 %collective-permute-start.4 = (bf16[32,1024]{1,0:T(8,128)(2,1)S(1)}, bf16[32,1024]{1,0:T(8,128)(2,1)S(1)}, u32[]{:S(2)}, u32[]{:S(2)}) collective-permute-start(bf16[32,1024]{1,0:T(8,128)(2,1)S(1)} %bitcast.9), channel_id=1, source_target_pairs={{0,6},{2,4},{4,2},{6,0},{8,14},{10,12},{12,10},{14,8},{1,7},{3,5},... | collective-permute-start | bytes 196616 | tf_op jit(solution)/shard_map/ppermute | solution.py:192
  9.0 3.2 %copy-start.2 = (f32[1,32,32]{2,1,0:T(8,128)S(1)}, f32[1,32,32]{2,1,0:T(8,128)}, u32[]{:S(2)}) copy-start(f32[1,32,32]{2,1,0:T(8,128)} %basis_in.1) | copy-start | bytes 12292
  9.0 3.2 %copy-start.3 = (f32[1,32,32]{2,1,0:T(8,128)S(1)}, f32[1,32,32]{2,1,0:T(8,128)}, u32[]{:S(2)}) copy-start(f32[1,32,32]{2,1,0:T(8,128)} %basis_out.1) | copy-start | bytes 12292
  9.0 3.2 %copy-start.4 = (f32[1,32,32]{2,1,0:T(8,128)S(1)}, f32[1,32,32]{2,1,0:T(8,128)}, u32[]{:S(2)}) copy-start(f32[1,32,32]{2,1,0:T(8,128)} %eigen.1) | copy-start | bytes 12292
  9.0 5.4 %collective-permute-start.5 = (bf16[32,1024]{1,0:T(8,128)(2,1)S(1)}, bf16[32,1024]{1,0:T(8,128)(2,1)S(1)}, u32[]{:S(2)}, u32[]{:S(2)}) collective-permute-start(bf16[32,1024]{1,0:T(8,128)(2,1)S(1)} %collective-permute-done.refs_1_), channel_id=1, source_target_pairs={{0,2},{2,0},{4,6},{6,4},{8,10},{10,8},{12,14},{14,12},{1,3},{3,1},... | collective-permute-start | bytes 196616 | tf_op jit(solution)/shard_map/ppermute | solution.py:192
  10.6 4.3 %collective-permute-start.6 = (bf16[32,1024]{1,0:T(8,128)(2,1)S(1)}, bf16[32,1024]{1,0:T(8,128)(2,1)S(1)}, u32[]{:S(2)}, u32[]{:S(2)}) collective-permute-start(bf16[32,1024]{1,0:T(8,128)(2,1)S(1)} %collective-permute-done.1.refs_2_), channel_id=1, source_target_pairs={{0,2},{2,0},{4,6},{6,4},{8,10},{10,8},{12,14},{14,12},{1,3},{3,1},... | collective-permute-start | bytes 196616 | tf_op jit(solution)/shard_map/ppermute | solution.py:192
  12.1 5.2 %collective-permute-start.9 = (bf16[1024,1024]{1,0:T(8,128)(2,1)S(1)}, bf16[1024,1024]{1,0:T(8,128)(2,1)S(1)}, u32[]{:S(2)}, u32[]{:S(2)}) collective-permute-start(bf16[1024,1024]{1,0:T(8,128)(2,1)S(1)} %other_half.1), channel_id=1, source_target_pairs={{0,1},{1,0},{2,3},{3,2},{4,5},{5,4},{6,7},{7,6},{8,9},{9,8},{10,11... | collective-permute-start | bytes 6291464 | tf_op jit(solution)/shard_map/ppermute | solution.py:196
  14.8 2.4 %collective-permute-start.7 = (bf16[192,1024]{1,0:T(8,128)(2,1)S(1)}, bf16[192,1024]{1,0:T(8,128)(2,1)S(1)}, u32[]{:S(2)}, u32[]{:S(2)}) collective-permute-start(bf16[192,1024]{1,0:T(8,128)(2,1)S(1)} %early_rows.1.refs_0_), channel_id=1, source_target_pairs={{0,1},{1,0},{2,3},{3,2},{4,5},{5,4},{6,7},{7,6},{8,9},{9,8},{10,11... | collective-permute-start | bytes 1179656 | tf_op jit(solution)/shard_map/ppermute | solution.py:196
  15.8 1.5 %collective-permute-start.8 = (bf16[64,1024]{1,0:T(8,128)(2,1)S(1)}, bf16[64,1024]{1,0:T(8,128)(2,1)S(1)}, u32[]{:S(2)}, u32[]{:S(2)}) collective-permute-start(bf16[64,1024]{1,0:T(8,128)(2,1)S(1)} %late_rows.1.refs_1_), channel_id=1, source_target_pairs={{0,1},{1,0},{2,3},{3,2},{4,5},{5,4},{6,7},{7,6},{8,9},{9,8},{10,11... | collective-permute-start | bytes 393224 | tf_op jit(solution)/shard_map/ppermute | solution.py:196

commit v7 on v6

--- a/solution.py
+++ b/solution.py
@@ -122,17 +122,18 @@
 def last_kernel(masks, *refs):
     *groups, q_ref, first_ref, out_hbm, w_ref, out_ref, sems = refs
     arrange(masks, groups, w_ref)
-    half, step, parts = first_ref.shape[0], min(w_ref.shape[0], 256), sems.shape[0]
-    rows = half // parts
+    half, train, parts = first_ref.shape[0], w_ref.shape[0], sems.shape[0]
+    step, rows = min(train, 256), half // parts
     copies = []
-    for r in range(parts):
-        here = pl.ds(r * rows, rows)
-        for i in range(w_ref.shape[0] // step):
-            cols = slice(i * step, (i + 1) * step)
-            second = lax.dot_general(q_ref[here, :], w_ref[cols, :], NT, preferred_element_type=F32)
-            out_ref[here, cols] = (first_ref[here, cols] + second).astype(BF16)
-        copies.append(pltpu.make_async_copy(out_ref.at[here], out_hbm.at[here], sems.at[r]))
-        copies[-1].start()
+    for i in range(train // step):
+        cols = slice(i * step, (i + 1) * step)
+        second = lax.dot_general(q_ref[...], w_ref[cols, :], NT, preferred_element_type=F32)
+        for r in range(parts):
+            here = slice(r * rows, (r + 1) * rows)
+            out_ref[here, cols] = (first_ref[here, cols] + second[here]).astype(BF16)
+            if (i + 1) * step == train:
+                copies.append(pltpu.make_async_copy(out_ref.at[here], out_hbm.at[here], sems.at[r]))
+                copies[-1].start()
     for copy in copies:
         copy.wait()
 
@@ -160,7 +161,7 @@
         out_shape=jax.ShapeDtypeStruct((half, train), BF16),
         in_specs=[VMEM] * (len(groups) + 2),
         out_specs=HBM,
-        scratch_shapes=[pltpu.VMEM((train, grad), BF16), pltpu.VMEM((half, train), BF16), pltpu.SemaphoreType.DMA((2,))],
+        scratch_shapes=[pltpu.VMEM((train, grad), BF16), pltpu.VMEM((half, train), BF16), pltpu.SemaphoreType.DMA((8,))],
         compiler_params=PARAMS,
         cost_estimate=estimate(2 * train * grad * half, 2 * half * grad),
         name="last_scores",
@@ -205,9 +206,8 @@
         behind, chosen = lax.optimization_barrier((train, chosen))
         near = [exchange(behind, n, mask) for mask in (2, 1, 3)]
         groups, masks = [[train] + far + near, [exchange(block, n, 1) for block in far]], (0, 4, 6, 2, 1, 3, 5, 7)
-        loose, *_ = lax.optimization_barrier([queries] + [])
-        sent = other_half(loose)
-        sent, *_ = lax.optimization_barrier([sent] + near[1:2])
+        loose, = lax.optimization_barrier((queries,))
+        sent, _ = lax.optimization_barrier((other_half(loose), near[1]))
     else:
         groups, masks = [[lax.all_gather(train, "pb", axis=0, tiled=True)]], (0,)
         sent = other_half(queries)

time: 19 us -> 18.9 us (level)
  no operation moved by 1% of the time
where the time goes in v7:
time: 18.9 us; the launch traced here: 18.8 us
  starting transfers between devices  12.5 us (66%)
  Pallas kernels  5.41 us (29%)
  waiting for transfers between devices  0.7 us (4%)
    ppermute x7, starting transfers between devices, exchange(): return lax.ppermute(x, 'pb', [(i, i ^ mask) for i in range(n)])  11.9 us
    pallas_call x2, Pallas kernels, precondition(): pl.pallas_call(precondition_kernel, out_shape=jax.ShapeDtypeStruct((rows,...  1.85 us
    pallas_call x1, Pallas kernels, last_scores(): pl.pallas_call(functools.partial(last_kernel, masks), out_shape=jax.Shape...  1.49 us
    pallas_call x1, Pallas kernels, kron_bases(): pl.pallas_call(kron_kernel, out_shape=tuple((jax.ShapeDtypeStruct(*x) for...  1.13 us
    pallas_call x1, Pallas kernels, first_scores(): pl.pallas_call(functools.partial(first_kernel, masks), out_shape=jax.Shap...  0.78 us
    ppermute x3, starting transfers between devices, other_layer(): return lax.ppermute(x, 'layer', [(0, 1), (1, 0)])  0.65 us
    ppermute x7, waiting for transfers between devices, exchange(): return lax.ppermute(x, 'pb', [(i, i ^ mask) for i in range(n)])  0.5 us
  transfers between devices with their start and end apart: 10, of which 2 were waited for; matrix products, arithmetic and copies ran while one was open for 0% of the time, Pallas kernels for 21%

profile of v7, /device:TPU:0, one launch (start us, length us, event | category | flops | bytes accessed | tf_op | source)
XLA Modules:
  0.0 18.8 jit_solution(13031528235755208835)
XLA Ops:
  0.0 0.0 copy-start.1
  0.0 0.0 copy-start
  0.0 4.0 %collective-permute-start = (bf16[32,1024]{1,0:T(8,128)(2,1)}, bf16[32,1024]{1,0:T(8,128)(2,1)S(1)}, u32[]{:S(2)}, u32[]{:S(2)}) collective-permute-start(bf16[32,1024]{1,0:T(8,128)(2,1)} %bitcast.5), channel_id=1, source_target_pairs={{0,8},{2,10},{4,12},{6,14},{8,0},{10,2},{12,4},{14,6},{1,9},{3,11}... | collective-permute-start | bytes 196616 | tf_op jit(solution)/shard_map/ppermute | solution.py:193
  4.0 1.3 %collective-permute-start.1 = (bf16[32,1024]{1,0:T(8,128)(2,1)}, bf16[32,1024]{1,0:T(8,128)(2,1)S(1)}, u32[]{:S(2)}, u32[]{:S(2)}) collective-permute-start(bf16[32,1024]{1,0:T(8,128)(2,1)} %bitcast.6), channel_id=1, source_target_pairs={{0,12},{2,14},{4,8},{6,10},{8,4},{10,6},{12,0},{14,2},{1,13},{3,15... | collective-permute-start | bytes 196616 | tf_op jit(solution)/shard_map/ppermute | solution.py:193
  5.4 0.0 copy-done.1
  5.4 0.3 %collective-permute-start.2 = (bf16[32,1024]{1,0:T(8,128)(2,1)S(1)}, bf16[32,1024]{1,0:T(8,128)(2,1)S(1)}, u32[]{:S(2)}, u32[]{:S(2)}) collective-permute-start(bf16[32,1024]{1,0:T(8,128)(2,1)S(1)} %bitcast.7), channel_id=1, source_target_pairs={{0,4},{2,6},{4,0},{6,2},{8,12},{10,14},{12,8},{14,10},{1,5},{3,7},... | collective-permute-start | bytes 196616 | tf_op jit(solution)/shard_map/ppermute | solution.py:193
  5.7 1.5 %collective-permute-start.3 = (bf16[32,1024]{1,0:T(8,128)(2,1)S(1)}, bf16[32,1024]{1,0:T(8,128)(2,1)S(1)}, u32[]{:S(2)}, u32[]{:S(2)}) collective-permute-start(bf16[32,1024]{1,0:T(8,128)(2,1)S(1)} %bitcast.8), channel_id=1, source_target_pairs={{0,2},{2,0},{4,6},{6,4},{8,10},{10,8},{12,14},{14,12},{1,3},{3,1},... | collective-permute-start | bytes 196616 | tf_op jit(solution)/shard_map/ppermute | solution.py:193
  7.2 1.8 %collective-permute-start.4 = (bf16[32,1024]{1,0:T(8,128)(2,1)S(1)}, bf16[32,1024]{1,0:T(8,128)(2,1)S(1)}, u32[]{:S(2)}, u32[]{:S(2)}) collective-permute-start(bf16[32,1024]{1,0:T(8,128)(2,1)S(1)} %bitcast.9), channel_id=1, source_target_pairs={{0,6},{2,4},{4,2},{6,0},{8,14},{10,12},{12,10},{14,8},{1,7},{3,5},... | collective-permute-start | bytes 196616 | tf_op jit(solution)/shard_map/ppermute | solution.py:193
  9.0 0.0 copy-start.2
  9.0 0.0 copy-start.3
  9.0 0.0 copy-start.4
  9.0 0.0 collective-permute-done.refs_1_
  9.0 1.6 %collective-permute-start.5 = (bf16[32,1024]{1,0:T(8,128)(2,1)S(1)}, bf16[32,1024]{1,0:T(8,128)(2,1)S(1)}, u32[]{:S(2)}, u32[]{:S(2)}) collective-permute-start(bf16[32,1024]{1,0:T(8,128)(2,1)S(1)} %collective-permute-done.refs_1_), channel_id=1, source_target_pairs={{0,2},{2,0},{4,6},{6,4},{8,10},{10,8},{12,14},{14,12},{1,3},{3,1},... | collective-permute-start | bytes 196616 | tf_op jit(solution)/shard_map/ppermute | solution.py:193
  10.6 0.0 collective-permute-done.1.refs_2_
  10.6 1.4 %collective-permute-start.6 = (bf16[32,1024]{1,0:T(8,128)(2,1)S(1)}, bf16[32,1024]{1,0:T(8,128)(2,1)S(1)}, u32[]{:S(2)}, u32[]{:S(2)}) collective-permute-start(bf16[32,1024]{1,0:T(8,128)(2,1)S(1)} %collective-permute-done.1.refs_2_), channel_id=1, source_target_pairs={{0,2},{2,0},{4,6},{6,4},{8,10},{10,8},{12,14},{14,12},{1,3},{3,1},... | collective-permute-start | bytes 196616 | tf_op jit(solution)/shard_map/ppermute | solution.py:193
  11.9 0.0 copy-done
  11.9 0.1 other_half.1
  12.1 0.0 collective-permute-done.3.refs_4_
  12.1 0.1 collective-permute-start.9
  12.2 0.0 copy-done.2
  12.2 0.0 copy-done.3
  12.2 0.0 copy-done.4
  12.2 1.1 %kron_bases.1 = (bf16[1024,1024]{1,0:T(8,128)(2,1)S(1)}, bf16[1024,1024]{1,0:T(8,128)(2,1)S(1)}, f32[1,1024]{1,0:T(1,128)S(1)}) custom-call(f32[1,32,32]{2,1,0:T(8,128)S(1)} %copy-done.2, f32[1,32,32]{2,1,0:T(8,128)S(1)} %copy-done.3, f32[1,32,32]{2,1,0:T(8,128)S(1)} %copy-done.4, bf16[64,1024]{1,0:T(8,128)(2,1)S(1)} %selectors.1.chosen_ref, ...), custom_call_target="tpu_custom_call" | custom-call | flops 536870912 | tf_op jit(solution)/shard_map/kron_bases/pallas_call | solution.py:65
  13.3 0.0 collective-permute-done.2.refs_3_
  13.3 0.0 collective-permute-done.4.refs_5_
  13.3 1.0 %early_rows.1.refs_0_ = bf16[192,1024]{1,0:T(8,128)(2,1)S(1)} custom-call(bf16[32,1024]{1,0:T(8,128)(2,1)S(1)} %bitcast.10, bf16[32,1024]{1,0:T(8,128)(2,1)S(1)} %collective-permute-done.refs_1_, bf16[32,1024]{1,0:T(8,128)(2,1)S(1)} %collective-permute-done.1.refs_2_, bf16[32,1024]{1,0:T(8,128)(2,1)S(1)} %collective-permute-done.2.refs_3_, ...), custom_call_target="tpu_custom_call" | custom-call | tf_op jit(solution)/shard_map/early_rows/pallas_call | solution.py:91
  14.3 0.0 collective-permute-done.5.refs_0_
  14.4 0.5 %collective-permute-done.6.refs_1_ = bf16[32,1024]{1,0:T(8,128)(2,1)S(1)} collective-permute-done((bf16[32,1024]{1,0:T(8,128)(2,1)S(1)}, bf16[32,1024]{1,0:T(8,128)(2,1)S(1)}, u32[]{:S(2)}, u32[]{:S(2)}) %collective-permute-start.6) | collective-permute-done | bytes 65568 | tf_op jit(solution)/shard_map/ppermute | solution.py:193
  14.8 0.1 collective-permute-start.7
  14.9 0.9 %late_rows.1.refs_1_ = bf16[64,1024]{1,0:T(8,128)(2,1)S(1)} custom-call(bf16[32,1024]{1,0:T(8,128)(2,1)S(1)} %collective-permute-done.5.refs_0_, bf16[32,1024]{1,0:T(8,128)(2,1)S(1)} %collective-permute-done.6.refs_1_, bf16[1024,1024]{1,0:T(8,128)(2,1)S(1)} %get-tuple-element.16.refs_6_.refs_2_, bf16[1024,1024]{1,0:T(8,128)(2,1)S(1)} %get-tuple-element.17.refs_7_.refs_3_, ...), custom_call_target="tpu_custom_call" | custom-call | flops 20937965568 | tf_op jit(solution)/shard_map/late_rows/pallas_call | solution.py:91
  15.8 0.5 %collective-permute-start.8 = (bf16[64,1024]{1,0:T(8,128)(2,1)S(1)}, bf16[64,1024]{1,0:T(8,128)(2,1)S(1)}, u32[]{:S(2)}, u32[]{:S(2)}) collective-permute-start(bf16[64,1024]{1,0:T(8,128)(2,1)S(1)} %late_rows.1.refs_1_), channel_id=1, source_target_pairs={{0,1},{1,0},{2,3},{3,2},{4,5},{5,4},{6,7},{7,6},{8,9},{9,8},{10,11... | collective-permute-start | bytes 393224 | tf_op jit(solution)/shard_map/ppermute | solution.py:197
  16.3 0.8 %first_scores.1.refs_3_ = f32[1024,256]{1,0:T(8,128)S(1)} custom-call(bf16[192,1024]{1,0:T(8,128)(2,1)S(1)} %early_rows.1.refs_0_, bf16[64,1024]{1,0:T(8,128)(2,1)S(1)} %late_rows.1.refs_1_, bf16[2048,1024]{1,0:T(8,128)(2,1)S(1)} %bitcast.4), custom_call_target="tpu_custom_call" | custom-call | flops 536870912 | bytes 2097152 | tf_op jit(solution)/shard_map/first_scores/pallas_call | solution.py:144
  17.1 0.2 %collective-permute-done.8.refs_1_ = bf16[64,1024]{1,0:T(8,128)(2,1)S(1)} collective-permute-done((bf16[64,1024]{1,0:T(8,128)(2,1)S(1)}, bf16[64,1024]{1,0:T(8,128)(2,1)S(1)}, u32[]{:S(2)}, u32[]{:S(2)}) %collective-permute-start.8) | collective-permute-done | bytes 131104 | tf_op jit(solution)/shard_map/ppermute | solution.py:197
  17.3 0.0 collective-permute-done.7.refs_0_
  17.3 0.0 collective-permute-done.9.refs_2_
  17.3 1.5 %last_scores.1 = bf16[1024,256]{1,0:T(8,128)(2,1)} custom-call(bf16[192,1024]{1,0:T(8,128)(2,1)S(1)} %collective-permute-done.7.refs_0_, bf16[64,1024]{1,0:T(8,128)(2,1)S(1)} %collective-permute-done.8.refs_1_, bf16[1024,1024]{1,0:T(8,128)(2,1)S(1)} %collective-permute-done.9.refs_2_, f32[1024,256]{1,0:T(8,128)S(1)} %first_scores.1.refs_3_), custom_call_target="tpu_custom_call" | custom-call | flops 536870912 | bytes 2097152 | tf_op jit(solution)/shard_map/last_scores/pallas_call | solution.py:159
  (1 shorter events, 0.0 us)
Async XLA Ops:
  0.0 5.4 %copy-start.1 = (bf16[32,1,1024]{2,0,1:T(8,128)(2,1)S(1)}, bf16[32,1,1024]{2,0,1:T(8,128)(2,1)}, u32[]{:S(2)}) copy-start(bf16[32,1,1024]{2,0,1:T(8,128)(2,1)} %param.6) | copy-start | bytes 196612
  0.0 11.9 %copy-start = (bf16[2048,1,1024]{2,0,1:T(8,128)(2,1)S(1)}, bf16[2048,1,1024]{2,0,1:T(8,128)(2,1)}, u32[]{:S(2)}) copy-start(bf16[2048,1,1024]{2,0,1:T(8,128)(2,1)} %param.5) | copy-start | bytes 12582916
  0.0 9.0 %collective-permute-start = (bf16[32,1024]{1,0:T(8,128)(2,1)}, bf16[32,1024]{1,0:T(8,128)(2,1)S(1)}, u32[]{:S(2)}, u32[]{:S(2)}) collective-permute-start(bf16[32,1024]{1,0:T(8,128)(2,1)} %bitcast.5), channel_id=1, source_target_pairs={{0,8},{2,10},{4,12},{6,14},{8,0},{10,2},{12,4},{14,6},{1,9},{3,11}... | collective-permute-start | bytes 196616 | tf_op jit(solution)/shard_map/ppermute | solution.py:193
  4.0 6.5 %collective-permute-start.1 = (bf16[32,1024]{1,0:T(8,128)(2,1)}, bf16[32,1024]{1,0:T(8,128)(2,1)S(1)}, u32[]{:S(2)}, u32[]{:S(2)}) collective-permute-start(bf16[32,1024]{1,0:T(8,128)(2,1)} %bitcast.6), channel_id=1, source_target_pairs={{0,12},{2,14},{4,8},{6,10},{8,4},{10,6},{12,0},{14,2},{1,13},{3,15... | collective-permute-start | bytes 196616 | tf_op jit(solution)/shard_map/ppermute | solution.py:193
  5.4 7.9 %collective-permute-start.2 = (bf16[32,1024]{1,0:T(8,128)(2,1)S(1)}, bf16[32,1024]{1,0:T(8,128)(2,1)S(1)}, u32[]{:S(2)}, u32[]{:S(2)}) collective-permute-start(bf16[32,1024]{1,0:T(8,128)(2,1)S(1)} %bitcast.7), channel_id=1, source_target_pairs={{0,4},{2,6},{4,0},{6,2},{8,12},{10,14},{12,8},{14,10},{1,5},{3,7},... | collective-permute-start | bytes 196616 | tf_op jit(solution)/shard_map/ppermute | solution.py:193
  5.7 6.3 %collective-permute-start.3 = (bf16[32,1024]{1,0:T(8,128)(2,1)S(1)}, bf16[32,1024]{1,0:T(8,128)(2,1)S(1)}, u32[]{:S(2)}, u32[]{:S(2)}) collective-permute-start(bf16[32,1024]{1,0:T(8,128)(2,1)S(1)} %bitcast.8), channel_id=1, source_target_pairs={{0,2},{2,0},{4,6},{6,4},{8,10},{10,8},{12,14},{14,12},{1,3},{3,1},... | collective-permute-start | bytes 196616 | tf_op jit(solution)/shard_map/ppermute | solution.py:193
  7.2 6.1 %collective-permute-start.4 = (bf16[32,1024]{1,0:T(8,128)(2,1)S(1)}, bf16[32,1024]{1,0:T(8,128)(2,1)S(1)}, u32[]{:S(2)}, u32[]{:S(2)}) collective-permute-start(bf16[32,1024]{1,0:T(8,128)(2,1)S(1)} %bitcast.9), channel_id=1, source_target_pairs={{0,6},{2,4},{4,2},{6,0},{8,14},{10,12},{12,10},{14,8},{1,7},{3,5},... | collective-permute-start | bytes 196616 | tf_op jit(solution)/shard_map/ppermute | solution.py:193
  9.0 3.2 %copy-start.2 = (f32[1,32,32]{2,1,0:T(8,128)S(1)}, f32[1,32,32]{2,1,0:T(8,128)}, u32[]{:S(2)}) copy-start(f32[1,32,32]{2,1,0:T(8,128)} %basis_in.1) | copy-start | bytes 12292
  9.0 3.2 %copy-start.3 = (f32[1,32,32]{2,1,0:T(8,128)S(1)}, f32[1,32,32]{2,1,0:T(8,128)}, u32[]{:S(2)}) copy-start(f32[1,32,32]{2,1,0:T(8,128)} %basis_out.1) | copy-start | bytes 12292
  9.0 3.2 %copy-start.4 = (f32[1,32,32]{2,1,0:T(8,128)S(1)}, f32[1,32,32]{2,1,0:T(8,128)}, u32[]{:S(2)}) copy-start(f32[1,32,32]{2,1,0:T(8,128)} %eigen.1) | copy-start | bytes 12292
  9.0 5.4 %collective-permute-start.5 = (bf16[32,1024]{1,0:T(8,128)(2,1)S(1)}, bf16[32,1024]{1,0:T(8,128)(2,1)S(1)}, u32[]{:S(2)}, u32[]{:S(2)}) collective-permute-start(bf16[32,1024]{1,0:T(8,128)(2,1)S(1)} %collective-permute-done.refs_1_), channel_id=1, source_target_pairs={{0,2},{2,0},{4,6},{6,4},{8,10},{10,8},{12,14},{14,12},{1,3},{3,1},... | collective-permute-start | bytes 196616 | tf_op jit(solution)/shard_map/ppermute | solution.py:193
  10.6 4.3 %collective-permute-start.6 = (bf16[32,1024]{1,0:T(8,128)(2,1)S(1)}, bf16[32,1024]{1,0:T(8,128)(2,1)S(1)}, u32[]{:S(2)}, u32[]{:S(2)}) collective-permute-start(bf16[32,1024]{1,0:T(8,128)(2,1)S(1)} %collective-permute-done.1.refs_2_), channel_id=1, source_target_pairs={{0,2},{2,0},{4,6},{6,4},{8,10},{10,8},{12,14},{14,12},{1,3},{3,1},... | collective-permute-start | bytes 196616 | tf_op jit(solution)/shard_map/ppermute | solution.py:193
  12.1 5.2 %collective-permute-start.9 = (bf16[1024,1024]{1,0:T(8,128)(2,1)S(1)}, bf16[1024,1024]{1,0:T(8,128)(2,1)S(1)}, u32[]{:S(2)}, u32[]{:S(2)}) collective-permute-start(bf16[1024,1024]{1,0:T(8,128)(2,1)S(1)} %other_half.1), channel_id=1, source_target_pairs={{0,1},{1,0},{2,3},{3,2},{4,5},{5,4},{6,7},{7,6},{8,9},{9,8},{10,11... | collective-permute-start | bytes 6291464 | tf_op jit(solution)/shard_map/ppermute | solution.py:197
  14.8 2.4 %collective-permute-start.7 = (bf16[192,1024]{1,0:T(8,128)(2,1)S(1)}, bf16[192,1024]{1,0:T(8,128)(2,1)S(1)}, u32[]{:S(2)}, u32[]{:S(2)}) collective-permute-start(bf16[192,1024]{1,0:T(8,128)(2,1)S(1)} %early_rows.1.refs_0_), channel_id=1, source_target_pairs={{0,1},{1,0},{2,3},{3,2},{4,5},{5,4},{6,7},{7,6},{8,9},{9,8},{10,11... | collective-permute-start | bytes 1179656 | tf_op jit(solution)/shard_map/ppermute | solution.py:197
  15.8 1.5 %collective-permute-start.8 = (bf16[64,1024]{1,0:T(8,128)(2,1)S(1)}, bf16[64,1024]{1,0:T(8,128)(2,1)S(1)}, u32[]{:S(2)}, u32[]{:S(2)}) collective-permute-start(bf16[64,1024]{1,0:T(8,128)(2,1)S(1)} %late_rows.1.refs_1_), channel_id=1, source_target_pairs={{0,1},{1,0},{2,3},{3,2},{4,5},{5,4},{6,7},{7,6},{8,9},{9,8},{10,11... | collective-permute-start | bytes 393224 | tf_op jit(solution)/shard_map/ppermute | solution.py:197

commit v8 on v7

--- a/solution.py
+++ b/solution.py
@@ -215,7 +215,6 @@
     bases = kron_bases(basis_in, basis_out, eigenvalues, chosen, queries)
     own = [precondition(groups[0], bases, "early_rows")]
     if len(groups) > 1:
-        own[0], *groups[1] = lax.optimization_barrier([own[0]] + groups[1])
         own.append(precondition(groups[1], bases, "late_rows"))
     other = [other_layer(w) for w in own]
     return last_scores(masks, other, other_queries, first_scores(masks, own, queries))

time: 18.9 us -> 18.8 us (level)
    ppermute x7, waiting for transfers between devices: 0.5 us -> 0.02 us  [exchange(): return lax.ppermute(x, 'pb', [(i, i ^ mask) for i in range(n)])]
    ppermute x3, waiting for transfers between devices: 0.2 us -> 0.52 us  [other_layer(): return lax.ppermute(x, 'layer', [(0, 1), (1, 0)])]
  transfers between devices with their start and end apart: 10 -> 10, of which waited for: 2 -> 1; matrix products, arithmetic and copies ran while one was open for 0% -> 0% of each run, Pallas kernels for 21% -> 21%
where the time goes in v8:
time: 18.8 us; the launch traced here: 18.6 us
  starting transfers between devices  12.6 us (67%)
  Pallas kernels  5.41 us (29%)
  waiting for transfers between devices  0.53 us (3%)
    ppermute x7, starting transfers between devices, exchange(): return lax.ppermute(x, 'pb', [(i, i ^ mask) for i in range(n)])  11.9 us
    pallas_call x2, Pallas kernels, precondition(): pl.pallas_call(precondition_kernel, out_shape=jax.ShapeDtypeStruct((rows,...  1.85 us
    pallas_call x1, Pallas kernels, last_scores(): pl.pallas_call(functools.partial(last_kernel, masks), out_shape=jax.Shape...  1.49 us
    pallas_call x1, Pallas kernels, kron_bases(): pl.pallas_call(kron_kernel, out_shape=tuple((jax.ShapeDtypeStruct(*x) for...  1.13 us
    pallas_call x1, Pallas kernels, first_scores(): pl.pallas_call(functools.partial(first_kernel, masks), out_shape=jax.Shap...  0.78 us
    ppermute x3, starting transfers between devices, other_layer(): return lax.ppermute(x, 'layer', [(0, 1), (1, 0)])  0.71 us
    ppermute x3, waiting for transfers between devices, other_layer(): return lax.ppermute(x, 'layer', [(0, 1), (1, 0)])  0.52 us
  transfers between devices with their start and end apart: 10, of which 1 were waited for; matrix products, arithmetic and copies ran while one was open for 0% of the time, Pallas kernels for 21%

profile of v8, /device:TPU:0, one launch (start us, length us, event | category | flops | bytes accessed | tf_op | source)
XLA Modules:
  0.0 18.6 jit_solution(11263425499602323690)
XLA Ops:
  0.0 0.0 copy-start.1
  0.0 0.0 copy-start
  0.0 4.0 %collective-permute-start = (bf16[32,1024]{1,0:T(8,128)(2,1)}, bf16[32,1024]{1,0:T(8,128)(2,1)S(1)}, u32[]{:S(2)}, u32[]{:S(2)}) collective-permute-start(bf16[32,1024]{1,0:T(8,128)(2,1)} %bitcast.5), channel_id=1, source_target_pairs={{0,8},{2,10},{4,12},{6,14},{8,0},{10,2},{12,4},{14,6},{1,9},{3,11}... | collective-permute-start | bytes 196616 | tf_op jit(solution)/shard_map/ppermute | solution.py:193
  4.0 1.3 %collective-permute-start.1 = (bf16[32,1024]{1,0:T(8,128)(2,1)}, bf16[32,1024]{1,0:T(8,128)(2,1)S(1)}, u32[]{:S(2)}, u32[]{:S(2)}) collective-permute-start(bf16[32,1024]{1,0:T(8,128)(2,1)} %bitcast.6), channel_id=1, source_target_pairs={{0,12},{2,14},{4,8},{6,10},{8,4},{10,6},{12,0},{14,2},{1,13},{3,15... | collective-permute-start | bytes 196616 | tf_op jit(solution)/shard_map/ppermute | solution.py:193
  5.4 0.0 copy-done.1
  5.4 0.3 %collective-permute-start.2 = (bf16[32,1024]{1,0:T(8,128)(2,1)S(1)}, bf16[32,1024]{1,0:T(8,128)(2,1)S(1)}, u32[]{:S(2)}, u32[]{:S(2)}) collective-permute-start(bf16[32,1024]{1,0:T(8,128)(2,1)S(1)} %bitcast.7), channel_id=1, source_target_pairs={{0,4},{2,6},{4,0},{6,2},{8,12},{10,14},{12,8},{14,10},{1,5},{3,7},... | collective-permute-start | bytes 196616 | tf_op jit(solution)/shard_map/ppermute | solution.py:193
  5.7 1.5 %collective-permute-start.3 = (bf16[32,1024]{1,0:T(8,128)(2,1)S(1)}, bf16[32,1024]{1,0:T(8,128)(2,1)S(1)}, u32[]{:S(2)}, u32[]{:S(2)}) collective-permute-start(bf16[32,1024]{1,0:T(8,128)(2,1)S(1)} %bitcast.8), channel_id=1, source_target_pairs={{0,2},{2,0},{4,6},{6,4},{8,10},{10,8},{12,14},{14,12},{1,3},{3,1},... | collective-permute-start | bytes 196616 | tf_op jit(solution)/shard_map/ppermute | solution.py:193
  7.2 1.8 %collective-permute-start.4 = (bf16[32,1024]{1,0:T(8,128)(2,1)S(1)}, bf16[32,1024]{1,0:T(8,128)(2,1)S(1)}, u32[]{:S(2)}, u32[]{:S(2)}) collective-permute-start(bf16[32,1024]{1,0:T(8,128)(2,1)S(1)} %bitcast.9), channel_id=1, source_target_pairs={{0,6},{2,4},{4,2},{6,0},{8,14},{10,12},{12,10},{14,8},{1,7},{3,5},... | collective-permute-start | bytes 196616 | tf_op jit(solution)/shard_map/ppermute | solution.py:193
  9.0 0.0 copy-start.2
  9.0 0.0 copy-start.3
  9.0 0.0 copy-start.4
  9.0 0.0 collective-permute-done.refs_1_
  9.0 1.6 %collective-permute-start.6 = (bf16[32,1024]{1,0:T(8,128)(2,1)S(1)}, bf16[32,1024]{1,0:T(8,128)(2,1)S(1)}, u32[]{:S(2)}, u32[]{:S(2)}) collective-permute-start(bf16[32,1024]{1,0:T(8,128)(2,1)S(1)} %collective-permute-done.refs_1_), channel_id=1, source_target_pairs={{0,2},{2,0},{4,6},{6,4},{8,10},{10,8},{12,14},{14,12},{1,3},{3,1},... | collective-permute-start | bytes 196616 | tf_op jit(solution)/shard_map/ppermute | solution.py:193
  10.6 0.0 collective-permute-done.1.refs_2_
  10.6 1.4 %collective-permute-start.7 = (bf16[32,1024]{1,0:T(8,128)(2,1)S(1)}, bf16[32,1024]{1,0:T(8,128)(2,1)S(1)}, u32[]{:S(2)}, u32[]{:S(2)}) collective-permute-start(bf16[32,1024]{1,0:T(8,128)(2,1)S(1)} %collective-permute-done.1.refs_2_), channel_id=1, source_target_pairs={{0,2},{2,0},{4,6},{6,4},{8,10},{10,8},{12,14},{14,12},{1,3},{3,1},... | collective-permute-start | bytes 196616 | tf_op jit(solution)/shard_map/ppermute | solution.py:193
  11.9 0.0 copy-done
  11.9 0.1 other_half.1
  12.1 0.0 collective-permute-done.3.refs_4_
  12.1 0.1 collective-permute-start.9
  12.2 0.0 copy-done.2
  12.2 0.0 copy-done.3
  12.2 0.0 copy-done.4
  12.2 1.1 %kron_bases.1 = (bf16[1024,1024]{1,0:T(8,128)(2,1)S(1)}, bf16[1024,1024]{1,0:T(8,128)(2,1)S(1)}, f32[1,1024]{1,0:T(1,128)S(1)}) custom-call(f32[1,32,32]{2,1,0:T(8,128)S(1)} %copy-done.2, f32[1,32,32]{2,1,0:T(8,128)S(1)} %copy-done.3, f32[1,32,32]{2,1,0:T(8,128)S(1)} %copy-done.4, bf16[64,1024]{1,0:T(8,128)(2,1)S(1)} %selectors.1.chosen_ref, ...), custom_call_target="tpu_custom_call" | custom-call | flops 536870912 | tf_op jit(solution)/shard_map/kron_bases/pallas_call | solution.py:65
  13.3 0.0 collective-permute-done.2.refs_3_
  13.3 0.0 collective-permute-done.4.refs_5_
  13.3 1.0 %early_rows.1.refs_0_ = bf16[192,1024]{1,0:T(8,128)(2,1)S(1)} custom-call(bf16[32,1024]{1,0:T(8,128)(2,1)S(1)} %bitcast.10, bf16[32,1024]{1,0:T(8,128)(2,1)S(1)} %collective-permute-done.refs_1_, bf16[32,1024]{1,0:T(8,128)(2,1)S(1)} %collective-permute-done.1.refs_2_, bf16[32,1024]{1,0:T(8,128)(2,1)S(1)} %collective-permute-done.2.refs_3_, ...), custom_call_target="tpu_custom_call" | custom-call | tf_op jit(solution)/shard_map/early_rows/pallas_call | solution.py:91
  14.3 0.5 %collective-permute-start.5 = (bf16[192,1024]{1,0:T(8,128)(2,1)S(1)}, bf16[192,1024]{1,0:T(8,128)(2,1)S(1)}, u32[]{:S(2)}, u32[]{:S(2)}) collective-permute-start(bf16[192,1024]{1,0:T(8,128)(2,1)S(1)} %early_rows.1.refs_0_), channel_id=1, source_target_pairs={{0,1},{1,0},{2,3},{3,2},{4,5},{5,4},{6,7},{7,6},{8,9},{9,8},{10,11... | collective-permute-start | bytes 1179656 | tf_op jit(solution)/shard_map/ppermute | solution.py:197
  14.9 0.0 collective-permute-done.6.refs_0_
  14.9 0.0 collective-permute-done.7.refs_1_
  14.9 0.9 %late_rows.1.refs_1_ = bf16[64,1024]{1,0:T(8,128)(2,1)S(1)} custom-call(bf16[32,1024]{1,0:T(8,128)(2,1)S(1)} %collective-permute-done.6.refs_0_, bf16[32,1024]{1,0:T(8,128)(2,1)S(1)} %collective-permute-done.7.refs_1_, bf16[1024,1024]{1,0:T(8,128)(2,1)S(1)} %get-tuple-element.13.refs_6_.refs_2_, bf16[1024,1024]{1,0:T(8,128)(2,1)S(1)} %get-tuple-element.14.refs_7_.refs_3_, ...), custom_call_target="tpu_custom_call" | custom-call | flops 20937965568 | tf_op jit(solution)/shard_map/late_rows/pallas_call | solution.py:91
  15.7 0.1 collective-permute-start.8
  15.9 0.8 %first_scores.1.refs_3_ = f32[1024,256]{1,0:T(8,128)S(1)} custom-call(bf16[192,1024]{1,0:T(8,128)(2,1)S(1)} %early_rows.1.refs_0_, bf16[64,1024]{1,0:T(8,128)(2,1)S(1)} %late_rows.1.refs_1_, bf16[2048,1024]{1,0:T(8,128)(2,1)S(1)} %bitcast.4), custom_call_target="tpu_custom_call" | custom-call | flops 536870912 | bytes 2097152 | tf_op jit(solution)/shard_map/first_scores/pallas_call | solution.py:144
  16.6 0.5 %collective-permute-done.8.refs_1_ = bf16[64,1024]{1,0:T(8,128)(2,1)S(1)} collective-permute-done((bf16[64,1024]{1,0:T(8,128)(2,1)S(1)}, bf16[64,1024]{1,0:T(8,128)(2,1)S(1)}, u32[]{:S(2)}, u32[]{:S(2)}) %collective-permute-start.8) | collective-permute-done | bytes 131104 | tf_op jit(solution)/shard_map/ppermute | solution.py:197
  17.2 0.0 collective-permute-done.5.refs_0_
  17.2 0.0 collective-permute-done.9.refs_2_
  17.2 1.5 %last_scores.1 = bf16[1024,256]{1,0:T(8,128)(2,1)} custom-call(bf16[192,1024]{1,0:T(8,128)(2,1)S(1)} %collective-permute-done.5.refs_0_, bf16[64,1024]{1,0:T(8,128)(2,1)S(1)} %collective-permute-done.8.refs_1_, bf16[1024,1024]{1,0:T(8,128)(2,1)S(1)} %collective-permute-done.9.refs_2_, f32[1024,256]{1,0:T(8,128)S(1)} %first_scores.1.refs_3_), custom_call_target="tpu_custom_call" | custom-call | flops 536870912 | bytes 2097152 | tf_op jit(solution)/shard_map/last_scores/pallas_call | solution.py:159
  (1 shorter events, 0.0 us)
Async XLA Ops:
  0.0 5.4 %copy-start.1 = (bf16[32,1,1024]{2,0,1:T(8,128)(2,1)S(1)}, bf16[32,1,1024]{2,0,1:T(8,128)(2,1)}, u32[]{:S(2)}) copy-start(bf16[32,1,1024]{2,0,1:T(8,128)(2,1)} %param.6) | copy-start | bytes 196612
  0.0 11.9 %copy-start = (bf16[2048,1,1024]{2,0,1:T(8,128)(2,1)S(1)}, bf16[2048,1,1024]{2,0,1:T(8,128)(2,1)}, u32[]{:S(2)}) copy-start(bf16[2048,1,1024]{2,0,1:T(8,128)(2,1)} %param.5) | copy-start | bytes 12582916
  0.0 9.0 %collective-permute-start = (bf16[32,1024]{1,0:T(8,128)(2,1)}, bf16[32,1024]{1,0:T(8,128)(2,1)S(1)}, u32[]{:S(2)}, u32[]{:S(2)}) collective-permute-start(bf16[32,1024]{1,0:T(8,128)(2,1)} %bitcast.5), channel_id=1, source_target_pairs={{0,8},{2,10},{4,12},{6,14},{8,0},{10,2},{12,4},{14,6},{1,9},{3,11}... | collective-permute-start | bytes 196616 | tf_op jit(solution)/shard_map/ppermute | solution.py:193
  4.0 6.5 %collective-permute-start.1 = (bf16[32,1024]{1,0:T(8,128)(2,1)}, bf16[32,1024]{1,0:T(8,128)(2,1)S(1)}, u32[]{:S(2)}, u32[]{:S(2)}) collective-permute-start(bf16[32,1024]{1,0:T(8,128)(2,1)} %bitcast.6), channel_id=1, source_target_pairs={{0,12},{2,14},{4,8},{6,10},{8,4},{10,6},{12,0},{14,2},{1,13},{3,15... | collective-permute-start | bytes 196616 | tf_op jit(solution)/shard_map/ppermute | solution.py:193
  5.4 7.9 %collective-permute-start.2 = (bf16[32,1024]{1,0:T(8,128)(2,1)S(1)}, bf16[32,1024]{1,0:T(8,128)(2,1)S(1)}, u32[]{:S(2)}, u32[]{:S(2)}) collective-permute-start(bf16[32,1024]{1,0:T(8,128)(2,1)S(1)} %bitcast.7), channel_id=1, source_target_pairs={{0,4},{2,6},{4,0},{6,2},{8,12},{10,14},{12,8},{14,10},{1,5},{3,7},... | collective-permute-start | bytes 196616 | tf_op jit(solution)/shard_map/ppermute | solution.py:193
  5.7 6.3 %collective-permute-start.3 = (bf16[32,1024]{1,0:T(8,128)(2,1)S(1)}, bf16[32,1024]{1,0:T(8,128)(2,1)S(1)}, u32[]{:S(2)}, u32[]{:S(2)}) collective-permute-start(bf16[32,1024]{1,0:T(8,128)(2,1)S(1)} %bitcast.8), channel_id=1, source_target_pairs={{0,2},{2,0},{4,6},{6,4},{8,10},{10,8},{12,14},{14,12},{1,3},{3,1},... | collective-permute-start | bytes 196616 | tf_op jit(solution)/shard_map/ppermute | solution.py:193
  7.2 6.1 %collective-permute-start.4 = (bf16[32,1024]{1,0:T(8,128)(2,1)S(1)}, bf16[32,1024]{1,0:T(8,128)(2,1)S(1)}, u32[]{:S(2)}, u32[]{:S(2)}) collective-permute-start(bf16[32,1024]{1,0:T(8,128)(2,1)S(1)} %bitcast.9), channel_id=1, source_target_pairs={{0,6},{2,4},{4,2},{6,0},{8,14},{10,12},{12,10},{14,8},{1,7},{3,5},... | collective-permute-start | bytes 196616 | tf_op jit(solution)/shard_map/ppermute | solution.py:193
  9.0 3.2 %copy-start.2 = (f32[1,32,32]{2,1,0:T(8,128)S(1)}, f32[1,32,32]{2,1,0:T(8,128)}, u32[]{:S(2)}) copy-start(f32[1,32,32]{2,1,0:T(8,128)} %basis_in.1) | copy-start | bytes 12292
  9.0 3.2 %copy-start.3 = (f32[1,32,32]{2,1,0:T(8,128)S(1)}, f32[1,32,32]{2,1,0:T(8,128)}, u32[]{:S(2)}) copy-start(f32[1,32,32]{2,1,0:T(8,128)} %basis_out.1) | copy-start | bytes 12292
  9.0 3.2 %copy-start.4 = (f32[1,32,32]{2,1,0:T(8,128)S(1)}, f32[1,32,32]{2,1,0:T(8,128)}, u32[]{:S(2)}) copy-start(f32[1,32,32]{2,1,0:T(8,128)} %eigen.1) | copy-start | bytes 12292
  9.0 5.9 %collective-permute-start.6 = (bf16[32,1024]{1,0:T(8,128)(2,1)S(1)}, bf16[32,1024]{1,0:T(8,128)(2,1)S(1)}, u32[]{:S(2)}, u32[]{:S(2)}) collective-permute-start(bf16[32,1024]{1,0:T(8,128)(2,1)S(1)} %collective-permute-done.refs_1_), channel_id=1, source_target_pairs={{0,2},{2,0},{4,6},{6,4},{8,10},{10,8},{12,14},{14,12},{1,3},{3,1},... | collective-permute-start | bytes 196616 | tf_op jit(solution)/shard_map/ppermute | solution.py:193
  10.6 4.3 %collective-permute-start.7 = (bf16[32,1024]{1,0:T(8,128)(2,1)S(1)}, bf16[32,1024]{1,0:T(8,128)(2,1)S(1)}, u32[]{:S(2)}, u32[]{:S(2)}) collective-permute-start(bf16[32,1024]{1,0:T(8,128)(2,1)S(1)} %collective-permute-done.1.refs_2_), channel_id=1, source_target_pairs={{0,2},{2,0},{4,6},{6,4},{8,10},{10,8},{12,14},{14,12},{1,3},{3,1},... | collective-permute-start | bytes 196616 | tf_op jit(solution)/shard_map/ppermute | solution.py:193
  12.1 5.1 %collective-permute-start.9 = (bf16[1024,1024]{1,0:T(8,128)(2,1)S(1)}, bf16[1024,1024]{1,0:T(8,128)(2,1)S(1)}, u32[]{:S(2)}, u32[]{:S(2)}) collective-permute-start(bf16[1024,1024]{1,0:T(8,128)(2,1)S(1)} %other_half.1), channel_id=1, source_target_pairs={{0,1},{1,0},{2,3},{3,2},{4,5},{5,4},{6,7},{7,6},{8,9},{9,8},{10,11... | collective-permute-start | bytes 6291464 | tf_op jit(solution)/shard_map/ppermute | solution.py:197
  14.3 2.8 %collective-permute-start.5 = (bf16[192,1024]{1,0:T(8,128)(2,1)S(1)}, bf16[192,1024]{1,0:T(8,128)(2,1)S(1)}, u32[]{:S(2)}, u32[]{:S(2)}) collective-permute-start(bf16[192,1024]{1,0:T(8,128)(2,1)S(1)} %early_rows.1.refs_0_), channel_id=1, source_target_pairs={{0,1},{1,0},{2,3},{3,2},{4,5},{5,4},{6,7},{7,6},{8,9},{9,8},{10,11... | collective-permute-start | bytes 1179656 | tf_op jit(solution)/shard_map/ppermute | solution.py:197
  15.7 1.4 %collective-permute-start.8 = (bf16[64,1024]{1,0:T(8,128)(2,1)S(1)}, bf16[64,1024]{1,0:T(8,128)(2,1)S(1)}, u32[]{:S(2)}, u32[]{:S(2)}) collective-permute-start(bf16[64,1024]{1,0:T(8,128)(2,1)S(1)} %late_rows.1.refs_1_), channel_id=1, source_target_pairs={{0,1},{1,0},{2,3},{3,2},{4,5},{5,4},{6,7},{7,6},{8,9},{9,8},{10,11... | collective-permute-start | bytes 393224 | tf_op jit(solution)/shard_map/ppermute | solution.py:197

commit v9 on v8

--- a/solution.py
+++ b/solution.py
@@ -75,9 +75,10 @@
 
 def precondition_kernel(*refs):
     *blocks, kron_ref, turned_ref, inverse_ref, w_ref = refs
-    size, total = blocks[0].shape[0], w_ref.shape[0]
-    for i, block in enumerate(blocks):
-        w_ref[pl.ds(i * size, size), :] = block[...]
+    row, total = 0, w_ref.shape[0]
+    for block in blocks:
+        w_ref[pl.ds(row, block.shape[0]), :] = block[...]
+        row += block.shape[0]
     step = min(total, 256)
     for i in range(total // step):
         rows = pl.ds(i * step, step)
@@ -94,7 +95,7 @@
         in_specs=[VMEM] * (len(blocks) + 3),
         out_specs=VMEM,
         compiler_params=PARAMS,
-        cost_estimate=estimate((0 if name == "early_rows" else int(19.5 * grad**3)), 0),
+        cost_estimate=estimate((0 if name == "early_rows" else int(18.5 * grad**3)), 0),
         name=name,
     )(*blocks, *bases)
 
@@ -189,6 +190,24 @@
     )(queries)
 
 
+def join_kernel(first_ref, second_ref, out_ref):
+    rows = first_ref.shape[0]
+    out_ref[:rows, :] = first_ref[...]
+    out_ref[rows:, :] = second_ref[...]
+
+
+def join(first, second):
+    return pl.pallas_call(
+        join_kernel,
+        out_shape=jax.ShapeDtypeStruct((2 * first.shape[0], first.shape[1]), BF16),
+        in_specs=[VMEM] * 2,
+        out_specs=VMEM,
+        compiler_params=PARAMS,
+        cost_estimate=estimate(0, 0),
+        name="join_blocks",
+    )(first, second)
+
+
 def exchange(x, n, mask):
     return lax.ppermute(x, "pb", [(i, i ^ mask) for i in range(n)])
 
@@ -202,12 +221,14 @@
     queries = query_grads.reshape(query_grads.shape[0], -1)
     chosen = selectors(basis_out.shape[1], basis_in.shape[1])
     if n == 8:
-        far = [exchange(train, n, mask) for mask in (4, 6)]
+        got = {mask: exchange(train, n, mask) for mask in (4,)}
         behind, chosen = lax.optimization_barrier((train, chosen))
-        near = [exchange(behind, n, mask) for mask in (2, 1, 3)]
-        groups, masks = [[train] + far + near, [exchange(block, n, 1) for block in far]], (0, 4, 6, 2, 1, 3, 5, 7)
+        got.update({mask: exchange(behind, n, mask) for mask in (2, 1, 3)})
+        late = [exchange(got[4], n, 3), exchange(got[4], n, 2), exchange(got[4], n, 1)]
+        masks = (0, *got, 7, 6, 5)
+        groups = [[train] + list(got.values()), late]
         loose, = lax.optimization_barrier((queries,))
-        sent, _ = lax.optimization_barrier((other_half(loose), near[1]))
+        sent, _ = lax.optimization_barrier((other_half(loose), got[1]))
     else:
         groups, masks = [[lax.all_gather(train, "pb", axis=0, tiled=True)]], (0,)
         sent = other_half(queries)

time: 18.8 us -> 18.9 us (level)
  waiting for transfers between devices: 0.53 us -> 1.64 us
  starting transfers between devices: 12.6 us -> 11.8 us
    ppermute x7, waiting for transfers between devices: 0.02 us -> 1 us  [exchange(): return lax.ppermute(x, 'pb', [(i, i ^ mask) for i in range(n)])]
    ppermute x7, starting transfers between devices: 11.9 us -> 11.1 us  [exchange(): return lax.ppermute(x, 'pb', [(i, i ^ mask) for i in range(n)])]
  transfers between devices with their start and end apart: 10 -> 10, of which waited for: 1 -> 4; matrix products, arithmetic and copies ran while one was open for 0% -> 0% of each run, Pallas kernels for 21% -> 20%
where the time goes in v9:
time: 18.9 us; the launch traced here: 18.8 us
  starting transfers between devices  11.8 us (62%)
  Pallas kernels  5.24 us (28%)
  waiting for transfers between devices  1.64 us (9%)
    ppermute x7, starting transfers between devices, exchange(): return lax.ppermute(x, 'pb', [(i, i ^ mask) for i in range(n)])  11.1 us
    pallas_call x2, Pallas kernels, precondition(): pl.pallas_call(precondition_kernel, out_shape=jax.ShapeDtypeStruct((rows,...  1.68 us
    pallas_call x1, Pallas kernels, last_scores(): pl.pallas_call(functools.partial(last_kernel, masks), out_shape=jax.Shape...  1.49 us
    pallas_call x1, Pallas kernels, kron_bases(): pl.pallas_call(kron_kernel, out_shape=tuple((jax.ShapeDtypeStruct(*x) for...  1.13 us
    ppermute x7, waiting for transfers between devices, exchange(): return lax.ppermute(x, 'pb', [(i, i ^ mask) for i in range(n)])  1 us
    pallas_call x1, Pallas kernels, first_scores(): pl.pallas_call(functools.partial(first_kernel, masks), out_shape=jax.Shap...  0.79 us
    ppermute x3, starting transfers between devices, other_layer(): return lax.ppermute(x, 'layer', [(0, 1), (1, 0)])  0.67 us
    ppermute x3, waiting for transfers between devices, other_layer(): return lax.ppermute(x, 'layer', [(0, 1), (1, 0)])  0.64 us
  transfers between devices with their start and end apart: 10, of which 4 were waited for; matrix products, arithmetic and copies ran while one was open for 0% of the time, Pallas kernels for 20%

profile of v9, /device:TPU:0, one launch (start us, length us, event | category | flops | bytes accessed | tf_op | source)
XLA Modules:
  0.0 18.8 jit_solution(10538876406593682763)
XLA Ops:
  0.0 0.0 copy-start.1
  0.0 0.0 copy-start
  0.0 4.0 %collective-permute-start = (bf16[32,1024]{1,0:T(8,128)(2,1)}, bf16[32,1024]{1,0:T(8,128)(2,1)S(1)}, u32[]{:S(2)}, u32[]{:S(2)}) collective-permute-start(bf16[32,1024]{1,0:T(8,128)(2,1)} %bitcast.5), channel_id=1, source_target_pairs={{0,8},{2,10},{4,12},{6,14},{8,0},{10,2},{12,4},{14,6},{1,9},{3,11}... | collective-permute-start | bytes 196616 | tf_op jit(solution)/shard_map/ppermute | solution.py:212
  4.1 0.0 copy-done.1
  4.1 1.6 %collective-permute-start.2 = (bf16[32,1024]{1,0:T(8,128)(2,1)S(1)}, bf16[32,1024]{1,0:T(8,128)(2,1)S(1)}, u32[]{:S(2)}, u32[]{:S(2)}) collective-permute-start(bf16[32,1024]{1,0:T(8,128)(2,1)S(1)} %bitcast.6), channel_id=1, source_target_pairs={{0,2},{2,0},{4,6},{6,4},{8,10},{10,8},{12,14},{14,12},{1,3},{3,1},... | collective-permute-start | bytes 196616 | tf_op jit(solution)/shard_map/ppermute | solution.py:212
  5.6 1.6 %collective-permute-start.1 = (bf16[32,1024]{1,0:T(8,128)(2,1)S(1)}, bf16[32,1024]{1,0:T(8,128)(2,1)S(1)}, u32[]{:S(2)}, u32[]{:S(2)}) collective-permute-start(bf16[32,1024]{1,0:T(8,128)(2,1)S(1)} %bitcast.7), channel_id=1, source_target_pairs={{0,4},{2,6},{4,0},{6,2},{8,12},{10,14},{12,8},{14,10},{1,5},{3,7},... | collective-permute-start | bytes 196616 | tf_op jit(solution)/shard_map/ppermute | solution.py:212
  7.2 0.4 %collective-permute-start.3 = (bf16[32,1024]{1,0:T(8,128)(2,1)S(1)}, bf16[32,1024]{1,0:T(8,128)(2,1)S(1)}, u32[]{:S(2)}, u32[]{:S(2)}) collective-permute-start(bf16[32,1024]{1,0:T(8,128)(2,1)S(1)} %bitcast.8), channel_id=1, source_target_pairs={{0,6},{2,4},{4,2},{6,0},{8,14},{10,12},{12,10},{14,8},{1,7},{3,5},... | collective-permute-start | bytes 196616 | tf_op jit(solution)/shard_map/ppermute | solution.py:212
  7.6 0.0 copy-start.2
  7.6 0.0 copy-start.3
  7.6 0.0 copy-start.4
  7.6 0.4 %collective-permute-done.refs_1_ = bf16[32,1024]{1,0:T(8,128)(2,1)S(1)} collective-permute-done((bf16[32,1024]{1,0:T(8,128)(2,1)}, bf16[32,1024]{1,0:T(8,128)(2,1)S(1)}, u32[]{:S(2)}, u32[]{:S(2)}) %collective-permute-start) | collective-permute-done | bytes 65568 | tf_op jit(solution)/shard_map/ppermute | solution.py:212
  8.1 2.1 %collective-permute-start.5 = (bf16[32,1024]{1,0:T(8,128)(2,1)S(1)}, bf16[32,1024]{1,0:T(8,128)(2,1)S(1)}, u32[]{:S(2)}, u32[]{:S(2)}) collective-permute-start(bf16[32,1024]{1,0:T(8,128)(2,1)S(1)} %collective-permute-done.refs_1_), channel_id=1, source_target_pairs={{0,6},{2,4},{4,2},{6,0},{8,14},{10,12},{12,10},{14,8},{1,7},{3,5},... | collective-permute-start | bytes 196616 | tf_op jit(solution)/shard_map/ppermute | solution.py:212
  10.2 0.4 %collective-permute-start.6 = (bf16[32,1024]{1,0:T(8,128)(2,1)S(1)}, bf16[32,1024]{1,0:T(8,128)(2,1)S(1)}, u32[]{:S(2)}, u32[]{:S(2)}) collective-permute-start(bf16[32,1024]{1,0:T(8,128)(2,1)S(1)} %collective-permute-done.refs_1_), channel_id=1, source_target_pairs={{0,4},{2,6},{4,0},{6,2},{8,12},{10,14},{12,8},{14,10},{1,5},{3,7},... | collective-permute-start | bytes 196616 | tf_op jit(solution)/shard_map/ppermute | solution.py:212
  10.7 0.0 collective-permute-done.2.refs_3_
  10.7 0.9 %collective-permute-start.7 = (bf16[32,1024]{1,0:T(8,128)(2,1)S(1)}, bf16[32,1024]{1,0:T(8,128)(2,1)S(1)}, u32[]{:S(2)}, u32[]{:S(2)}) collective-permute-start(bf16[32,1024]{1,0:T(8,128)(2,1)S(1)} %collective-permute-done.refs_1_), channel_id=1, source_target_pairs={{0,2},{2,0},{4,6},{6,4},{8,10},{10,8},{12,14},{14,12},{1,3},{3,1},... | collective-permute-start | bytes 196616 | tf_op jit(solution)/shard_map/ppermute | solution.py:212
  11.6 0.0 copy-done
  11.6 0.1 other_half.1
  11.7 0.0 collective-permute-done.1.refs_2_
  11.7 0.1 collective-permute-start.9
  11.8 0.0 copy-done.2
  11.8 0.0 copy-done.3
  11.8 0.0 copy-done.4
  11.8 1.1 %kron_bases.1 = (bf16[1024,1024]{1,0:T(8,128)(2,1)S(1)}, bf16[1024,1024]{1,0:T(8,128)(2,1)S(1)}, f32[1,1024]{1,0:T(1,128)S(1)}) custom-call(f32[1,32,32]{2,1,0:T(8,128)S(1)} %copy-done.2, f32[1,32,32]{2,1,0:T(8,128)S(1)} %copy-done.3, f32[1,32,32]{2,1,0:T(8,128)S(1)} %copy-done.4, bf16[64,1024]{1,0:T(8,128)(2,1)S(1)} %selectors.1.chosen_ref, ...), custom_call_target="tpu_custom_call" | custom-call | flops 536870912 | tf_op jit(solution)/shard_map/kron_bases/pallas_call | solution.py:65
  13.0 0.0 collective-permute-done.3.refs_4_
  13.0 0.9 %early_rows.1.refs_0_ = bf16[160,1024]{1,0:T(8,128)(2,1)S(1)} custom-call(bf16[32,1024]{1,0:T(8,128)(2,1)S(1)} %bitcast.9, bf16[32,1024]{1,0:T(8,128)(2,1)S(1)} %collective-permute-done.refs_1_, bf16[32,1024]{1,0:T(8,128)(2,1)S(1)} %collective-permute-done.1.refs_2_, bf16[32,1024]{1,0:T(8,128)(2,1)S(1)} %collective-permute-done.2.refs_3_, ...), custom_call_target="tpu_custom_call" | custom-call | tf_op jit(solution)/shard_map/early_rows/pallas_call | solution.py:92
  13.8 0.5 %collective-permute-start.4 = (bf16[160,1024]{1,0:T(8,128)(2,1)S(1)}, bf16[160,1024]{1,0:T(8,128)(2,1)S(1)}, u32[]{:S(2)}, u32[]{:S(2)}) collective-permute-start(bf16[160,1024]{1,0:T(8,128)(2,1)S(1)} %early_rows.1.refs_0_), channel_id=1, source_target_pairs={{0,1},{1,0},{2,3},{3,2},{4,5},{5,4},{6,7},{7,6},{8,9},{9,8},{10,11... | collective-permute-start | bytes 983048 | tf_op jit(solution)/shard_map/ppermute | solution.py:216
  14.4 0.0 collective-permute-done.5.refs_0_
  14.4 0.1 collective-permute-done.6.refs_1_
  14.5 0.5 %collective-permute-done.7.refs_2_ = bf16[32,1024]{1,0:T(8,128)(2,1)S(1)} collective-permute-done((bf16[32,1024]{1,0:T(8,128)(2,1)S(1)}, bf16[32,1024]{1,0:T(8,128)(2,1)S(1)}, u32[]{:S(2)}, u32[]{:S(2)}) %collective-permute-start.7) | collective-permute-done | bytes 65568 | tf_op jit(solution)/shard_map/ppermute | solution.py:212
  14.9 0.8 %late_rows.1.refs_1_ = bf16[96,1024]{1,0:T(8,128)(2,1)S(1)} custom-call(bf16[32,1024]{1,0:T(8,128)(2,1)S(1)} %collective-permute-done.5.refs_0_, bf16[32,1024]{1,0:T(8,128)(2,1)S(1)} %collective-permute-done.6.refs_1_, bf16[32,1024]{1,0:T(8,128)(2,1)S(1)} %collective-permute-done.7.refs_2_, bf16[1024,1024]{1,0:T(8,128)(2,1)S(1)} %get-tuple-element.13.refs_5_.refs_3_, ...), custom_call_target="tpu_custom_call" | custom-call | flops 19864223744 | tf_op jit(solution)/shard_map/late_rows/pallas_call | solution.py:92
  15.8 0.1 collective-permute-start.8
  15.8 0.8 %first_scores.1.refs_3_ = f32[1024,256]{1,0:T(8,128)S(1)} custom-call(bf16[160,1024]{1,0:T(8,128)(2,1)S(1)} %early_rows.1.refs_0_, bf16[96,1024]{1,0:T(8,128)(2,1)S(1)} %late_rows.1.refs_1_, bf16[2048,1024]{1,0:T(8,128)(2,1)S(1)} %bitcast.4), custom_call_target="tpu_custom_call" | custom-call | flops 536870912 | bytes 2097152 | tf_op jit(solution)/shard_map/first_scores/pallas_call | solution.py:145
  16.6 0.6 %collective-permute-done.8.refs_1_ = bf16[96,1024]{1,0:T(8,128)(2,1)S(1)} collective-permute-done((bf16[96,1024]{1,0:T(8,128)(2,1)S(1)}, bf16[96,1024]{1,0:T(8,128)(2,1)S(1)}, u32[]{:S(2)}, u32[]{:S(2)}) %collective-permute-start.8) | collective-permute-done | bytes 196640 | tf_op jit(solution)/shard_map/ppermute | solution.py:216
  17.3 0.0 collective-permute-done.4.refs_0_
  17.3 0.0 collective-permute-done.9.refs_2_
  17.3 1.5 %last_scores.1 = bf16[1024,256]{1,0:T(8,128)(2,1)} custom-call(bf16[160,1024]{1,0:T(8,128)(2,1)S(1)} %collective-permute-done.4.refs_0_, bf16[96,1024]{1,0:T(8,128)(2,1)S(1)} %collective-permute-done.8.refs_1_, bf16[1024,1024]{1,0:T(8,128)(2,1)S(1)} %collective-permute-done.9.refs_2_, f32[1024,256]{1,0:T(8,128)S(1)} %first_scores.1.refs_3_), custom_call_target="tpu_custom_call" | custom-call | flops 536870912 | bytes 2097152 | tf_op jit(solution)/shard_map/last_scores/pallas_call | solution.py:160
  (1 shorter events, 0.0 us)
Async XLA Ops:
  0.0 4.1 %copy-start.1 = (bf16[32,1,1024]{2,0,1:T(8,128)(2,1)S(1)}, bf16[32,1,1024]{2,0,1:T(8,128)(2,1)}, u32[]{:S(2)}) copy-start(bf16[32,1,1024]{2,0,1:T(8,128)(2,1)} %param.6) | copy-start | bytes 196612
  0.0 11.6 %copy-start = (bf16[2048,1,1024]{2,0,1:T(8,128)(2,1)S(1)}, bf16[2048,1,1024]{2,0,1:T(8,128)(2,1)}, u32[]{:S(2)}) copy-start(bf16[2048,1,1024]{2,0,1:T(8,128)(2,1)} %param.5) | copy-start | bytes 12582916
  0.0 8.1 %collective-permute-start = (bf16[32,1024]{1,0:T(8,128)(2,1)}, bf16[32,1024]{1,0:T(8,128)(2,1)S(1)}, u32[]{:S(2)}, u32[]{:S(2)}) collective-permute-start(bf16[32,1024]{1,0:T(8,128)(2,1)} %bitcast.5), channel_id=1, source_target_pairs={{0,8},{2,10},{4,12},{6,14},{8,0},{10,2},{12,4},{14,6},{1,9},{3,11}... | collective-permute-start | bytes 196616 | tf_op jit(solution)/shard_map/ppermute | solution.py:212
  4.1 6.6 %collective-permute-start.2 = (bf16[32,1024]{1,0:T(8,128)(2,1)S(1)}, bf16[32,1024]{1,0:T(8,128)(2,1)S(1)}, u32[]{:S(2)}, u32[]{:S(2)}) collective-permute-start(bf16[32,1024]{1,0:T(8,128)(2,1)S(1)} %bitcast.6), channel_id=1, source_target_pairs={{0,2},{2,0},{4,6},{6,4},{8,10},{10,8},{12,14},{14,12},{1,3},{3,1},... | collective-permute-start | bytes 196616 | tf_op jit(solution)/shard_map/ppermute | solution.py:212
  5.6 6.1 %collective-permute-start.1 = (bf16[32,1024]{1,0:T(8,128)(2,1)S(1)}, bf16[32,1024]{1,0:T(8,128)(2,1)S(1)}, u32[]{:S(2)}, u32[]{:S(2)}) collective-permute-start(bf16[32,1024]{1,0:T(8,128)(2,1)S(1)} %bitcast.7), channel_id=1, source_target_pairs={{0,4},{2,6},{4,0},{6,2},{8,12},{10,14},{12,8},{14,10},{1,5},{3,7},... | collective-permute-start | bytes 196616 | tf_op jit(solution)/shard_map/ppermute | solution.py:212
  7.2 5.8 %collective-permute-start.3 = (bf16[32,1024]{1,0:T(8,128)(2,1)S(1)}, bf16[32,1024]{1,0:T(8,128)(2,1)S(1)}, u32[]{:S(2)}, u32[]{:S(2)}) collective-permute-start(bf16[32,1024]{1,0:T(8,128)(2,1)S(1)} %bitcast.8), channel_id=1, source_target_pairs={{0,6},{2,4},{4,2},{6,0},{8,14},{10,12},{12,10},{14,8},{1,7},{3,5},... | collective-permute-start | bytes 196616 | tf_op jit(solution)/shard_map/ppermute | solution.py:212
  7.6 4.2 %copy-start.2 = (f32[1,32,32]{2,1,0:T(8,128)S(1)}, f32[1,32,32]{2,1,0:T(8,128)}, u32[]{:S(2)}) copy-start(f32[1,32,32]{2,1,0:T(8,128)} %basis_in.1) | copy-start | bytes 12292
  7.6 4.2 %copy-start.3 = (f32[1,32,32]{2,1,0:T(8,128)S(1)}, f32[1,32,32]{2,1,0:T(8,128)}, u32[]{:S(2)}) copy-start(f32[1,32,32]{2,1,0:T(8,128)} %basis_out.1) | copy-start | bytes 12292
  7.6 4.2 %copy-start.4 = (f32[1,32,32]{2,1,0:T(8,128)S(1)}, f32[1,32,32]{2,1,0:T(8,128)}, u32[]{:S(2)}) copy-start(f32[1,32,32]{2,1,0:T(8,128)} %eigen.1) | copy-start | bytes 12292
  8.1 6.3 %collective-permute-start.5 = (bf16[32,1024]{1,0:T(8,128)(2,1)S(1)}, bf16[32,1024]{1,0:T(8,128)(2,1)S(1)}, u32[]{:S(2)}, u32[]{:S(2)}) collective-permute-start(bf16[32,1024]{1,0:T(8,128)(2,1)S(1)} %collective-permute-done.refs_1_), channel_id=1, source_target_pairs={{0,6},{2,4},{4,2},{6,0},{8,14},{10,12},{12,10},{14,8},{1,7},{3,5},... | collective-permute-start | bytes 196616 | tf_op jit(solution)/shard_map/ppermute | solution.py:212
  10.2 4.3 %collective-permute-start.6 = (bf16[32,1024]{1,0:T(8,128)(2,1)S(1)}, bf16[32,1024]{1,0:T(8,128)(2,1)S(1)}, u32[]{:S(2)}, u32[]{:S(2)}) collective-permute-start(bf16[32,1024]{1,0:T(8,128)(2,1)S(1)} %collective-permute-done.refs_1_), channel_id=1, source_target_pairs={{0,4},{2,6},{4,0},{6,2},{8,12},{10,14},{12,8},{14,10},{1,5},{3,7},... | collective-permute-start | bytes 196616 | tf_op jit(solution)/shard_map/ppermute | solution.py:212
  10.7 4.3 %collective-permute-start.7 = (bf16[32,1024]{1,0:T(8,128)(2,1)S(1)}, bf16[32,1024]{1,0:T(8,128)(2,1)S(1)}, u32[]{:S(2)}, u32[]{:S(2)}) collective-permute-start(bf16[32,1024]{1,0:T(8,128)(2,1)S(1)} %collective-permute-done.refs_1_), channel_id=1, source_target_pairs={{0,2},{2,0},{4,6},{6,4},{8,10},{10,8},{12,14},{14,12},{1,3},{3,1},... | collective-permute-start | bytes 196616 | tf_op jit(solution)/shard_map/ppermute | solution.py:212
  11.7 5.5 %collective-permute-start.9 = (bf16[1024,1024]{1,0:T(8,128)(2,1)S(1)}, bf16[1024,1024]{1,0:T(8,128)(2,1)S(1)}, u32[]{:S(2)}, u32[]{:S(2)}) collective-permute-start(bf16[1024,1024]{1,0:T(8,128)(2,1)S(1)} %other_half.1), channel_id=1, source_target_pairs={{0,1},{1,0},{2,3},{3,2},{4,5},{5,4},{6,7},{7,6},{8,9},{9,8},{10,11... | collective-permute-start | bytes 6291464 | tf_op jit(solution)/shard_map/ppermute | solution.py:216
  13.8 3.4 %collective-permute-start.4 = (bf16[160,1024]{1,0:T(8,128)(2,1)S(1)}, bf16[160,1024]{1,0:T(8,128)(2,1)S(1)}, u32[]{:S(2)}, u32[]{:S(2)}) collective-permute-start(bf16[160,1024]{1,0:T(8,128)(2,1)S(1)} %early_rows.1.refs_0_), channel_id=1, source_target_pairs={{0,1},{1,0},{2,3},{3,2},{4,5},{5,4},{6,7},{7,6},{8,9},{9,8},{10,11... | collective-permute-start | bytes 983048 | tf_op jit(solution)/shard_map/ppermute | solution.py:216
  15.8 1.5 %collective-permute-start.8 = (bf16[96,1024]{1,0:T(8,128)(2,1)S(1)}, bf16[96,1024]{1,0:T(8,128)(2,1)S(1)}, u32[]{:S(2)}, u32[]{:S(2)}) collective-permute-start(bf16[96,1024]{1,0:T(8,128)(2,1)S(1)} %late_rows.1.refs_1_), channel_id=1, source_target_pairs={{0,1},{1,0},{2,3},{3,2},{4,5},{5,4},{6,7},{7,6},{8,9},{9,8},{10,11... | collective-permute-start | bytes 589832 | tf_op jit(solution)/shard_map/ppermute | solution.py:216

commit v10 on v8

--- a/solution.py
+++ b/solution.py
@@ -133,7 +133,7 @@
             out_ref[here, cols] = (first_ref[here, cols] + second[here]).astype(BF16)
             if (i + 1) * step == train:
                 copies.append(pltpu.make_async_copy(out_ref.at[here], out_hbm.at[here], sems.at[r]))
-                copies[-1].start()
+                copies[-1].start(priority=r % 2)
     for copy in copies:
         copy.wait()
 

time: 18.8 us -> 18.8 us (level)
  no operation moved by 1% of the time
where the time goes in v10:
time: 18.8 us; the launch traced here: 18.6 us
  starting transfers between devices  12.6 us (67%)
  Pallas kernels  5.41 us (29%)
  waiting for transfers between devices  0.53 us (3%)
    ppermute x7, starting transfers between devices, exchange(): return lax.ppermute(x, 'pb', [(i, i ^ mask) for i in range(n)])  11.9 us
    pallas_call x2, Pallas kernels, precondition(): pl.pallas_call(precondition_kernel, out_shape=jax.ShapeDtypeStruct((rows,...  1.85 us
    pallas_call x1, Pallas kernels, last_scores(): pl.pallas_call(functools.partial(last_kernel, masks), out_shape=jax.Shape...  1.49 us
    pallas_call x1, Pallas kernels, kron_bases(): pl.pallas_call(kron_kernel, out_shape=tuple((jax.ShapeDtypeStruct(*x) for...  1.13 us
    pallas_call x1, Pallas kernels, first_scores(): pl.pallas_call(functools.partial(first_kernel, masks), out_shape=jax.Shap...  0.78 us
    ppermute x3, starting transfers between devices, other_layer(): return lax.ppermute(x, 'layer', [(0, 1), (1, 0)])  0.71 us
    ppermute x3, waiting for transfers between devices, other_layer(): return lax.ppermute(x, 'layer', [(0, 1), (1, 0)])  0.52 us
  transfers between devices with their start and end apart: 10, of which 1 were waited for; matrix products, arithmetic and copies ran while one was open for 0% of the time, Pallas kernels for 21%

profile of v10, /device:TPU:0, one launch (start us, length us, event | category | flops | bytes accessed | tf_op | source)
XLA Modules:
  0.0 18.6 jit_solution(7130931125968936550)
XLA Ops:
  0.0 0.0 copy-start.1
  0.0 0.0 copy-start
  0.0 4.0 %collective-permute-start = (bf16[32,1024]{1,0:T(8,128)(2,1)}, bf16[32,1024]{1,0:T(8,128)(2,1)S(1)}, u32[]{:S(2)}, u32[]{:S(2)}) collective-permute-start(bf16[32,1024]{1,0:T(8,128)(2,1)} %bitcast.5), channel_id=1, source_target_pairs={{0,8},{2,10},{4,12},{6,14},{8,0},{10,2},{12,4},{14,6},{1,9},{3,11}... | collective-permute-start | bytes 196616 | tf_op jit(solution)/shard_map/ppermute | solution.py:193
  4.0 1.3 %collective-permute-start.1 = (bf16[32,1024]{1,0:T(8,128)(2,1)}, bf16[32,1024]{1,0:T(8,128)(2,1)S(1)}, u32[]{:S(2)}, u32[]{:S(2)}) collective-permute-start(bf16[32,1024]{1,0:T(8,128)(2,1)} %bitcast.6), channel_id=1, source_target_pairs={{0,12},{2,14},{4,8},{6,10},{8,4},{10,6},{12,0},{14,2},{1,13},{3,15... | collective-permute-start | bytes 196616 | tf_op jit(solution)/shard_map/ppermute | solution.py:193
  5.4 0.0 copy-done.1
  5.4 0.3 %collective-permute-start.2 = (bf16[32,1024]{1,0:T(8,128)(2,1)S(1)}, bf16[32,1024]{1,0:T(8,128)(2,1)S(1)}, u32[]{:S(2)}, u32[]{:S(2)}) collective-permute-start(bf16[32,1024]{1,0:T(8,128)(2,1)S(1)} %bitcast.7), channel_id=1, source_target_pairs={{0,4},{2,6},{4,0},{6,2},{8,12},{10,14},{12,8},{14,10},{1,5},{3,7},... | collective-permute-start | bytes 196616 | tf_op jit(solution)/shard_map/ppermute | solution.py:193
  5.7 1.5 %collective-permute-start.3 = (bf16[32,1024]{1,0:T(8,128)(2,1)S(1)}, bf16[32,1024]{1,0:T(8,128)(2,1)S(1)}, u32[]{:S(2)}, u32[]{:S(2)}) collective-permute-start(bf16[32,1024]{1,0:T(8,128)(2,1)S(1)} %bitcast.8), channel_id=1, source_target_pairs={{0,2},{2,0},{4,6},{6,4},{8,10},{10,8},{12,14},{14,12},{1,3},{3,1},... | collective-permute-start | bytes 196616 | tf_op jit(solution)/shard_map/ppermute | solution.py:193
  7.2 1.8 %collective-permute-start.4 = (bf16[32,1024]{1,0:T(8,128)(2,1)S(1)}, bf16[32,1024]{1,0:T(8,128)(2,1)S(1)}, u32[]{:S(2)}, u32[]{:S(2)}) collective-permute-start(bf16[32,1024]{1,0:T(8,128)(2,1)S(1)} %bitcast.9), channel_id=1, source_target_pairs={{0,6},{2,4},{4,2},{6,0},{8,14},{10,12},{12,10},{14,8},{1,7},{3,5},... | collective-permute-start | bytes 196616 | tf_op jit(solution)/shard_map/ppermute | solution.py:193
  9.0 0.0 copy-start.2
  9.0 0.0 copy-start.3
  9.0 0.0 copy-start.4
  9.0 0.0 collective-permute-done.refs_1_
  9.0 1.6 %collective-permute-start.6 = (bf16[32,1024]{1,0:T(8,128)(2,1)S(1)}, bf16[32,1024]{1,0:T(8,128)(2,1)S(1)}, u32[]{:S(2)}, u32[]{:S(2)}) collective-permute-start(bf16[32,1024]{1,0:T(8,128)(2,1)S(1)} %collective-permute-done.refs_1_), channel_id=1, source_target_pairs={{0,2},{2,0},{4,6},{6,4},{8,10},{10,8},{12,14},{14,12},{1,3},{3,1},... | collective-permute-start | bytes 196616 | tf_op jit(solution)/shard_map/ppermute | solution.py:193
  10.6 0.0 collective-permute-done.1.refs_2_
  10.6 1.4 %collective-permute-start.7 = (bf16[32,1024]{1,0:T(8,128)(2,1)S(1)}, bf16[32,1024]{1,0:T(8,128)(2,1)S(1)}, u32[]{:S(2)}, u32[]{:S(2)}) collective-permute-start(bf16[32,1024]{1,0:T(8,128)(2,1)S(1)} %collective-permute-done.1.refs_2_), channel_id=1, source_target_pairs={{0,2},{2,0},{4,6},{6,4},{8,10},{10,8},{12,14},{14,12},{1,3},{3,1},... | collective-permute-start | bytes 196616 | tf_op jit(solution)/shard_map/ppermute | solution.py:193
  11.9 0.0 copy-done
  11.9 0.1 other_half.1
  12.1 0.0 collective-permute-done.3.refs_4_
  12.1 0.1 collective-permute-start.9
  12.2 0.0 copy-done.2
  12.2 0.0 copy-done.3
  12.2 0.0 copy-done.4
  12.2 1.1 %kron_bases.1 = (bf16[1024,1024]{1,0:T(8,128)(2,1)S(1)}, bf16[1024,1024]{1,0:T(8,128)(2,1)S(1)}, f32[1,1024]{1,0:T(1,128)S(1)}) custom-call(f32[1,32,32]{2,1,0:T(8,128)S(1)} %copy-done.2, f32[1,32,32]{2,1,0:T(8,128)S(1)} %copy-done.3, f32[1,32,32]{2,1,0:T(8,128)S(1)} %copy-done.4, bf16[64,1024]{1,0:T(8,128)(2,1)S(1)} %selectors.1.chosen_ref, ...), custom_call_target="tpu_custom_call" | custom-call | flops 536870912 | tf_op jit(solution)/shard_map/kron_bases/pallas_call | solution.py:65
  13.3 0.0 collective-permute-done.2.refs_3_
  13.3 0.0 collective-permute-done.4.refs_5_
  13.3 1.0 %early_rows.1.refs_0_ = bf16[192,1024]{1,0:T(8,128)(2,1)S(1)} custom-call(bf16[32,1024]{1,0:T(8,128)(2,1)S(1)} %bitcast.10, bf16[32,1024]{1,0:T(8,128)(2,1)S(1)} %collective-permute-done.refs_1_, bf16[32,1024]{1,0:T(8,128)(2,1)S(1)} %collective-permute-done.1.refs_2_, bf16[32,1024]{1,0:T(8,128)(2,1)S(1)} %collective-permute-done.2.refs_3_, ...), custom_call_target="tpu_custom_call" | custom-call | tf_op jit(solution)/shard_map/early_rows/pallas_call | solution.py:91
  14.3 0.5 %collective-permute-start.5 = (bf16[192,1024]{1,0:T(8,128)(2,1)S(1)}, bf16[192,1024]{1,0:T(8,128)(2,1)S(1)}, u32[]{:S(2)}, u32[]{:S(2)}) collective-permute-start(bf16[192,1024]{1,0:T(8,128)(2,1)S(1)} %early_rows.1.refs_0_), channel_id=1, source_target_pairs={{0,1},{1,0},{2,3},{3,2},{4,5},{5,4},{6,7},{7,6},{8,9},{9,8},{10,11... | collective-permute-start | bytes 1179656 | tf_op jit(solution)/shard_map/ppermute | solution.py:197
  14.9 0.0 collective-permute-done.6.refs_0_
  14.9 0.0 collective-permute-done.7.refs_1_
  14.9 0.9 %late_rows.1.refs_1_ = bf16[64,1024]{1,0:T(8,128)(2,1)S(1)} custom-call(bf16[32,1024]{1,0:T(8,128)(2,1)S(1)} %collective-permute-done.6.refs_0_, bf16[32,1024]{1,0:T(8,128)(2,1)S(1)} %collective-permute-done.7.refs_1_, bf16[1024,1024]{1,0:T(8,128)(2,1)S(1)} %get-tuple-element.13.refs_6_.refs_2_, bf16[1024,1024]{1,0:T(8,128)(2,1)S(1)} %get-tuple-element.14.refs_7_.refs_3_, ...), custom_call_target="tpu_custom_call" | custom-call | flops 20937965568 | tf_op jit(solution)/shard_map/late_rows/pallas_call | solution.py:91
  15.7 0.1 collective-permute-start.8
  15.9 0.8 %first_scores.1.refs_3_ = f32[1024,256]{1,0:T(8,128)S(1)} custom-call(bf16[192,1024]{1,0:T(8,128)(2,1)S(1)} %early_rows.1.refs_0_, bf16[64,1024]{1,0:T(8,128)(2,1)S(1)} %late_rows.1.refs_1_, bf16[2048,1024]{1,0:T(8,128)(2,1)S(1)} %bitcast.4), custom_call_target="tpu_custom_call" | custom-call | flops 536870912 | bytes 2097152 | tf_op jit(solution)/shard_map/first_scores/pallas_call | solution.py:144
  16.6 0.5 %collective-permute-done.8.refs_1_ = bf16[64,1024]{1,0:T(8,128)(2,1)S(1)} collective-permute-done((bf16[64,1024]{1,0:T(8,128)(2,1)S(1)}, bf16[64,1024]{1,0:T(8,128)(2,1)S(1)}, u32[]{:S(2)}, u32[]{:S(2)}) %collective-permute-start.8) | collective-permute-done | bytes 131104 | tf_op jit(solution)/shard_map/ppermute | solution.py:197
  17.2 0.0 collective-permute-done.5.refs_0_
  17.2 0.0 collective-permute-done.9.refs_2_
  17.2 1.5 %last_scores.1 = bf16[1024,256]{1,0:T(8,128)(2,1)} custom-call(bf16[192,1024]{1,0:T(8,128)(2,1)S(1)} %collective-permute-done.5.refs_0_, bf16[64,1024]{1,0:T(8,128)(2,1)S(1)} %collective-permute-done.8.refs_1_, bf16[1024,1024]{1,0:T(8,128)(2,1)S(1)} %collective-permute-done.9.refs_2_, f32[1024,256]{1,0:T(8,128)S(1)} %first_scores.1.refs_3_), custom_call_target="tpu_custom_call" | custom-call | flops 536870912 | bytes 2097152 | tf_op jit(solution)/shard_map/last_scores/pallas_call | solution.py:159
  (1 shorter events, 0.0 us)
Async XLA Ops:
  0.0 5.4 %copy-start.1 = (bf16[32,1,1024]{2,0,1:T(8,128)(2,1)S(1)}, bf16[32,1,1024]{2,0,1:T(8,128)(2,1)}, u32[]{:S(2)}) copy-start(bf16[32,1,1024]{2,0,1:T(8,128)(2,1)} %param.6) | copy-start | bytes 196612
  0.0 11.9 %copy-start = (bf16[2048,1,1024]{2,0,1:T(8,128)(2,1)S(1)}, bf16[2048,1,1024]{2,0,1:T(8,128)(2,1)}, u32[]{:S(2)}) copy-start(bf16[2048,1,1024]{2,0,1:T(8,128)(2,1)} %param.5) | copy-start | bytes 12582916
  0.0 9.0 %collective-permute-start = (bf16[32,1024]{1,0:T(8,128)(2,1)}, bf16[32,1024]{1,0:T(8,128)(2,1)S(1)}, u32[]{:S(2)}, u32[]{:S(2)}) collective-permute-start(bf16[32,1024]{1,0:T(8,128)(2,1)} %bitcast.5), channel_id=1, source_target_pairs={{0,8},{2,10},{4,12},{6,14},{8,0},{10,2},{12,4},{14,6},{1,9},{3,11}... | collective-permute-start | bytes 196616 | tf_op jit(solution)/shard_map/ppermute | solution.py:193
  4.0 6.5 %collective-permute-start.1 = (bf16[32,1024]{1,0:T(8,128)(2,1)}, bf16[32,1024]{1,0:T(8,128)(2,1)S(1)}, u32[]{:S(2)}, u32[]{:S(2)}) collective-permute-start(bf16[32,1024]{1,0:T(8,128)(2,1)} %bitcast.6), channel_id=1, source_target_pairs={{0,12},{2,14},{4,8},{6,10},{8,4},{10,6},{12,0},{14,2},{1,13},{3,15... | collective-permute-start | bytes 196616 | tf_op jit(solution)/shard_map/ppermute | solution.py:193
  5.4 7.9 %collective-permute-start.2 = (bf16[32,1024]{1,0:T(8,128)(2,1)S(1)}, bf16[32,1024]{1,0:T(8,128)(2,1)S(1)}, u32[]{:S(2)}, u32[]{:S(2)}) collective-permute-start(bf16[32,1024]{1,0:T(8,128)(2,1)S(1)} %bitcast.7), channel_id=1, source_target_pairs={{0,4},{2,6},{4,0},{6,2},{8,12},{10,14},{12,8},{14,10},{1,5},{3,7},... | collective-permute-start | bytes 196616 | tf_op jit(solution)/shard_map/ppermute | solution.py:193
  5.7 6.3 %collective-permute-start.3 = (bf16[32,1024]{1,0:T(8,128)(2,1)S(1)}, bf16[32,1024]{1,0:T(8,128)(2,1)S(1)}, u32[]{:S(2)}, u32[]{:S(2)}) collective-permute-start(bf16[32,1024]{1,0:T(8,128)(2,1)S(1)} %bitcast.8), channel_id=1, source_target_pairs={{0,2},{2,0},{4,6},{6,4},{8,10},{10,8},{12,14},{14,12},{1,3},{3,1},... | collective-permute-start | bytes 196616 | tf_op jit(solution)/shard_map/ppermute | solution.py:193
  7.2 6.1 %collective-permute-start.4 = (bf16[32,1024]{1,0:T(8,128)(2,1)S(1)}, bf16[32,1024]{1,0:T(8,128)(2,1)S(1)}, u32[]{:S(2)}, u32[]{:S(2)}) collective-permute-start(bf16[32,1024]{1,0:T(8,128)(2,1)S(1)} %bitcast.9), channel_id=1, source_target_pairs={{0,6},{2,4},{4,2},{6,0},{8,14},{10,12},{12,10},{14,8},{1,7},{3,5},... | collective-permute-start | bytes 196616 | tf_op jit(solution)/shard_map/ppermute | solution.py:193
  9.0 3.2 %copy-start.2 = (f32[1,32,32]{2,1,0:T(8,128)S(1)}, f32[1,32,32]{2,1,0:T(8,128)}, u32[]{:S(2)}) copy-start(f32[1,32,32]{2,1,0:T(8,128)} %basis_in.1) | copy-start | bytes 12292
  9.0 3.2 %copy-start.3 = (f32[1,32,32]{2,1,0:T(8,128)S(1)}, f32[1,32,32]{2,1,0:T(8,128)}, u32[]{:S(2)}) copy-start(f32[1,32,32]{2,1,0:T(8,128)} %basis_out.1) | copy-start | bytes 12292
  9.0 3.2 %copy-start.4 = (f32[1,32,32]{2,1,0:T(8,128)S(1)}, f32[1,32,32]{2,1,0:T(8,128)}, u32[]{:S(2)}) copy-start(f32[1,32,32]{2,1,0:T(8,128)} %eigen.1) | copy-start | bytes 12292
  9.0 5.9 %collective-permute-start.6 = (bf16[32,1024]{1,0:T(8,128)(2,1)S(1)}, bf16[32,1024]{1,0:T(8,128)(2,1)S(1)}, u32[]{:S(2)}, u32[]{:S(2)}) collective-permute-start(bf16[32,1024]{1,0:T(8,128)(2,1)S(1)} %collective-permute-done.refs_1_), channel_id=1, source_target_pairs={{0,2},{2,0},{4,6},{6,4},{8,10},{10,8},{12,14},{14,12},{1,3},{3,1},... | collective-permute-start | bytes 196616 | tf_op jit(solution)/shard_map/ppermute | solution.py:193
  10.6 4.3 %collective-permute-start.7 = (bf16[32,1024]{1,0:T(8,128)(2,1)S(1)}, bf16[32,1024]{1,0:T(8,128)(2,1)S(1)}, u32[]{:S(2)}, u32[]{:S(2)}) collective-permute-start(bf16[32,1024]{1,0:T(8,128)(2,1)S(1)} %collective-permute-done.1.refs_2_), channel_id=1, source_target_pairs={{0,2},{2,0},{4,6},{6,4},{8,10},{10,8},{12,14},{14,12},{1,3},{3,1},... | collective-permute-start | bytes 196616 | tf_op jit(solution)/shard_map/ppermute | solution.py:193
  12.1 5.1 %collective-permute-start.9 = (bf16[1024,1024]{1,0:T(8,128)(2,1)S(1)}, bf16[1024,1024]{1,0:T(8,128)(2,1)S(1)}, u32[]{:S(2)}, u32[]{:S(2)}) collective-permute-start(bf16[1024,1024]{1,0:T(8,128)(2,1)S(1)} %other_half.1), channel_id=1, source_target_pairs={{0,1},{1,0},{2,3},{3,2},{4,5},{5,4},{6,7},{7,6},{8,9},{9,8},{10,11... | collective-permute-start | bytes 6291464 | tf_op jit(solution)/shard_map/ppermute | solution.py:197
  14.3 2.8 %collective-permute-start.5 = (bf16[192,1024]{1,0:T(8,128)(2,1)S(1)}, bf16[192,1024]{1,0:T(8,128)(2,1)S(1)}, u32[]{:S(2)}, u32[]{:S(2)}) collective-permute-start(bf16[192,1024]{1,0:T(8,128)(2,1)S(1)} %early_rows.1.refs_0_), channel_id=1, source_target_pairs={{0,1},{1,0},{2,3},{3,2},{4,5},{5,4},{6,7},{7,6},{8,9},{9,8},{10,11... | collective-permute-start | bytes 1179656 | tf_op jit(solution)/shard_map/ppermute | solution.py:197
  15.7 1.4 %collective-permute-start.8 = (bf16[64,1024]{1,0:T(8,128)(2,1)S(1)}, bf16[64,1024]{1,0:T(8,128)(2,1)S(1)}, u32[]{:S(2)}, u32[]{:S(2)}) collective-permute-start(bf16[64,1024]{1,0:T(8,128)(2,1)S(1)} %late_rows.1.refs_1_), channel_id=1, source_target_pairs={{0,1},{1,0},{2,3},{3,2},{4,5},{5,4},{6,7},{7,6},{8,9},{9,8},{10,11... | collective-permute-start | bytes 393224 | tf_op jit(solution)/shard_map/ppermute | solution.py:197

commit v11 on v8

--- a/solution.py
+++ b/solution.py
@@ -161,7 +161,7 @@
         out_shape=jax.ShapeDtypeStruct((half, train), BF16),
         in_specs=[VMEM] * (len(groups) + 2),
         out_specs=HBM,
-        scratch_shapes=[pltpu.VMEM((train, grad), BF16), pltpu.VMEM((half, train), BF16), pltpu.SemaphoreType.DMA((8,))],
+        scratch_shapes=[pltpu.VMEM((train, grad), BF16), pltpu.VMEM((half, train), BF16), pltpu.SemaphoreType.DMA((16,))],
         compiler_params=PARAMS,
         cost_estimate=estimate(2 * train * grad * half, 2 * half * grad),
         name="last_scores",

time: 18.8 us -> 18.8 us (level)
  no operation moved by 1% of the time
where the time goes in v11:
time: 18.8 us; the launch traced here: 18.7 us
  starting transfers between devices  12.6 us (67%)
  Pallas kernels  5.47 us (29%)
  waiting for transfers between devices  0.53 us (3%)
    ppermute x7, starting transfers between devices, exchange(): return lax.ppermute(x, 'pb', [(i, i ^ mask) for i in range(n)])  11.9 us
    pallas_call x2, Pallas kernels, precondition(): pl.pallas_call(precondition_kernel, out_shape=jax.ShapeDtypeStruct((rows,...  1.85 us
    pallas_call x1, Pallas kernels, last_scores(): pl.pallas_call(functools.partial(last_kernel, masks), out_shape=jax.Shape...  1.55 us
    pallas_call x1, Pallas kernels, kron_bases(): pl.pallas_call(kron_kernel, out_shape=tuple((jax.ShapeDtypeStruct(*x) for...  1.13 us
    pallas_call x1, Pallas kernels, first_scores(): pl.pallas_call(functools.partial(first_kernel, masks), out_shape=jax.Shap...  0.78 us
    ppermute x3, starting transfers between devices, other_layer(): return lax.ppermute(x, 'layer', [(0, 1), (1, 0)])  0.71 us
    ppermute x3, waiting for transfers between devices, other_layer(): return lax.ppermute(x, 'layer', [(0, 1), (1, 0)])  0.52 us
  transfers between devices with their start and end apart: 10, of which 1 were waited for; matrix products, arithmetic and copies ran while one was open for 0% of the time, Pallas kernels for 21%

profile of v11, /device:TPU:0, one launch (start us, length us, event | category | flops | bytes accessed | tf_op | source)
XLA Modules:
  0.0 18.7 jit_solution(14403666544658367612)
XLA Ops:
  0.0 0.0 copy-start.1
  0.0 0.0 copy-start
  0.0 4.0 %collective-permute-start = (bf16[32,1024]{1,0:T(8,128)(2,1)}, bf16[32,1024]{1,0:T(8,128)(2,1)S(1)}, u32[]{:S(2)}, u32[]{:S(2)}) collective-permute-start(bf16[32,1024]{1,0:T(8,128)(2,1)} %bitcast.5), channel_id=1, source_target_pairs={{0,8},{2,10},{4,12},{6,14},{8,0},{10,2},{12,4},{14,6},{1,9},{3,11}... | collective-permute-start | bytes 196616 | tf_op jit(solution)/shard_map/ppermute | solution.py:193
  4.0 1.3 %collective-permute-start.1 = (bf16[32,1024]{1,0:T(8,128)(2,1)}, bf16[32,1024]{1,0:T(8,128)(2,1)S(1)}, u32[]{:S(2)}, u32[]{:S(2)}) collective-permute-start(bf16[32,1024]{1,0:T(8,128)(2,1)} %bitcast.6), channel_id=1, source_target_pairs={{0,12},{2,14},{4,8},{6,10},{8,4},{10,6},{12,0},{14,2},{1,13},{3,15... | collective-permute-start | bytes 196616 | tf_op jit(solution)/shard_map/ppermute | solution.py:193
  5.4 0.0 copy-done.1
  5.4 0.3 %collective-permute-start.2 = (bf16[32,1024]{1,0:T(8,128)(2,1)S(1)}, bf16[32,1024]{1,0:T(8,128)(2,1)S(1)}, u32[]{:S(2)}, u32[]{:S(2)}) collective-permute-start(bf16[32,1024]{1,0:T(8,128)(2,1)S(1)} %bitcast.7), channel_id=1, source_target_pairs={{0,4},{2,6},{4,0},{6,2},{8,12},{10,14},{12,8},{14,10},{1,5},{3,7},... | collective-permute-start | bytes 196616 | tf_op jit(solution)/shard_map/ppermute | solution.py:193
  5.7 1.5 %collective-permute-start.3 = (bf16[32,1024]{1,0:T(8,128)(2,1)S(1)}, bf16[32,1024]{1,0:T(8,128)(2,1)S(1)}, u32[]{:S(2)}, u32[]{:S(2)}) collective-permute-start(bf16[32,1024]{1,0:T(8,128)(2,1)S(1)} %bitcast.8), channel_id=1, source_target_pairs={{0,2},{2,0},{4,6},{6,4},{8,10},{10,8},{12,14},{14,12},{1,3},{3,1},... | collective-permute-start | bytes 196616 | tf_op jit(solution)/shard_map/ppermute | solution.py:193
  7.2 1.8 %collective-permute-start.4 = (bf16[32,1024]{1,0:T(8,128)(2,1)S(1)}, bf16[32,1024]{1,0:T(8,128)(2,1)S(1)}, u32[]{:S(2)}, u32[]{:S(2)}) collective-permute-start(bf16[32,1024]{1,0:T(8,128)(2,1)S(1)} %bitcast.9), channel_id=1, source_target_pairs={{0,6},{2,4},{4,2},{6,0},{8,14},{10,12},{12,10},{14,8},{1,7},{3,5},... | collective-permute-start | bytes 196616 | tf_op jit(solution)/shard_map/ppermute | solution.py:193
  9.0 0.0 copy-start.2
  9.0 0.0 copy-start.3
  9.0 0.0 copy-start.4
  9.0 0.0 collective-permute-done.refs_1_
  9.0 1.6 %collective-permute-start.6 = (bf16[32,1024]{1,0:T(8,128)(2,1)S(1)}, bf16[32,1024]{1,0:T(8,128)(2,1)S(1)}, u32[]{:S(2)}, u32[]{:S(2)}) collective-permute-start(bf16[32,1024]{1,0:T(8,128)(2,1)S(1)} %collective-permute-done.refs_1_), channel_id=1, source_target_pairs={{0,2},{2,0},{4,6},{6,4},{8,10},{10,8},{12,14},{14,12},{1,3},{3,1},... | collective-permute-start | bytes 196616 | tf_op jit(solution)/shard_map/ppermute | solution.py:193
  10.6 0.0 collective-permute-done.1.refs_2_
  10.6 1.4 %collective-permute-start.7 = (bf16[32,1024]{1,0:T(8,128)(2,1)S(1)}, bf16[32,1024]{1,0:T(8,128)(2,1)S(1)}, u32[]{:S(2)}, u32[]{:S(2)}) collective-permute-start(bf16[32,1024]{1,0:T(8,128)(2,1)S(1)} %collective-permute-done.1.refs_2_), channel_id=1, source_target_pairs={{0,2},{2,0},{4,6},{6,4},{8,10},{10,8},{12,14},{14,12},{1,3},{3,1},... | collective-permute-start | bytes 196616 | tf_op jit(solution)/shard_map/ppermute | solution.py:193
  11.9 0.0 copy-done
  11.9 0.1 other_half.1
  12.1 0.0 collective-permute-done.3.refs_4_
  12.1 0.1 collective-permute-start.9
  12.2 0.0 copy-done.2
  12.2 0.0 copy-done.3
  12.2 0.0 copy-done.4
  12.2 1.1 %kron_bases.1 = (bf16[1024,1024]{1,0:T(8,128)(2,1)S(1)}, bf16[1024,1024]{1,0:T(8,128)(2,1)S(1)}, f32[1,1024]{1,0:T(1,128)S(1)}) custom-call(f32[1,32,32]{2,1,0:T(8,128)S(1)} %copy-done.2, f32[1,32,32]{2,1,0:T(8,128)S(1)} %copy-done.3, f32[1,32,32]{2,1,0:T(8,128)S(1)} %copy-done.4, bf16[64,1024]{1,0:T(8,128)(2,1)S(1)} %selectors.1.chosen_ref, ...), custom_call_target="tpu_custom_call" | custom-call | flops 536870912 | tf_op jit(solution)/shard_map/kron_bases/pallas_call | solution.py:65
  13.3 0.0 collective-permute-done.2.refs_3_
  13.3 0.0 collective-permute-done.4.refs_5_
  13.3 1.0 %early_rows.1.refs_0_ = bf16[192,1024]{1,0:T(8,128)(2,1)S(1)} custom-call(bf16[32,1024]{1,0:T(8,128)(2,1)S(1)} %bitcast.10, bf16[32,1024]{1,0:T(8,128)(2,1)S(1)} %collective-permute-done.refs_1_, bf16[32,1024]{1,0:T(8,128)(2,1)S(1)} %collective-permute-done.1.refs_2_, bf16[32,1024]{1,0:T(8,128)(2,1)S(1)} %collective-permute-done.2.refs_3_, ...), custom_call_target="tpu_custom_call" | custom-call | tf_op jit(solution)/shard_map/early_rows/pallas_call | solution.py:91
  14.3 0.5 %collective-permute-start.5 = (bf16[192,1024]{1,0:T(8,128)(2,1)S(1)}, bf16[192,1024]{1,0:T(8,128)(2,1)S(1)}, u32[]{:S(2)}, u32[]{:S(2)}) collective-permute-start(bf16[192,1024]{1,0:T(8,128)(2,1)S(1)} %early_rows.1.refs_0_), channel_id=1, source_target_pairs={{0,1},{1,0},{2,3},{3,2},{4,5},{5,4},{6,7},{7,6},{8,9},{9,8},{10,11... | collective-permute-start | bytes 1179656 | tf_op jit(solution)/shard_map/ppermute | solution.py:197
  14.9 0.0 collective-permute-done.6.refs_0_
  14.9 0.0 collective-permute-done.7.refs_1_
  14.9 0.9 %late_rows.1.refs_1_ = bf16[64,1024]{1,0:T(8,128)(2,1)S(1)} custom-call(bf16[32,1024]{1,0:T(8,128)(2,1)S(1)} %collective-permute-done.6.refs_0_, bf16[32,1024]{1,0:T(8,128)(2,1)S(1)} %collective-permute-done.7.refs_1_, bf16[1024,1024]{1,0:T(8,128)(2,1)S(1)} %get-tuple-element.13.refs_6_.refs_2_, bf16[1024,1024]{1,0:T(8,128)(2,1)S(1)} %get-tuple-element.14.refs_7_.refs_3_, ...), custom_call_target="tpu_custom_call" | custom-call | flops 20937965568 | tf_op jit(solution)/shard_map/late_rows/pallas_call | solution.py:91
  15.7 0.1 collective-permute-start.8
  15.9 0.8 %first_scores.1.refs_3_ = f32[1024,256]{1,0:T(8,128)S(1)} custom-call(bf16[192,1024]{1,0:T(8,128)(2,1)S(1)} %early_rows.1.refs_0_, bf16[64,1024]{1,0:T(8,128)(2,1)S(1)} %late_rows.1.refs_1_, bf16[2048,1024]{1,0:T(8,128)(2,1)S(1)} %bitcast.4), custom_call_target="tpu_custom_call" | custom-call | flops 536870912 | bytes 2097152 | tf_op jit(solution)/shard_map/first_scores/pallas_call | solution.py:144
  16.6 0.5 %collective-permute-done.8.refs_1_ = bf16[64,1024]{1,0:T(8,128)(2,1)S(1)} collective-permute-done((bf16[64,1024]{1,0:T(8,128)(2,1)S(1)}, bf16[64,1024]{1,0:T(8,128)(2,1)S(1)}, u32[]{:S(2)}, u32[]{:S(2)}) %collective-permute-start.8) | collective-permute-done | bytes 131104 | tf_op jit(solution)/shard_map/ppermute | solution.py:197
  17.2 0.0 collective-permute-done.5.refs_0_
  17.2 0.0 collective-permute-done.9.refs_2_
  17.2 1.5 %last_scores.1 = bf16[1024,256]{1,0:T(8,128)(2,1)} custom-call(bf16[192,1024]{1,0:T(8,128)(2,1)S(1)} %collective-permute-done.5.refs_0_, bf16[64,1024]{1,0:T(8,128)(2,1)S(1)} %collective-permute-done.8.refs_1_, bf16[1024,1024]{1,0:T(8,128)(2,1)S(1)} %collective-permute-done.9.refs_2_, f32[1024,256]{1,0:T(8,128)S(1)} %first_scores.1.refs_3_), custom_call_target="tpu_custom_call" | custom-call | flops 536870912 | bytes 2097152 | tf_op jit(solution)/shard_map/last_scores/pallas_call | solution.py:159
  (1 shorter events, 0.0 us)
Async XLA Ops:
  0.0 5.4 %copy-start.1 = (bf16[32,1,1024]{2,0,1:T(8,128)(2,1)S(1)}, bf16[32,1,1024]{2,0,1:T(8,128)(2,1)}, u32[]{:S(2)}) copy-start(bf16[32,1,1024]{2,0,1:T(8,128)(2,1)} %param.6) | copy-start | bytes 196612
  0.0 11.9 %copy-start = (bf16[2048,1,1024]{2,0,1:T(8,128)(2,1)S(1)}, bf16[2048,1,1024]{2,0,1:T(8,128)(2,1)}, u32[]{:S(2)}) copy-start(bf16[2048,1,1024]{2,0,1:T(8,128)(2,1)} %param.5) | copy-start | bytes 12582916
  0.0 9.0 %collective-permute-start = (bf16[32,1024]{1,0:T(8,128)(2,1)}, bf16[32,1024]{1,0:T(8,128)(2,1)S(1)}, u32[]{:S(2)}, u32[]{:S(2)}) collective-permute-start(bf16[32,1024]{1,0:T(8,128)(2,1)} %bitcast.5), channel_id=1, source_target_pairs={{0,8},{2,10},{4,12},{6,14},{8,0},{10,2},{12,4},{14,6},{1,9},{3,11}... | collective-permute-start | bytes 196616 | tf_op jit(solution)/shard_map/ppermute | solution.py:193
  4.0 6.5 %collective-permute-start.1 = (bf16[32,1024]{1,0:T(8,128)(2,1)}, bf16[32,1024]{1,0:T(8,128)(2,1)S(1)}, u32[]{:S(2)}, u32[]{:S(2)}) collective-permute-start(bf16[32,1024]{1,0:T(8,128)(2,1)} %bitcast.6), channel_id=1, source_target_pairs={{0,12},{2,14},{4,8},{6,10},{8,4},{10,6},{12,0},{14,2},{1,13},{3,15... | collective-permute-start | bytes 196616 | tf_op jit(solution)/shard_map/ppermute | solution.py:193
  5.4 7.9 %collective-permute-start.2 = (bf16[32,1024]{1,0:T(8,128)(2,1)S(1)}, bf16[32,1024]{1,0:T(8,128)(2,1)S(1)}, u32[]{:S(2)}, u32[]{:S(2)}) collective-permute-start(bf16[32,1024]{1,0:T(8,128)(2,1)S(1)} %bitcast.7), channel_id=1, source_target_pairs={{0,4},{2,6},{4,0},{6,2},{8,12},{10,14},{12,8},{14,10},{1,5},{3,7},... | collective-permute-start | bytes 196616 | tf_op jit(solution)/shard_map/ppermute | solution.py:193
  5.7 6.3 %collective-permute-start.3 = (bf16[32,1024]{1,0:T(8,128)(2,1)S(1)}, bf16[32,1024]{1,0:T(8,128)(2,1)S(1)}, u32[]{:S(2)}, u32[]{:S(2)}) collective-permute-start(bf16[32,1024]{1,0:T(8,128)(2,1)S(1)} %bitcast.8), channel_id=1, source_target_pairs={{0,2},{2,0},{4,6},{6,4},{8,10},{10,8},{12,14},{14,12},{1,3},{3,1},... | collective-permute-start | bytes 196616 | tf_op jit(solution)/shard_map/ppermute | solution.py:193
  7.2 6.1 %collective-permute-start.4 = (bf16[32,1024]{1,0:T(8,128)(2,1)S(1)}, bf16[32,1024]{1,0:T(8,128)(2,1)S(1)}, u32[]{:S(2)}, u32[]{:S(2)}) collective-permute-start(bf16[32,1024]{1,0:T(8,128)(2,1)S(1)} %bitcast.9), channel_id=1, source_target_pairs={{0,6},{2,4},{4,2},{6,0},{8,14},{10,12},{12,10},{14,8},{1,7},{3,5},... | collective-permute-start | bytes 196616 | tf_op jit(solution)/shard_map/ppermute | solution.py:193
  9.0 3.2 %copy-start.2 = (f32[1,32,32]{2,1,0:T(8,128)S(1)}, f32[1,32,32]{2,1,0:T(8,128)}, u32[]{:S(2)}) copy-start(f32[1,32,32]{2,1,0:T(8,128)} %basis_in.1) | copy-start | bytes 12292
  9.0 3.2 %copy-start.3 = (f32[1,32,32]{2,1,0:T(8,128)S(1)}, f32[1,32,32]{2,1,0:T(8,128)}, u32[]{:S(2)}) copy-start(f32[1,32,32]{2,1,0:T(8,128)} %basis_out.1) | copy-start | bytes 12292
  9.0 3.2 %copy-start.4 = (f32[1,32,32]{2,1,0:T(8,128)S(1)}, f32[1,32,32]{2,1,0:T(8,128)}, u32[]{:S(2)}) copy-start(f32[1,32,32]{2,1,0:T(8,128)} %eigen.1) | copy-start | bytes 12292
  9.0 5.9 %collective-permute-start.6 = (bf16[32,1024]{1,0:T(8,128)(2,1)S(1)}, bf16[32,1024]{1,0:T(8,128)(2,1)S(1)}, u32[]{:S(2)}, u32[]{:S(2)}) collective-permute-start(bf16[32,1024]{1,0:T(8,128)(2,1)S(1)} %collective-permute-done.refs_1_), channel_id=1, source_target_pairs={{0,2},{2,0},{4,6},{6,4},{8,10},{10,8},{12,14},{14,12},{1,3},{3,1},... | collective-permute-start | bytes 196616 | tf_op jit(solution)/shard_map/ppermute | solution.py:193
  10.6 4.3 %collective-permute-start.7 = (bf16[32,1024]{1,0:T(8,128)(2,1)S(1)}, bf16[32,1024]{1,0:T(8,128)(2,1)S(1)}, u32[]{:S(2)}, u32[]{:S(2)}) collective-permute-start(bf16[32,1024]{1,0:T(8,128)(2,1)S(1)} %collective-permute-done.1.refs_2_), channel_id=1, source_target_pairs={{0,2},{2,0},{4,6},{6,4},{8,10},{10,8},{12,14},{14,12},{1,3},{3,1},... | collective-permute-start | bytes 196616 | tf_op jit(solution)/shard_map/ppermute | solution.py:193
  12.1 5.1 %collective-permute-start.9 = (bf16[1024,1024]{1,0:T(8,128)(2,1)S(1)}, bf16[1024,1024]{1,0:T(8,128)(2,1)S(1)}, u32[]{:S(2)}, u32[]{:S(2)}) collective-permute-start(bf16[1024,1024]{1,0:T(8,128)(2,1)S(1)} %other_half.1), channel_id=1, source_target_pairs={{0,1},{1,0},{2,3},{3,2},{4,5},{5,4},{6,7},{7,6},{8,9},{9,8},{10,11... | collective-permute-start | bytes 6291464 | tf_op jit(solution)/shard_map/ppermute | solution.py:197
  14.3 2.8 %collective-permute-start.5 = (bf16[192,1024]{1,0:T(8,128)(2,1)S(1)}, bf16[192,1024]{1,0:T(8,128)(2,1)S(1)}, u32[]{:S(2)}, u32[]{:S(2)}) collective-permute-start(bf16[192,1024]{1,0:T(8,128)(2,1)S(1)} %early_rows.1.refs_0_), channel_id=1, source_target_pairs={{0,1},{1,0},{2,3},{3,2},{4,5},{5,4},{6,7},{7,6},{8,9},{9,8},{10,11... | collective-permute-start | bytes 1179656 | tf_op jit(solution)/shard_map/ppermute | solution.py:197
  15.7 1.4 %collective-permute-start.8 = (bf16[64,1024]{1,0:T(8,128)(2,1)S(1)}, bf16[64,1024]{1,0:T(8,128)(2,1)S(1)}, u32[]{:S(2)}, u32[]{:S(2)}) collective-permute-start(bf16[64,1024]{1,0:T(8,128)(2,1)S(1)} %late_rows.1.refs_1_), channel_id=1, source_target_pairs={{0,1},{1,0},{2,3},{3,2},{4,5},{5,4},{6,7},{7,6},{8,9},{9,8},{10,11... | collective-permute-start | bytes 393224 | tf_op jit(solution)/shard_map/ppermute | solution.py:197
